TPU v7x, 256 devices: a whole 4x4x8 slice. The times are simulated.
256 devices in a mesh: gx: 8 (over y, x_lo), gy: 16 (over x_hi, z), gz: 2 (over core).
Axes of the slice: x: 4 (x_hi: 2, x_lo: 2; x = x_hi * 2 + x_lo), y: 4, z: 8, core: 2. Of those that a mesh axis runs over, the one named last changes fastest.
Arguments:
- charges: bfloat16 [8, 16, 2, 16, 2048], P('gx', 'gy', 'gz'), may hold values from -6 to 6
- positions: float32 [8, 16, 2, 3, 2048], P('gx', 'gy', 'gz'), may hold values from -0.5 to 0.5
- atom_cells: int32 [8, 16, 2, 2048], P('gx', 'gy', 'gz'), may hold values from 0 to 216, never falling along the last dimension, each value on 1 to 32 neighbouring positions
- offsets: int32 [2, 128, 3], replicated, may hold values from -3 to 3, as said below
- far_tables: bfloat16 [2, 49, 49, 128], replicated, may hold values from -0.01953125 to 0.01953125
- upward_tables: bfloat16 [8, 49, 49], replicated, may hold values from -0.3125 to 0.3125
- downward_tables: bfloat16 [8, 49, 49], replicated, may hold values from -0.875 to 0.875
Outputs:
- potential: float32 [8, 16, 2, 16, 2048], P('gx', 'gy', 'gz')
Inputs may be any that keep to these rules, and one draw needn't show every extreme that they name: `atom_cells`: within each device block the entries never fall along the slots; the value 216 marks padding slots, which come last; every cell and the padding hold 1 to 32 slots. For each level the 128 offsets are distinct, the largest magnitude of each offset's coordinates is 2 to 3, and the six offsets of 3 cells along a single axis are always among them.
All inputs are finite; a program needn't handle non-finite values.
Results may differ from a plain program's by a relative error of at most 0.0041.
Values may be sent and summed in bfloat16 or wider, within the bound.
No kernel may reach another device: no remote copies, remote signals or barrier semaphores. Data moves between devices by JAX's collectives and lax.ppermute only.
A program may use at most 128 MiB of HBM per device.

v0:
```python
import math

import jax
import jax.numpy as jnp
from jax import lax
from jax.sharding import PartitionSpec as P

CH = 16
ORDER = 6
TERMS = 49
REACH = 3
NOFF = 128
CX = 6
CY = 6
CZ = 6
CELLS = 216


radial_scale = 1.6


def extended(block, sides, width):
    for axis, dim in sides:
        count = lax.axis_size(axis)
        forward = [(i, i + 1) for i in range(count - 1)]
        forward.append((count - 1, 0))
        backward = [(target, source) for source, target in forward]
        low = lax.ppermute(
            lax.slice_in_dim(block, block.shape[dim] - width, None, axis=dim), axis, forward
        )
        high = lax.ppermute(lax.slice_in_dim(block, 0, width, axis=dim), axis, backward)
        block = jnp.concatenate([low, block, high], axis=dim)
    return block


def solid_harmonics(coords):
    x_part = coords[0]
    y_part = coords[1]
    z_part = coords[2]
    radius_sq = x_part * x_part + y_part * y_part + z_part * z_part
    zeros_row = jnp.zeros_like(x_part)
    cosines = {(0, 0): jnp.ones_like(x_part)}
    sines = {(0, 0): zeros_row}
    for degree in range(1, ORDER + 1):
        for order_m in range(degree):
            lower_c = cosines[degree - 1, order_m]
            lower_s = sines[degree - 1, order_m]
            if order_m <= degree - 2:
                second_c = cosines[degree - 2, order_m]
                second_s = sines[degree - 2, order_m]
            else:
                second_c = zeros_row
                second_s = zeros_row
            divisor = float((degree + order_m) * (degree - order_m))
            cosines[degree, order_m] = (
                (2 * degree - 1) * z_part * lower_c - radius_sq * second_c
            ) / divisor
            sines[degree, order_m] = (
                (2 * degree - 1) * z_part * lower_s - radius_sq * second_s
            ) / divisor
        prev_c = cosines[degree - 1, degree - 1]
        prev_s = sines[degree - 1, degree - 1]
        cosines[degree, degree] = -(x_part * prev_c - y_part * prev_s) / (2.0 * degree)
        sines[degree, degree] = -(x_part * prev_s + y_part * prev_c) / (2.0 * degree)
    terms_list = []
    for degree in range(ORDER + 1):
        terms_list.append(cosines[degree, 0] * float(math.factorial(degree)))
        for order_m in range(1, degree + 1):
            factor = math.sqrt(math.factorial(degree + order_m) * math.factorial(degree - order_m))
            terms_list.append(cosines[degree, order_m] * factor)
            terms_list.append(sines[degree, order_m] * factor)
    return jnp.stack(terms_list, 0)


def extend_rims(field):
    wider = extended(field, (("gx", 0), ("gy", 1), ("gz", 2)), REACH)
    return wider


def flat_table(level_tables):
    return level_tables.transpose(2, 1, 0).reshape(NOFF * TERMS, TERMS)


def far_field(padded_field, table_rows, level_offsets, extent, y_block):
    ext_x, ext_y, ext_z = extent
    shaped = padded_field.reshape(
        ext_x + 2 * REACH, ext_y + 2 * REACH, ext_z + 2 * REACH, CH, TERMS
    )
    slab_list = []
    for start_x in range(ext_x):
        part_list = []
        for start_y in range(0, ext_y, y_block):

            def take_window(offset_now):
                begin = (
                    start_x + REACH + offset_now[0],
                    start_y + REACH + offset_now[1],
                    REACH + offset_now[2],
                    0,
                    0,
                )
                return lax.dynamic_slice(shaped, begin, (1, y_block, ext_z, CH, TERMS))

            columns = jax.vmap(take_window, out_axes=4)(level_offsets)
            row_block = columns.reshape(y_block * ext_z * CH, NOFF * TERMS)
            product = jnp.dot(row_block, table_rows, preferred_element_type=jnp.float32)
            part_list.append(product.reshape(1, y_block, ext_z, CH, TERMS))
        slab_list.append(jnp.concatenate(part_list, axis=1))
    return jnp.concatenate(slab_list, axis=0)


def per_device(charges, positions, atom_cells, offsets, far_tables, upward_tables, downward_tables):
    charge_block = charges[0, 0, 0]
    place_block = positions[0, 0, 0]
    cell_block = atom_cells[0, 0, 0]
    slot_count = charge_block.shape[-1]
    harmonics = solid_harmonics(radial_scale * place_block)
    cell_numbers = jnp.arange(CELLS, dtype=jnp.int32)
    onehot = (cell_numbers[:, None] == cell_block[None, :]).astype(jnp.float32)
    weighted = (charge_block.astype(jnp.float32)[:, None, :] * harmonics[None, :, :]).reshape(
        CH * TERMS, slot_count
    )
    pole_columns = lax.dot_general(
        weighted,
        onehot,
        (((1,), (1,)), ((), ())),
        precision=lax.Precision.HIGHEST,
        preferred_element_type=jnp.float32,
    )
    leaf_poles = pole_columns.T.astype(jnp.bfloat16).reshape(CX, CY, CZ, CH * TERMS)
    children = leaf_poles.reshape(CX // 2, 2, CY // 2, 2, CZ // 2, 2, CH, TERMS)
    upward = upward_tables.reshape(2, 2, 2, TERMS, TERMS)
    parent_poles = jnp.einsum(
        "xaybzcqk,abcjk->xyzqj", children, upward, preferred_element_type=jnp.float32
    )
    parent_poles = parent_poles.astype(jnp.bfloat16).reshape(CX // 2, CY // 2, CZ // 2, CH * TERMS)
    leaf_far = far_field(
        extend_rims(leaf_poles), flat_table(far_tables[0]), offsets[0], (CX, CY, CZ), CY // 2
    )
    parent_far = far_field(
        extend_rims(parent_poles),
        flat_table(far_tables[1]),
        offsets[1],
        (CX // 2, CY // 2, CZ // 2),
        CY // 2,
    )
    parent_far = parent_far.astype(jnp.bfloat16)
    downward = downward_tables.reshape(2, 2, 2, TERMS, TERMS)
    lifted = jnp.einsum(
        "xyzqk,abcjk->xaybzcqj", parent_far, downward, preferred_element_type=jnp.float32
    )
    leaf_locals = leaf_far + lifted.reshape(CX, CY, CZ, CH, TERMS)
    local_table = leaf_locals.reshape(CELLS, CH * TERMS)
    spread = lax.dot_general(
        local_table,
        onehot,
        (((0,), (0,)), ((), ())),
        precision=lax.Precision.HIGHEST,
        preferred_element_type=jnp.float32,
    )
    potential = jnp.sum(spread.reshape(CH, TERMS, slot_count) * harmonics[None, :, :], axis=1)
    return potential[None, None, None]


def solution(mesh):
    placed = (
        P("gx", "gy", "gz", None, None),
        P("gx", "gy", "gz", None, None),
        P("gx", "gy", "gz", None),
        P(),
        P(),
        P(),
        P(),
    )
    return jax.shard_map(
        per_device,
        mesh=mesh,
        in_specs=placed,
        out_specs=P("gx", "gy", "gz", None, None),
        check_vma=False,
    )
```

profile of v0, /device:TPU:1, one launch (start us, length us, event | category | flops | bytes accessed | tf_op | source)
XLA Modules:
  0.0 691.2 jit_solution(8452023877744876469)
XLA Ops:
  3.3 3.8 broadcast_multiply_fusion
  7.1 5.3 mul.1406
  12.5 6.1 fusion.3
  20.6 4.6 collective-permute-start.7
  26.1 15.5 %collective-permute-start.1 = (bf16[3,6,6,784]{3,2,1,0:T(8,128)(2,1)S(1)}, bf16[3,6,6,784]{3,2,1,0:T(8,128)(2,1)}, u32[]{:S(2)}, u32[]{:S(2)}) collective-permute-start(bf16[3,6,6,784]{3,2,1,0:T(8,128)(2,1)S(1)} %slice.120), channel_id=1, source_target_pairs={{32,0},{64,32},{96,64},{128,96},{160,128},{192,160},{224,192},{0,2... | collective-permute-start | bytes 508040 | tf_op jit(solution)/shard_map/ppermute | solution.py:31
  46.6 4.1 copy.61
  54.2 3.8 copy.60
  61.7 7.8 %collective-permute-start.9 = (bf16[9,3,3,784]{3,2,1,0:T(4,128)(2,1)S(1)}, bf16[9,3,3,784]{3,2,1,0:T(4,128)(2,1)S(1)}, u32[]{:S(2)}, u32[]{:S(2)}) collective-permute-start(bf16[9,3,3,784]{3,2,1,0:T(4,128)(2,1)S(1)} %constant_dynamic-update-slice_fusion.3), channel_id=1, source_target_pairs={{2,0},{4,2},{6,4},{8,6},{10,8},{12,10},{14,12},{16,14},{18,16},{20... | collective-permute-start | bytes 381032 | tf_op jit(solution)/shard_map/ppermute | solution.py:31
  72.7 5.2 collective-permute-start.3
  82.2 7.7 %collective-permute-done.2 = bf16[12,3,6,784]{3,2,1,0:T(8,128)(2,1)S(1)} collective-permute-done((bf16[12,3,6,784]{3,2,1,0:T(8,128)(2,1)S(1)}, bf16[12,3,6,784]{3,2,1,0:T(8,128)(2,1)S(1)}, u32[]{:S(2)}, u32[]{:S(2)}) %collective-permute-start.2) | collective-permute-done | bytes 338720 | tf_op jit(solution)/shard_map/ppermute | solution.py:28
  97.8 7.0 %reshape.207 = bf16[9,9,9,16,49]{4,3,0,2,1:T(8,128)(2,1)S(1)} reshape(bf16[9,9,9,784]{3,0,2,1:T(8,128)(2,1)} %copy.35) | data formatting | bytes 2286144 | tf_op jit(solution)/shard_map/reshape | solution.py:86
  108.4 5.9 copy.40
  114.2 8.1 %reshape.211 = bf16[3,3,16,6272]{3,2,1,0:T(8,128)(2,1)} reshape(bf16[1,3,3,16,128,49]{5,4,3,2,1,0:T(8,128)(2,1)} %copy.40) | data formatting | bytes 3612672 | tf_op jit(solution)/shard_map/reshape.110
  125.9 5.9 copy.39
  131.8 8.1 %reshape.210 = bf16[3,3,16,6272]{3,2,1,0:T(8,128)(2,1)} reshape(bf16[1,3,3,16,128,49]{5,4,3,2,1,0:T(8,128)(2,1)} %copy.39) | data formatting | bytes 3612672 | tf_op jit(solution)/shard_map/reshape.107
  143.5 5.9 copy.36
  149.4 8.4 %reshape.208 = bf16[3,3,16,6272]{3,2,1,0:T(8,128)(2,1)} reshape(bf16[1,3,3,16,128,49]{5,4,3,2,1,0:T(8,128)(2,1)} %copy.36) | data formatting | bytes 3612672 | tf_op jit(solution)/shard_map/reshape.104
  163.6 4.3 pad_maximum_fusion
  167.9 3.8 copy.17
  171.7 14.4 %reshape.191 = bf16[12,12,12,16,49]{4,3,0,2,1:T(8,128)(2,1)} reshape(bf16[12,12,12,784]{3,0,2,1:T(8,128)(2,1)} %copy.17) | data formatting | bytes 5419008 | tf_op jit(solution)/shard_map/reshape | solution.py:86
  186.1 12.5 %gather_fusion.11 = bf16[128,3,6,16,49]{4,3,2,1,0:T(8,128)(2,1)} fusion(bf16[12,12,12,16,49]{4,3,0,2,1:T(8,128)(2,1)} %reshape.191, s32[128]{0:T(128)S(1)} %get-tuple-element.122), kind=kCustom, calls=%fused_computation.11 | custom fusion | bytes 7227904 | tf_op jit(solution)/shard_map/vmap()/gather | solution.py:102
  198.6 11.0 %copy.32 = bf16[1,3,6,16,128,49]{5,4,3,2,1,0:T(8,128)(2,1)} copy(bf16[1,3,6,16,128,49]{5,3,2,1,4,0:T(8,128)(2,1)} %bitcast.410) | data formatting | bytes 7225344 | tf_op jit(solution)/shard_map/vmap()/transpose | solution.py:104
  209.5 14.7 %reshape.204 = bf16[3,6,16,6272]{3,2,1,0:T(8,128)(2,1)} reshape(bf16[1,3,6,16,128,49]{5,4,3,2,1,0:T(8,128)(2,1)} %copy.32) | data formatting | bytes 7225344 | tf_op jit(solution)/shard_map/reshape.101
  224.2 12.3 %gather_fusion.10 = bf16[128,3,6,16,49]{4,3,2,1,0:T(8,128)(2,1)} fusion(bf16[12,12,12,16,49]{4,3,0,2,1:T(8,128)(2,1)} %reshape.191, s32[128]{0:T(128)S(1)} %get-tuple-element.8), kind=kCustom, calls=%fused_computation.10 | custom fusion | bytes 7227904 | tf_op jit(solution)/shard_map/vmap()/gather | solution.py:102
  236.5 11.0 %copy.31 = bf16[1,3,6,16,128,49]{5,4,3,2,1,0:T(8,128)(2,1)} copy(bf16[1,3,6,16,128,49]{5,3,2,1,4,0:T(8,128)(2,1)} %bitcast.411) | data formatting | bytes 7225344 | tf_op jit(solution)/shard_map/vmap()/transpose | solution.py:104
  247.5 15.1 %reshape.203 = bf16[3,6,16,6272]{3,2,1,0:T(8,128)(2,1)} reshape(bf16[1,3,6,16,128,49]{5,4,3,2,1,0:T(8,128)(2,1)} %copy.31) | data formatting | bytes 7225344 | tf_op jit(solution)/shard_map/reshape.98
  262.6 3.9 convolution_bitcast_fusion.1
  268.2 12.3 %gather_fusion.9 = bf16[128,3,6,16,49]{4,3,2,1,0:T(8,128)(2,1)} fusion(bf16[12,12,12,16,49]{4,3,0,2,1:T(8,128)(2,1)} %reshape.191, s32[128]{0:T(128)S(1)} %get-tuple-element.117), kind=kCustom, calls=%fused_computation.9 | custom fusion | bytes 7227904 | tf_op jit(solution)/shard_map/vmap()/gather | solution.py:102
  280.5 11.0 %copy.30 = bf16[1,3,6,16,128,49]{5,4,3,2,1,0:T(8,128)(2,1)} copy(bf16[1,3,6,16,128,49]{5,3,2,1,4,0:T(8,128)(2,1)} %bitcast.412) | data formatting | bytes 7225344 | tf_op jit(solution)/shard_map/vmap()/transpose | solution.py:104
  291.5 14.7 %reshape.202 = bf16[3,6,16,6272]{3,2,1,0:T(8,128)(2,1)} reshape(bf16[1,3,6,16,128,49]{5,4,3,2,1,0:T(8,128)(2,1)} %copy.30) | data formatting | bytes 7225344 | tf_op jit(solution)/shard_map/reshape.95
  309.3 12.5 %gather_fusion.8 = bf16[128,3,6,16,49]{4,3,2,1,0:T(8,128)(2,1)} fusion(bf16[12,12,12,16,49]{4,3,0,2,1:T(8,128)(2,1)} %reshape.191, s32[128]{0:T(128)S(1)} %get-tuple-element.112), kind=kCustom, calls=%fused_computation.8 | custom fusion | bytes 7227904 | tf_op jit(solution)/shard_map/vmap()/gather | solution.py:102
  321.7 11.0 %copy.29 = bf16[1,3,6,16,128,49]{5,4,3,2,1,0:T(8,128)(2,1)} copy(bf16[1,3,6,16,128,49]{5,3,2,1,4,0:T(8,128)(2,1)} %bitcast.413) | data formatting | bytes 7225344 | tf_op jit(solution)/shard_map/vmap()/transpose | solution.py:104
  332.7 14.7 %reshape.201 = bf16[3,6,16,6272]{3,2,1,0:T(8,128)(2,1)} reshape(bf16[1,3,6,16,128,49]{5,4,3,2,1,0:T(8,128)(2,1)} %copy.29) | data formatting | bytes 7225344 | tf_op jit(solution)/shard_map/reshape.92
  350.5 12.5 %gather_fusion.7 = bf16[128,3,6,16,49]{4,3,2,1,0:T(8,128)(2,1)} fusion(bf16[12,12,12,16,49]{4,3,0,2,1:T(8,128)(2,1)} %reshape.191, s32[128]{0:T(128)S(1)} %get-tuple-element.118), kind=kCustom, calls=%fused_computation.7 | custom fusion | bytes 7227904 | tf_op jit(solution)/shard_map/vmap()/gather | solution.py:102
  363.0 11.0 %copy.28 = bf16[1,3,6,16,128,49]{5,4,3,2,1,0:T(8,128)(2,1)} copy(bf16[1,3,6,16,128,49]{5,3,2,1,4,0:T(8,128)(2,1)} %bitcast.414) | data formatting | bytes 7225344 | tf_op jit(solution)/shard_map/vmap()/transpose | solution.py:104
  373.9 14.7 %reshape.200 = bf16[3,6,16,6272]{3,2,1,0:T(8,128)(2,1)} reshape(bf16[1,3,6,16,128,49]{5,4,3,2,1,0:T(8,128)(2,1)} %copy.28) | data formatting | bytes 7225344 | tf_op jit(solution)/shard_map/reshape.89
  391.7 12.3 %gather_fusion.6 = bf16[128,3,6,16,49]{4,3,2,1,0:T(8,128)(2,1)} fusion(bf16[12,12,12,16,49]{4,3,0,2,1:T(8,128)(2,1)} %reshape.191, s32[128]{0:T(128)S(1)} %get-tuple-element.113), kind=kCustom, calls=%fused_computation.6 | custom fusion | bytes 7227904 | tf_op jit(solution)/shard_map/vmap()/gather | solution.py:102
  404.0 11.0 %copy.27 = bf16[1,3,6,16,128,49]{5,4,3,2,1,0:T(8,128)(2,1)} copy(bf16[1,3,6,16,128,49]{5,3,2,1,4,0:T(8,128)(2,1)} %bitcast.415) | data formatting | bytes 7225344 | tf_op jit(solution)/shard_map/vmap()/transpose | solution.py:104
  415.0 15.1 %reshape.199 = bf16[3,6,16,6272]{3,2,1,0:T(8,128)(2,1)} reshape(bf16[1,3,6,16,128,49]{5,4,3,2,1,0:T(8,128)(2,1)} %copy.27) | data formatting | bytes 7225344 | tf_op jit(solution)/shard_map/reshape.86
  430.1 3.8 convolution_bitcast_fusion.6
  433.8 12.3 %gather_fusion.5 = bf16[128,3,6,16,49]{4,3,2,1,0:T(8,128)(2,1)} fusion(bf16[12,12,12,16,49]{4,3,0,2,1:T(8,128)(2,1)} %reshape.191, s32[128]{0:T(128)S(1)} %get-tuple-element.119), kind=kCustom, calls=%fused_computation.5 | custom fusion | bytes 7227904 | tf_op jit(solution)/shard_map/vmap()/gather | solution.py:102
  446.1 11.0 %copy.26 = bf16[1,3,6,16,128,49]{5,4,3,2,1,0:T(8,128)(2,1)} copy(bf16[1,3,6,16,128,49]{5,3,2,1,4,0:T(8,128)(2,1)} %bitcast.416) | data formatting | bytes 7225344 | tf_op jit(solution)/shard_map/vmap()/transpose | solution.py:104
  457.1 14.7 %reshape.198 = bf16[3,6,16,6272]{3,2,1,0:T(8,128)(2,1)} reshape(bf16[1,3,6,16,128,49]{5,4,3,2,1,0:T(8,128)(2,1)} %copy.26) | data formatting | bytes 7225344 | tf_op jit(solution)/shard_map/reshape.41
  471.8 3.8 convolution_bitcast_fusion.7
  475.5 12.5 %gather_fusion.4 = bf16[128,3,6,16,49]{4,3,2,1,0:T(8,128)(2,1)} fusion(bf16[12,12,12,16,49]{4,3,0,2,1:T(8,128)(2,1)} %reshape.191, s32[128]{0:T(128)S(1)} %copy-done.8), kind=kCustom, calls=%fused_computation.4 | custom fusion | bytes 7227904 | tf_op jit(solution)/shard_map/vmap()/gather | solution.py:102
  488.0 11.0 %copy.25 = bf16[1,3,6,16,128,49]{5,4,3,2,1,0:T(8,128)(2,1)} copy(bf16[1,3,6,16,128,49]{5,3,2,1,4,0:T(8,128)(2,1)} %bitcast.417) | data formatting | bytes 7225344 | tf_op jit(solution)/shard_map/vmap()/transpose | solution.py:104
  499.0 14.7 %reshape.197 = bf16[3,6,16,6272]{3,2,1,0:T(8,128)(2,1)} reshape(bf16[1,3,6,16,128,49]{5,4,3,2,1,0:T(8,128)(2,1)} %copy.25) | data formatting | bytes 7225344 | tf_op jit(solution)/shard_map/reshape.38
  513.7 3.8 convolution_bitcast_fusion.8
  517.4 12.5 %gather_fusion.3 = bf16[128,3,6,16,49]{4,3,2,1,0:T(8,128)(2,1)} fusion(bf16[12,12,12,16,49]{4,3,0,2,1:T(8,128)(2,1)} %reshape.191, s32[128]{0:T(128)S(1)} %copy-done.9), kind=kCustom, calls=%fused_computation.3 | custom fusion | bytes 7227904 | tf_op jit(solution)/shard_map/vmap()/gather | solution.py:102
  529.9 11.0 %copy.24 = bf16[1,3,6,16,128,49]{5,4,3,2,1,0:T(8,128)(2,1)} copy(bf16[1,3,6,16,128,49]{5,3,2,1,4,0:T(8,128)(2,1)} %bitcast.418) | data formatting | bytes 7225344 | tf_op jit(solution)/shard_map/vmap()/transpose | solution.py:104
  540.9 14.7 %reshape.196 = bf16[3,6,16,6272]{3,2,1,0:T(8,128)(2,1)} reshape(bf16[1,3,6,16,128,49]{5,4,3,2,1,0:T(8,128)(2,1)} %copy.24) | data formatting | bytes 7225344 | tf_op jit(solution)/shard_map/reshape.35
  555.6 3.8 convolution_bitcast_fusion.9
  559.3 12.3 %gather_fusion.2 = bf16[128,3,6,16,49]{4,3,2,1,0:T(8,128)(2,1)} fusion(bf16[12,12,12,16,49]{4,3,0,2,1:T(8,128)(2,1)} %reshape.191, s32[128]{0:T(128)S(1)} %copy-done.6), kind=kCustom, calls=%fused_computation.2 | custom fusion | bytes 7227904 | tf_op jit(solution)/shard_map/vmap()/gather | solution.py:102
  571.6 11.0 %copy.23 = bf16[1,3,6,16,128,49]{5,4,3,2,1,0:T(8,128)(2,1)} copy(bf16[1,3,6,16,128,49]{5,3,2,1,4,0:T(8,128)(2,1)} %bitcast.419) | data formatting | bytes 7225344 | tf_op jit(solution)/shard_map/vmap()/transpose | solution.py:104
  582.6 15.1 %reshape.195 = bf16[3,6,16,6272]{3,2,1,0:T(8,128)(2,1)} reshape(bf16[1,3,6,16,128,49]{5,4,3,2,1,0:T(8,128)(2,1)} %copy.23) | data formatting | bytes 7225344 | tf_op jit(solution)/shard_map/reshape.32
  597.7 3.7 convolution_bitcast_fusion.10
  601.4 12.3 %gather_fusion.1 = bf16[128,3,6,16,49]{4,3,2,1,0:T(8,128)(2,1)} fusion(bf16[12,12,12,16,49]{4,3,0,2,1:T(8,128)(2,1)} %reshape.191, s32[128]{0:T(128)S(1)} %copy-done.7), kind=kCustom, calls=%fused_computation.1 | custom fusion | bytes 7227904 | tf_op jit(solution)/shard_map/vmap()/gather | solution.py:102
  613.7 11.0 %copy.22 = bf16[1,3,6,16,128,49]{5,4,3,2,1,0:T(8,128)(2,1)} copy(bf16[1,3,6,16,128,49]{5,3,2,1,4,0:T(8,128)(2,1)} %bitcast.420) | data formatting | bytes 7225344 | tf_op jit(solution)/shard_map/vmap()/transpose | solution.py:104
  624.7 14.7 %reshape.194 = bf16[3,6,16,6272]{3,2,1,0:T(8,128)(2,1)} reshape(bf16[1,3,6,16,128,49]{5,4,3,2,1,0:T(8,128)(2,1)} %copy.22) | data formatting | bytes 7225344 | tf_op jit(solution)/shard_map/reshape.29
  639.4 3.8 convolution_bitcast_fusion.11
  643.1 12.5 %gather_fusion = bf16[128,3,6,16,49]{4,3,2,1,0:T(8,128)(2,1)} fusion(bf16[12,12,12,16,49]{4,3,0,2,1:T(8,128)(2,1)} %reshape.191, s32[128]{0:T(128)S(1)} %copy-done.5), kind=kCustom, calls=%fused_computation | custom fusion | bytes 7227904 | tf_op jit(solution)/shard_map/vmap()/gather | solution.py:102
  655.6 11.0 %copy.19 = bf16[1,3,6,16,128,49]{5,4,3,2,1,0:T(8,128)(2,1)} copy(bf16[1,3,6,16,128,49]{5,3,2,1,4,0:T(8,128)(2,1)} %bitcast.409) | data formatting | bytes 7225344 | tf_op jit(solution)/shard_map/vmap()/transpose | solution.py:104
  666.6 14.7 %reshape.192 = bf16[3,6,16,6272]{3,2,1,0:T(8,128)(2,1)} reshape(bf16[1,3,6,16,128,49]{5,4,3,2,1,0:T(8,128)(2,1)} %copy.19) | data formatting | bytes 7225344 | tf_op jit(solution)/shard_map/reshape.26
  686.7 4.2 multiply_reduce_fusion
  (162 shorter events, 66.5 us)
Async XLA Ops:
  0.0 161.2 %copy-start = (bf16[8,49,49]{2,0,1:T(8,128)(2,1)S(1)}, bf16[8,49,49]{2,0,1:T(8,128)(2,1)}, u32[]{:S(2)}) copy-start(bf16[8,49,49]{2,0,1:T(8,128)(2,1)} %param.13) | copy-start | bytes 115252
  3.3 9.1 %copy-start.17 = (f32[49,2048]{1,0:T(8,128)}, f32[49,2048]{1,0:T(8,128)S(1)}, u32[]{:S(2)}) copy-start(f32[49,2048]{1,0:T(8,128)S(1)} %stack.5) | copy-start | bytes 1204228
  7.1 5.3 copy-start.28
  12.4 7.5 %copy-start.31 = (bf16[8,49,49]{2,0,1:T(8,128)(2,1)S(1)}, bf16[8,49,49]{2,0,1:T(8,128)(2,1)}, u32[]{:S(2)}) copy-start(bf16[8,49,49]{2,0,1:T(8,128)(2,1)} %param.12) | copy-start | bytes 115252
  12.4 29.2 %copy-start.30 = (s32[2,128,3]{1,0,2:T(2,128)S(1)}, s32[2,128,3]{1,0,2:T(2,128)}, u32[]{:S(2)}) copy-start(s32[2,128,3]{1,0,2:T(2,128)} %param.10) | copy-start | bytes 9220
  12.4 30.4 %copy-start.12 = (bf16[2,49,49,128]{3,0,2,1:T(2,128)(2,1)S(1)}, bf16[2,49,49,128]{3,0,2,1:T(2,128)(2,1)}, u32[]{:S(2)}) copy-start(bf16[2,49,49,128]{3,0,2,1:T(2,128)(2,1)} %param.11) | copy-start | bytes 3687940
  20.6 41.0 %collective-permute-start.7 = (bf16[3,3,3,784]{3,2,1,0:T(4,128)(2,1)S(1)}, bf16[3,3,3,784]{3,2,1,0:T(4,128)(2,1)S(1)}, u32[]{:S(2)}, u32[]{:S(2)}) collective-permute-start(bf16[3,3,3,784]{3,2,1,0:T(4,128)(2,1)S(1)} %reshape.206), channel_id=1, source_target_pairs={{32,0},{64,32},{96,64},{128,96},{160,128},{192,160},{224,192},{0,2... | collective-permute-start | bytes 127016 | tf_op jit(solution)/shard_map/ppermute | solution.py:31
  25.1 36.4 %collective-permute-start.6 = (bf16[3,3,3,784]{3,2,1,0:T(4,128)(2,1)S(1)}, bf16[3,3,3,784]{3,2,1,0:T(4,128)(2,1)S(1)}, u32[]{:S(2)}, u32[]{:S(2)}) collective-permute-start(bf16[3,3,3,784]{3,2,1,0:T(4,128)(2,1)S(1)} %reshape.206), channel_id=1, source_target_pairs={{0,32},{32,64},{64,96},{96,128},{128,160},{160,192},{192,224},{224... | collective-permute-start | bytes 127016 | tf_op jit(solution)/shard_map/ppermute | solution.py:28
  26.0 43.5 %collective-permute-start = (bf16[3,6,6,784]{3,2,1,0:T(8,128)(2,1)}, bf16[3,6,6,784]{3,2,1,0:T(8,128)(2,1)}, u32[]{:S(2)}, u32[]{:S(2)}) collective-permute-start(bf16[3,6,6,784]{3,2,1,0:T(8,128)(2,1)} %slice.118), channel_id=1, source_target_pairs={{0,32},{32,64},{64,96},{96,128},{128,160},{160,192},{192,224},{224... | collective-permute-start | bytes 508040 | tf_op jit(solution)/shard_map/ppermute | solution.py:28
  26.1 45.5 %collective-permute-start.1 = (bf16[3,6,6,784]{3,2,1,0:T(8,128)(2,1)S(1)}, bf16[3,6,6,784]{3,2,1,0:T(8,128)(2,1)}, u32[]{:S(2)}, u32[]{:S(2)}) collective-permute-start(bf16[3,6,6,784]{3,2,1,0:T(8,128)(2,1)S(1)} %slice.120), channel_id=1, source_target_pairs={{32,0},{64,32},{96,64},{128,96},{160,128},{192,160},{224,192},{0,2... | collective-permute-start | bytes 508040 | tf_op jit(solution)/shard_map/ppermute | solution.py:31
  61.7 16.2 %collective-permute-start.9 = (bf16[9,3,3,784]{3,2,1,0:T(4,128)(2,1)S(1)}, bf16[9,3,3,784]{3,2,1,0:T(4,128)(2,1)S(1)}, u32[]{:S(2)}, u32[]{:S(2)}) collective-permute-start(bf16[9,3,3,784]{3,2,1,0:T(4,128)(2,1)S(1)} %constant_dynamic-update-slice_fusion.3), channel_id=1, source_target_pairs={{2,0},{4,2},{6,4},{8,6},{10,8},{12,10},{14,12},{16,14},{18,16},{20... | collective-permute-start | bytes 381032 | tf_op jit(solution)/shard_map/ppermute | solution.py:31
  69.5 8.4 %collective-permute-start.8 = (bf16[9,3,3,784]{3,2,1,0:T(4,128)(2,1)S(1)}, bf16[9,3,3,784]{3,2,1,0:T(4,128)(2,1)S(1)}, u32[]{:S(2)}, u32[]{:S(2)}) collective-permute-start(bf16[9,3,3,784]{3,2,1,0:T(4,128)(2,1)S(1)} %constant_dynamic-update-slice_fusion.3), channel_id=1, source_target_pairs={{0,2},{2,4},{4,6},{6,8},{8,10},{10,12},{12,14},{14,16},{16,18},{18... | collective-permute-start | bytes 381032 | tf_op jit(solution)/shard_map/ppermute | solution.py:28
  72.6 20.0 %copy-start.3 = (bf16[12,6,6,784]{3,2,1,0:T(8,128)(2,1)}, bf16[12,6,6,784]{3,2,1,0:T(8,128)(2,1)S(1)}, u32[]{:S(2)}) copy-start(bf16[12,6,6,784]{3,2,1,0:T(8,128)(2,1)S(1)} %constant_dynamic-update-slice_fusion) | copy-start | bytes 2032132
  72.7 17.3 %collective-permute-start.2 = (bf16[12,3,6,784]{3,2,1,0:T(8,128)(2,1)S(1)}, bf16[12,3,6,784]{3,2,1,0:T(8,128)(2,1)S(1)}, u32[]{:S(2)}, u32[]{:S(2)}) collective-permute-start(bf16[12,3,6,784]{3,2,1,0:T(8,128)(2,1)S(1)} %get-tuple-element.54), channel_id=1, source_target_pairs={{0,2},{2,4},{4,6},{6,8},{8,10},{10,12},{12,14},{14,16},{16,18},{18... | collective-permute-start | bytes 1016072 | tf_op jit(solution)/shard_map/ppermute | solution.py:28
  72.7 17.2 %collective-permute-start.3 = (bf16[12,3,6,784]{3,2,1,0:T(8,128)(2,1)S(1)}, bf16[12,3,6,784]{3,2,1,0:T(8,128)(2,1)S(1)}, u32[]{:S(2)}, u32[]{:S(2)}) collective-permute-start(bf16[12,3,6,784]{3,2,1,0:T(8,128)(2,1)S(1)} %get-tuple-element.55), channel_id=1, source_target_pairs={{2,0},{4,2},{6,4},{8,6},{10,8},{12,10},{14,12},{16,14},{18,16},{20... | collective-permute-start | bytes 1016072 | tf_op jit(solution)/shard_map/ppermute | solution.py:31
  78.4 16.0 %collective-permute-start.11 = (bf16[9,9,3,784]{3,2,1,0:T(4,128)(2,1)S(1)}, bf16[9,9,3,784]{3,2,1,0:T(4,128)(2,1)S(1)}, u32[]{:S(2)}, u32[]{:S(2)}) collective-permute-start(bf16[9,9,3,784]{3,2,1,0:T(4,128)(2,1)S(1)} %pad_maximum_fusion.3), channel_id=1, source_target_pairs={{1,0},{0,1},{3,2},{2,3},{5,4},{4,5},{7,6},{6,7},{9,8},{8,9},{11,10... | collective-permute-start | bytes 1143080 | tf_op jit(solution)/shard_map/ppermute | solution.py:31
  82.1 12.3 %collective-permute-start.10 = (bf16[9,9,3,784]{3,2,1,0:T(4,128)(2,1)S(1)}, bf16[9,9,3,784]{3,2,1,0:T(4,128)(2,1)S(1)}, u32[]{:S(2)}, u32[]{:S(2)}) collective-permute-start(bf16[9,9,3,784]{3,2,1,0:T(4,128)(2,1)S(1)} %pad_maximum_fusion.3), channel_id=1, source_target_pairs={{0,1},{1,0},{2,3},{3,2},{4,5},{5,4},{6,7},{7,6},{8,9},{9,8},{10,11... | collective-permute-start | bytes 1143080 | tf_op jit(solution)/shard_map/ppermute | solution.py:28
  89.9 2.6 copy-start.15
  89.9 2.6 copy-start.16
  92.6 71.0 %collective-permute-start.4 = (bf16[12,12,3,784]{3,2,1,0:T(4,128)(2,1)}, bf16[12,12,3,784]{3,2,1,0:T(4,128)(2,1)}, u32[]{:S(2)}, u32[]{:S(2)}) collective-permute-start(bf16[12,12,3,784]{3,2,1,0:T(4,128)(2,1)} %get-tuple-element.50), channel_id=1, source_target_pairs={{0,1},{1,0},{2,3},{3,2},{4,5},{5,4},{6,7},{7,6},{8,9},{9,8},{10,11... | collective-permute-start | bytes 2032136 | tf_op jit(solution)/shard_map/ppermute | solution.py:28
  94.3 69.3 %collective-permute-start.5 = (bf16[12,12,3,784]{3,2,1,0:T(4,128)(2,1)}, bf16[12,12,3,784]{3,2,1,0:T(4,128)(2,1)}, u32[]{:S(2)}, u32[]{:S(2)}) collective-permute-start(bf16[12,12,3,784]{3,2,1,0:T(4,128)(2,1)} %get-tuple-element.51), channel_id=1, source_target_pairs={{1,0},{0,1},{3,2},{2,3},{5,4},{4,5},{7,6},{6,7},{9,8},{8,9},{11,10... | collective-permute-start | bytes 2032136 | tf_op jit(solution)/shard_map/ppermute | solution.py:31
  149.4 8.4 %copy-start.2 = (bf16[6272,49,1,1]{0,1,2,3:T(8,128)(2,1)S(1)}, bf16[6272,49,1,1]{0,1,2,3:T(8,128)(2,1)}, u32[]{:S(2)}) copy-start(bf16[6272,49,1,1]{0,1,2,3:T(8,128)(2,1)} %reshape.323) | copy-start | bytes 1843972
  149.4 8.4 %copy-start.10 = (bf16[3,3,16,6272]{3,2,1,0:T(8,128)(2,1)S(1)}, bf16[3,3,16,6272]{3,2,1,0:T(8,128)(2,1)}, u32[]{:S(2)}) copy-start(bf16[3,3,16,6272]{3,2,1,0:T(8,128)(2,1)} %reshape.211) | copy-start | bytes 5419012
  157.8 2.8 copy-start.11
  161.2 2.4 copy-start.4
  247.5 15.1 %copy-start.19 = (bf16[6272,49,1,1]{0,1,2,3:T(8,128)(2,1)S(1)}, bf16[6272,49,1,1]{0,1,2,3:T(8,128)(2,1)}, u32[]{:S(2)}) copy-start(bf16[6272,49,1,1]{0,1,2,3:T(8,128)(2,1)} %reshape.320) | copy-start | bytes 1843972
  262.6 3.9 copy-start.13
  471.8 3.8 copy-start.8
  513.7 3.8 copy-start.9
  555.6 3.8 copy-start.6
  597.7 3.8 copy-start.7
  639.4 3.8 copy-start.5
  681.2 3.3 copy-start.27
  681.2 3.3 copy-start.25
  681.2 3.3 copy-start.26
  681.3 3.4 copy-start.23
  681.3 3.4 copy-start.24
  681.3 3.4 copy-start.22
  681.3 3.5 copy-start.20
  681.3 3.5 copy-start.21
  684.5 1.2 copy-start.14
  684.8 1.5 copy-start.29
  685.7 1.0 copy-start.18
  685.7 5.2 copy-start.1
where the time goes:
time: 698 us; the launch traced here: 691 us
  local copies, waits for them, and re-layouts  574 us (82%)
  matrix products  55.2 us (8%)
  starting transfers between devices  38.8 us (6%)
  other arithmetic  14.6 us (2%)
  waiting for transfers between devices  7.77 us (1%)
    another operation x15, local copies, waits for them, and re-layouts  202 us
    gather x15, local copies, waits for them, and re-layouts, take_window(): return lax.dynamic_slice(shaped, begin, (1, y_block, ext_z, CH, TERMS))  159 us
    transpose x15, local copies, waits for them, and re-layouts, far_field(): columns = jax.vmap(take_window, out_axes=4)(level_offsets)  149 us
    dot_general x15, matrix products, far_field(): product = jnp.dot(row_block, table_rows, preferred_element_type=jnp.float32)  44.1 us
    ppermute x6, starting transfers between devices, extended(): lax.ppermute(lax.slice_in_dim(block, 0, width, axis=dim), axis, backward)  36.9 us
    reshape x2, local copies, waits for them, and re-layouts, far_field(): padded_field.reshape(ext_x + 2 * REACH, ext_y + 2 * REACH, ext_z + 2 * RE...  21.3 us
  transfers between devices with their start and end apart: 12, of which 1 were waited for; matrix products, arithmetic and copies ran while one was open for 14% of the time, Pallas kernels for 0%

commit v1 on v0

v1 whole, which is shorter than its diff:
```python
import math

import numpy as np
import jax
import jax.numpy as jnp
from jax import lax
from jax.experimental import pallas as pl
from jax.experimental.pallas import tpu as pltpu
from jax.sharding import PartitionSpec as P

CH = 16
ORDER = 6
TERMS = 49
NOFF = 128
SLOTS = 3
PSLOTS = 2
F32 = jnp.float32
BF16 = jnp.bfloat16
NT = (((1,), (1,)), ((), ()))
TN = (((0,), (0,)), ((), ()))
radial_scale = 1.6
MIB = 1 << 20


def spectral_constants():
    leaf_freq = [[None, 2, 4], [1, 3, 5]]
    pair_freq = [[2, 0], [1, 3]]
    turn = 2 * math.pi / 12
    pturn = 2 * math.pi / 6

    def fwd(core, s, ri, z):
        f = leaf_freq[core][s]
        if f is None:
            return float(z % 2 == ri)
        return math.cos(turn * f * z) if ri == 0 else -math.sin(turn * f * z)

    def inv(core, s, ri, z):
        f = leaf_freq[core][s]
        if f is None:
            return float(z % 2 == ri) / 6
        return (math.cos(turn * f * z) if ri == 0 else -math.sin(turn * f * z)) / 6

    def pfwd(core, s, ri, z):
        f = pair_freq[core][s]
        if s == 1:
            return math.cos(pturn * f * z) if ri == 0 else 0.0
        return math.cos(pturn * f * z) if ri == 0 else -math.sin(pturn * f * z)

    def pinv(core, s, ri, z):
        return pfwd(core, s, ri, z) / (6 if s == 1 else 3)

    halves = np.zeros((2, 104, 128))
    for core in range(2):
        row = 0

        def put(a, b):
            nonlocal row
            halves[core, row, :64] = a
            halves[core, row, 64:] = b
            row += 1

        for s in range(SLOTS):
            for v in range(6):
                z = (core if v < 3 else 1 - core) * 6 + 2 * (v % 3)
                put(fwd(core, s, 0, z), fwd(core, s, 1, z + 1))
                put(fwd(core, s, 0, z + 1), fwd(core, s, 1, z))
        for p in range(3):
            z = core * 6 + 2 * p
            for u in range(6):
                own = core if u < 3 else 1 - core
                s = u % 3
                put(inv(own, s, 0, z), inv(own, s, 1, z + 1))
                put(inv(own, s, 1, z), inv(own, s, 0, z + 1))
        for s in range(PSLOTS):
            for v in range(4):
                z = (core if v < 2 else 1 - core) * 3 + 2 * (v % 2)
                on = float(v % 2 == 0)
                put(pfwd(core, s, 0, z), on * pfwd(core, s, 1, z + 1))
                put(on * pfwd(core, s, 0, z + 1), pfwd(core, s, 1, z))
        for p in range(2):
            z = core * 3 + 2 * p
            on = float(p == 0)
            for u in range(4):
                own = core if u < 2 else 1 - core
                s = u % 2
                put(pinv(own, s, 0, z), on * pinv(own, s, 1, z + 1))
                put(pinv(own, s, 1, z), on * pinv(own, s, 0, z + 1))
        assert row == 104
    table = np.zeros((2, 80))
    for core in range(2):
        for pq in range(2):
            for s in range(SLOTS):
                f = leaf_freq[core][s]
                for d in range(7):
                    dz = d - 3
                    if f is None:
                        val = float(dz % 2 == pq)
                    else:
                        val = math.sin(turn * f * dz) if pq else math.cos(turn * f * dz)
                    table[core, (pq * SLOTS + s) * 7 + d] = val
            for s in range(PSLOTS):
                f = pair_freq[core][s]
                for d in range(7):
                    dz = d - 3
                    if s == 1:
                        val = 0.0 if pq else math.cos(pturn * f * dz)
                    else:
                        val = math.sin(pturn * f * dz) if pq else math.cos(pturn * f * dz)
                    table[core, 42 + (pq * PSLOTS + s) * 7 + d] = val
        table[core, 70] = 1.0 if core == 0 else -1.0
    return halves.astype(np.float32), table.reshape(-1).astype(np.float32)


COEFS, ZTABLE = spectral_constants()


def harmonic_terms(x, y, z):
    rsq = x * x + y * y + z * z
    cosines = {(0, 0): jnp.ones_like(x)}
    sines = {}
    for deg in range(1, ORDER + 1):
        for m in range(deg):
            inv = 1.0 / float((deg + m) * (deg - m))
            for part in (cosines, sines):
                if part is sines and m == 0:
                    continue
                val = ((2 * deg - 1) * inv) * (z * part[deg - 1, m])
                if m <= deg - 2:
                    val = val - inv * (rsq * part[deg - 2, m])
                part[deg, m] = val
        scale = -1.0 / (2.0 * deg)
        pc = cosines[deg - 1, deg - 1]
        if deg == 1:
            cosines[1, 1] = scale * x
            sines[1, 1] = scale * y
        else:
            ps = sines[deg - 1, deg - 1]
            cosines[deg, deg] = scale * (x * pc - y * ps)
            sines[deg, deg] = scale * (x * ps + y * pc)
    out = []
    for deg in range(ORDER + 1):
        out.append(cosines[deg, 0] * float(math.factorial(deg)))
        for m in range(1, deg + 1):
            factor = math.sqrt(math.factorial(deg + m) * math.factorial(deg - m))
            out.append(cosines[deg, m] * factor)
            out.append(sines[deg, m] * factor)
    return out


def low_lanes(rows):
    return lax.broadcasted_iota(jnp.int32, (rows, 128), 1) < 64


def cell_number_rows():
    row = lax.broadcasted_iota(jnp.int32, (240, 128), 0)
    z = jnp.zeros_like(row)
    for i in range(1, 6):
        z = z + (row >= 40 * i).astype(jnp.int32)
    xy = row - 40 * z
    return jnp.where(xy < 36, xy * 6 + z, -1)


def poles_kernel(ch_ref, pos_ref, cell_ref, up_ref, zs_ref, h_ref, pos_s, h3_s, chf_s, whi_s, wlo_s, one_s, f_s):
    for d in range(3):
        for i in range(16):
            pos_s[d * 16 + i : d * 16 + i + 1, :] = pos_ref[0, 0, 0, d : d + 1, i * 128 : (i + 1) * 128]
    terms = harmonic_terms(
        radial_scale * pos_s[0:16, :], radial_scale * pos_s[16:32, :], radial_scale * pos_s[32:48, :]
    )
    for k in range(TERMS):
        h3_s[k * 16 : (k + 1) * 16, :] = terms[k]
    h3_s[TERMS * 16 : 1024, :] = jnp.zeros((1024 - TERMS * 16, 128), F32)
    for i in range(16):
        h_ref[:, i * 128 : (i + 1) * 128] = h3_s[pl.ds(i, 64, stride=16), :]
    chf_s[...] = ch_ref[0, 0, 0].astype(F32)
    number = cell_number_rows()
    for i in range(16):
        sl = slice(i * 128, (i + 1) * 128)
        cells = cell_ref[0, 0, :, sl]
        one_s[:, sl] = jnp.where(number == cells, 1.0, 0.0).astype(BF16)
    for c in range(CH):
        for i in range(4):
            sl = slice(i * 512, (i + 1) * 512)
            w = h_ref[:, sl] * chf_s[c : c + 1, sl]
            hi = w.astype(BF16)
            whi_s[c * 64 : (c + 1) * 64, sl] = hi
            wlo_s[c * 64 : (c + 1) * 64, sl] = (w - hi.astype(F32)).astype(BF16)
    low = low_lanes(40)
    for n in range(4):
        rows = slice(n * 256, (n + 1) * 256)
        r = lax.dot_general(one_s[...], whi_s[rows, :], NT, preferred_element_type=F32)
        r = r + lax.dot_general(one_s[...], wlo_s[rows, :], NT, preferred_element_type=F32)
        for half in range(2):
            c = n * 4 + half * 2
            for zp in range(3):
                a = r[zp * 80 : zp * 80 + 40, half * 128 : half * 128 + 128]
                b = r[zp * 80 + 40 : zp * 80 + 80, half * 128 : half * 128 + 128]
                f_s[zp, pl.ds(c, 40, stride=16), :] = jnp.where(low, a, pltpu.roll(b, 64, 1))
                f_s[zp, pl.ds(c + 1, 40, stride=16), :] = jnp.where(low, pltpu.roll(a, 64, 1), b)
    res = []
    for zp in range(3):
        leaf = f_s[zp, 0:576, :].astype(BF16)
        zs_ref[zp * 576 : (zp + 1) * 576, :] = leaf
        split = leaf.reshape(3, 2, 3, 2, 16, 128)
        lhs = jnp.concatenate(
            [split[:, p, :, q].reshape(144, 128) for p in range(2) for q in range(2)], axis=1
        )
        res.append(lax.dot_general(lhs, up_ref[...], NT, preferred_element_type=F32))
    low = low_lanes(144)
    zs_ref[1728:1872, :] = jnp.where(low, res[0], res[1]).astype(BF16)
    zs_ref[1872:2016, :] = jnp.where(low, res[2], 0.0).astype(BF16)


def combine(values, coef, row):
    total = None
    for v, val in enumerate(values):
        part = val * coef(row + 2 * v) + pltpu.roll(val, 64, 1) * coef(row + 2 * v + 1)
        total = part if total is None else total + part
    return total


def forward_kernel(own_ref, other_ref, coef_ref, sl_ref, sr_ref):
    core = lax.axis_index("gz")

    def coef(row):
        return coef_ref[core, row : row + 1, :]

    for x in range(6):
        face = sl_ref if x < 3 else sr_ref
        for y in range(6):
            at = (x * 6 + y) * 16
            values = [
                ref[zp * 576 + at : zp * 576 + at + 16, :].astype(F32)
                for ref in (own_ref, other_ref)
                for zp in range(3)
            ]
            for s in range(SLOTS):
                row = (((s * 3 + x % 3) * 2 + y % 2) * 3 + y // 2) * 16
                face[row : row + 16, :] = combine(values, coef, s * 12).astype(BF16)
    for x in range(3):
        for y in range(3):
            at = 1728 + (x * 3 + y) * 16
            values = [
                ref[at + v * 144 : at + v * 144 + 16, :].astype(F32)
                for ref in (own_ref, other_ref)
                for v in range(2)
            ]
            for s in range(PSLOTS):
                row = 864 + ((s * 3 + x) * 3 + (0, 2, 1)[y]) * 16
                done = combine(values, coef, 72 + s * 8).astype(BF16)
                sl_ref[row : row + 16, :] = done
                sr_ref[row : row + 16, :] = done


def table_kernel(off_ref, zt_ref, far_ref, wl_ref, wp_ref, t3_s, w_s, a_s):
    core = lax.axis_index("gz")
    base = core * 80
    t3_s[...] = jnp.zeros_like(t3_s)
    for level, slots, out_ref, start in ((0, SLOTS, wl_ref, 0), (1, PSLOTS, wp_ref, 42)):
        for j in range(TERMS):
            t3_s[j * 56 : j * 56 + TERMS, :] = far_ref[level, j].astype(F32)
        ox = off_ref[level, 0:1, :]
        oy = off_ref[level, 1:2, :]
        oz = off_ref[level, 2:3, :]
        code = (ox + 3) * 7 + (oy + 3)
        chosen = lax.broadcasted_iota(jnp.int32, (56, 128), 0) == code
        for q in range(2 * slots):
            row = jnp.zeros((1, 128), F32)
            for d in range(7):
                row = jnp.where(oz == d - 3, zt_ref[base + start + q * 7 + d], row)
            full = jnp.where(chosen, row, 0.0)
            hi = full.astype(BF16).astype(F32)
            a_s[q * 56 : (q + 1) * 56, 0:128] = hi
            a_s[q * 56 : (q + 1) * 56, 128:256] = full - hi
        coefs = a_s[0 : 2 * slots * 56, :].astype(BF16)
        count = slots * 56
        low = low_lanes(count)
        block = lax.broadcasted_iota(jnp.int32, (count, 128), 0)
        if level == 0:
            sign = jnp.where(block < 56, zt_ref[base + 70], -1.0)
        else:
            sign = jnp.full((count, 128), -1.0, F32)

        def one_term(k, carry):
            tk = t3_s[pl.ds(k, 64, stride=56), :].astype(BF16)
            wide = jnp.concatenate([tk, tk], axis=1)
            rhs = jnp.concatenate([wide, wide], axis=0)
            out = lax.dot_general(coefs, rhs, NT, preferred_element_type=F32)
            even = out[0:count]
            odd = out[count : 2 * count]
            w_s[pl.ds(k, count, stride=128), :] = jnp.where(low, even, odd)
            w_s[pl.ds(k + 64, count, stride=128), :] = jnp.where(low, sign * odd, even)
            return carry

        lax.fori_loop(0, TERMS, one_term, 0, unroll=7)
        inner = lax.broadcasted_iota(jnp.int32, (128, 128), 0)
        filled = (inner < TERMS) | ((inner >= 64) & (inner < 64 + TERMS))

        def one_block(b, carry):
            val = w_s[pl.ds(pl.multiple_of(b * 128, 128), 128), :]
            out_ref[b] = jnp.where(filled, val, 0.0).astype(BF16)
            return carry

        lax.fori_loop(0, count, one_block, 0, unroll=4)


def far_kernel(a_ref, sl_ref, sr_ref, b_ref, wl_ref, wp_ref, dn_ref, up_ref, own_ref, fl_s, fp_s):
    for i, ref in enumerate((a_ref, sl_ref, sr_ref, b_ref)):
        fl_s[:, 3 * i : 3 * i + 3] = ref[0:864, :].reshape(SLOTS, 3, 2, 48, 128)
    fp_s[...] = jnp.zeros_like(fp_s)
    for i, ref in enumerate((a_ref, sl_ref, b_ref)):
        part = ref[864:1152, :].reshape(PSLOTS, 3, 48, 128)
        fp_s[:, 3 * i : 3 * i + 3, 0] = part[:, :, 0:32]
        fp_s[:, 3 * i : 3 * i + 3, 1, 0:16] = part[:, :, 32:48]

    def level(field, weights, slots, xs, pairs, ys, send_at, own_at):
        spots = ys // 2 if ys % 2 == 0 else ys // 2 + 1
        rows = xs * spots * 16
        zero = jnp.zeros((128, 128), BF16)
        for s in range(slots):

            def weight(xi, dy):
                if dy < -3 or dy > 3:
                    return zero
                return weights[s * 56 + xi * 7 + dy + 3]

            accs = []
            lhs = jnp.concatenate(
                [field[s, xi : xi + xs, p].reshape(rows, 128) for xi in range(7) for p in range(2)],
                axis=1,
            )
            for diff in range(-3, 1):
                d = 2 * diff + 3
                rhs = jnp.concatenate(
                    [
                        jnp.concatenate([weight(xi, d + p), weight(xi, d + p - 1)], axis=1)
                        for xi in range(7)
                        for p in range(2)
                    ],
                    axis=0,
                )
                acc = jnp.dot(lhs, rhs, preferred_element_type=F32)
                accs.append(acc.reshape(xs, spots, 16, 256))
            for pair in range(pairs):
                for o in range(2):
                    yo = 2 * pair - 3 + o
                    if yo >= ys + 3:
                        continue
                    val = None
                    for diff in range(-3, 1):
                        ysp = pair + diff
                        if 0 <= ysp < spots:
                            part = accs[diff + 3][:, ysp, :, o * 128 : (o + 1) * 128]
                            val = part if val is None else val + part
                    for x in range(xs):
                        if yo < 0:
                            at = send_at + ((s * xs + x) * 3 + yo + 3) * 16
                            dn_ref[at : at + 16, :] = val[x].astype(BF16)
                        elif yo < ys:
                            at = own_at + ((s * xs + x) * ys + yo) * 16
                            own_ref[at : at + 16, :] = val[x]
                        else:
                            at = send_at + ((s * xs + x) * 3 + yo - ys) * 16
                            up_ref[at : at + 16, :] = val[x].astype(BF16)

    level(fl_s, wl_ref, SLOTS, 6, 6, 6, 0, 0)
    level(fp_s, wp_ref, PSLOTS, 3, 5, 3, 864, 1728)


def join_kernel(own_ref, from_up_ref, from_dn_ref, full_ref, zs_ref):
    for i in range(18):
        for ref, at in ((from_up_ref, 0), (from_dn_ref, 48)):
            rows = slice(i * 96 + at, i * 96 + at + 48)
            total = own_ref[rows, :] + ref[i * 48 : (i + 1) * 48, :].astype(F32)
            full_ref[rows, :] = total
            zs_ref[rows, :] = total.astype(BF16)
    for i in range(6):
        rows = slice(1728 + i * 48, 1776 + i * 48)
        far = slice(864 + i * 48, 912 + i * 48)
        total = own_ref[rows, :] + from_up_ref[far, :].astype(F32) + from_dn_ref[far, :].astype(F32)
        full_ref[rows, :] = total
        zs_ref[rows, :] = total.astype(BF16)


def atoms_kernel(own_ref, other_ref, coef_ref, cell_ref, h_ref, down_ref, out_ref, pf_s, lift_s, l_s, l2_s, l3_s):
    core = lax.axis_index("gz")

    def coef(row):
        return coef_ref[core, row : row + 1, :]

    for i in range(9):
        at = 1728 + i * 16
        values = [
            ref[at + s * 144 : at + s * 144 + 16, :].astype(F32)
            for ref in (own_ref, other_ref)
            for s in range(PSLOTS)
        ]
        for p in range(2):
            pf_s[p, i * 16 : (i + 1) * 16, :] = combine(values, coef, 88 + p * 8).astype(BF16)
    for k in range(3):
        lift_s[k] = lax.dot_general(pf_s[k // 2], down_ref[k % 2], NT, preferred_element_type=F32)
    for x in range(6):
        for y in range(6):
            at = (x * 6 + y) * 16
            values = [
                ref[s * 576 + at : s * 576 + at + 16, :].astype(F32)
                for ref in (own_ref, other_ref)
                for s in range(SLOTS)
            ]
            par = ((x // 2) * 3 + y // 2) * 16
            lane = ((x % 2) * 2 + y % 2) * 128
            for zp in range(3):
                l_s[zp, at : at + 16, :] = (
                    combine(values, coef, 36 + zp * 12) + lift_s[zp, par : par + 16, lane : lane + 128]
                )
    low = low_lanes(40)
    for zp in range(3):
        l_s[zp, 576:640, :] = jnp.zeros((64, 128), F32)
        for cp in range(8):
            a = l_s[zp, pl.ds(2 * cp, 40, stride=16), :]
            b = l_s[zp, pl.ds(2 * cp + 1, 40, stride=16), :]
            first = jnp.where(low, a, pltpu.roll(b, 64, 1))
            second = jnp.where(low, pltpu.roll(a, 64, 1), b)
            for z, val in ((2 * zp, first), (2 * zp + 1, second)):
                hi = val.astype(BF16).astype(F32)
                l2_s[z * 40 : (z + 1) * 40, cp * 128 : (cp + 1) * 128] = hi
                l3_s[z * 40 : (z + 1) * 40, cp * 128 : (cp + 1) * 128] = val - hi
    high_rows = l2_s[...].T.astype(BF16)
    low_rows = l3_s[...].T.astype(BF16)
    number = cell_number_rows()
    for i in range(8):
        one = []
        for half in range(2):
            cells = cell_ref[0, 0, :, i * 256 + half * 128 : i * 256 + half * 128 + 128]
            one.append(jnp.where(number == cells, 1.0, 0.0).astype(BF16))
        one = jnp.concatenate(one, axis=1)
        spread = jnp.dot(high_rows, one, preferred_element_type=F32)
        spread = spread + jnp.dot(low_rows, one, preferred_element_type=F32)
        spread = spread.reshape(CH, 64, 256)[:, 0:56] * h_ref[0:56, i * 256 : (i + 1) * 256][None]
        out_ref[0, 0, 0, :, i * 256 : (i + 1) * 256] = jnp.sum(spread, axis=1)


def call(kernel, outs, scratch, flops=0, moved=0):
    return pl.pallas_call(
        kernel,
        out_shape=outs,
        scratch_shapes=scratch,
        compiler_params=pltpu.CompilerParams(vmem_limit_bytes=48 * MIB),
        cost_estimate=pl.CostEstimate(flops=flops, bytes_accessed=moved, transcendentals=0),
    )


def shape(dims, dtype):
    return jax.ShapeDtypeStruct(dims, dtype)


def ring(axis):
    count = lax.axis_size(axis)
    forward = [(i, (i + 1) % count) for i in range(count)]
    backward = [(target, source) for source, target in forward]
    return forward, backward


def per_device(charges, positions, atom_cells, offsets, far_tables, upward_tables, downward_tables):
    up = jnp.pad(upward_tables, ((0, 0), (0, 15), (0, 15))).transpose(1, 0, 2).reshape(64, 512)
    up = jnp.concatenate([up, up], axis=0)
    down = jnp.pad(downward_tables, ((0, 0), (0, 15), (0, 15))).reshape(512, 64)
    blank = jnp.zeros_like(down)
    down = jnp.stack(
        [jnp.concatenate([down, blank], axis=1), jnp.concatenate([blank, down], axis=1)], axis=0
    )
    off = offsets.transpose(0, 2, 1)
    coefs = jnp.asarray(COEFS)
    swap = [(0, 1), (1, 0)]

    zs, harm = call(
        poles_kernel,
        (shape((2016, 128), BF16), shape((64, 2048), F32)),
        [
            pltpu.VMEM((48, 128), F32),
            pltpu.VMEM((1024, 128), F32),
            pltpu.VMEM((16, 2048), F32),
            pltpu.VMEM((1024, 2048), BF16),
            pltpu.VMEM((1024, 2048), BF16),
            pltpu.VMEM((240, 2048), BF16),
            pltpu.VMEM((3, 640, 128), F32),
        ],
        2 * 2 * 256 * 2048 * 1024,
        2 * MIB,
    )(charges, positions, atom_cells, up)
    zother = lax.ppermute(zs, "gz", swap)
    wl, wp = pl.pallas_call(
        table_kernel,
        out_shape=(shape((168, 128, 128), BF16), shape((112, 128, 128), BF16)),
        in_specs=[
            pl.BlockSpec(memory_space=pltpu.VMEM),
            pl.BlockSpec(memory_space=pltpu.SMEM),
            pl.BlockSpec(memory_space=pltpu.VMEM),
        ],
        scratch_shapes=[
            pltpu.VMEM((64 * 56, 128), F32),
            pltpu.VMEM((168 * 128, 128), F32),
            pltpu.VMEM((336, 256), F32),
        ],
        compiler_params=pltpu.CompilerParams(vmem_limit_bytes=48 * MIB),
        cost_estimate=pl.CostEstimate(
            flops=2 * 49 * 560 * 256 * 256, bytes_accessed=20 * MIB, transcendentals=0
        ),
    )(off, jnp.asarray(ZTABLE), far_tables)
    sl, sr = call(
        forward_kernel, (shape((1152, 128), BF16), shape((1152, 128), BF16)), [], 0, 2 * MIB
    )(zs, zother, coefs)
    forward, backward = ring("gx")
    from_left = lax.ppermute(sr, "gx", forward)
    from_right = lax.ppermute(sl, "gx", backward)
    dn, ups, own = call(
        far_kernel,
        (shape((1152, 128), BF16), shape((1152, 128), BF16), shape((2016, 128), F32)),
        [pltpu.VMEM((SLOTS, 12, 2, 48, 128), BF16), pltpu.VMEM((PSLOTS, 9, 2, 32, 128), BF16)],
        2 * 288 * 1792 * 256 * 20,
        14 * MIB,
    )(from_left, sl, sr, from_right, wl, wp)
    forward, backward = ring("gy")
    from_above = lax.ppermute(dn, "gy", backward)
    from_below = lax.ppermute(ups, "gy", forward)
    full, zsend = call(
        join_kernel, (shape((2016, 128), F32), shape((2016, 128), BF16)), [], 0, 3 * MIB
    )(own, from_below, from_above)
    zrecv = lax.ppermute(zsend, "gz", swap)
    potential = call(
        atoms_kernel,
        shape((1, 1, 1, CH, 2048), F32),
        [
            pltpu.VMEM((2, 144, 128), BF16),
            pltpu.VMEM((3, 144, 512), F32),
            pltpu.VMEM((3, 640, 128), F32),
            pltpu.VMEM((240, 1024), F32),
            pltpu.VMEM((240, 1024), F32),
        ],
        2 * 2 * 256 * 2048 * 1024,
        2 * MIB,
    )(full, zrecv, coefs, atom_cells, harm, down)
    return potential


def solution(mesh):
    placed = (
        P("gx", "gy", "gz", None, None),
        P("gx", "gy", "gz", None, None),
        P("gx", "gy", "gz", None),
        P(),
        P(),
        P(),
        P(),
    )
    return jax.shard_map(
        per_device,
        mesh=mesh,
        in_specs=placed,
        out_specs=P("gx", "gy", "gz", None, None),
        check_vma=False,
    )
```

time: 698 us -> 66.7 us (0.10)
  local copies, waits for them, and re-layouts: 574 us -> 5.56 us
  matrix products: 55.2 us -> 0 us
  Pallas kernels: 0 us -> 36.5 us
  starting transfers between devices: 38.8 us -> 15.2 us
  other arithmetic: 14.6 us -> 0.04 us
    another operation x18 -> x1, local copies, waits for them, and re-layouts: 204 us -> 0.11 us  [per_device(): jnp.stack([jnp.concatenate([down, blank], axis=1), jnp.concatenate([blank...]
    gather x15 -> x0, local copies, waits for them, and re-layouts: 159 us -> none  [take_window(): return lax.dynamic_slice(shaped, begin, (1, y_block, ext_z, CH, TERMS))]
    transpose x18 -> x1, local copies, waits for them, and re-layouts: 157 us -> 0.92 us  [per_device(): jnp.pad(upward_tables, ((0, 0), (0, 15), (0, 15))).transpose(1, 0, 2)]
    dot_general x19 -> x0, matrix products: 55.2 us -> none  [the longest x15 44.1 us: far_field(): product = jnp.dot(row_block, table_rows, preferred_element_type=jnp.float32)]
    pallas_call x0 -> x6, Pallas kernels: none -> 36.5 us  [the longest x1 19 us: per_device(): pl.pallas_call(table_kernel, out_shape=(shape((168, 128, 128), BF16), sha...]
    reshape x7 -> x1, local copies, waits for them, and re-layouts: 31.3 us -> 0.14 us  [per_device(): jnp.pad(upward_tables, ((0, 0), (0, 15), (0, 15))).transpose(1, 0, 2)]
    ppermute x12 -> x6, starting transfers between devices: 38.8 us -> 15.2 us  [the longest x1 6.32 us: per_device(): from_above = lax.ppermute(dn, 'gy', backward)]
    concatenate x10 -> x1, other arithmetic: 8.08 us -> 0.01 us  [per_device(): up = jnp.concatenate([up, up], axis=0)]
  transfers between devices with their start and end apart: 12 -> 6, of which waited for: 1 -> 3; matrix products, arithmetic and copies ran while one was open for 14% -> 1% of each run, Pallas kernels for 0% -> 29%
where the time goes in v1:
time: 66.7 us; the launch traced here: 66.4 us
  Pallas kernels  36.5 us (55%)
  starting transfers between devices  15.2 us (23%)
  waiting for transfers between devices  9.04 us (14%)
  local copies, waits for them, and re-layouts  5.56 us (8%)
    pallas_call x1, Pallas kernels, per_device(): pl.pallas_call(table_kernel, out_shape=(shape((168, 128, 128), BF16), sha...  19 us
    pallas_call x1, Pallas kernels, per_device(): call(far_kernel, (shape((1152, 128), BF16), shape((1152, 128), BF16), sha...  8.1 us
    ppermute x1, waiting for transfers between devices, per_device(): from_below = lax.ppermute(ups, 'gy', forward)  6.4 us
    ppermute x1, starting transfers between devices, per_device(): from_above = lax.ppermute(dn, 'gy', backward)  6.32 us
    pallas_call x1, Pallas kernels, per_device(): call(atoms_kernel, shape((1, 1, 1, CH, 2048), F32), [pltpu.VMEM((2, 144,...  4.62 us
    unnamed x22, local copies, waits for them, and re-layouts  4.37 us
    pallas_call x1, Pallas kernels, per_device(): call(poles_kernel, (shape((2016, 128), BF16), shape((64, 2048), F32)), [p...  3.57 us
    ppermute x1, starting transfers between devices, per_device(): from_right = lax.ppermute(sl, 'gx', backward)  3.56 us
  transfers between devices with their start and end apart: 6, of which 3 were waited for; matrix products, arithmetic and copies ran while one was open for 1% of the time, Pallas kernels for 29%

profile of v1, /device:TPU:1, one launch (start us, length us, event | category | flops | bytes accessed | tf_op | source)
XLA Modules:
  0.0 66.4 jit_solution(9423907130201530756)
XLA Ops:
  0.0 0.9 %pad_bitcast_fusion.2 = bf16[64,8,64]{2,1,0:T(8,128)(2,1)S(1)} fusion(bf16[8,49,49]{2,0,1:T(8,128)(2,1)} %param.14), kind=kLoop, calls=%fused_computation.4 | loop fusion | bytes 103952 | tf_op jit(solution)/shard_map/transpose | solution.py:465
  0.9 0.1 reshape.6
  1.1 0.8 %copy.10.pos_ref = f32[1,1,1,3,2048]{4,3,2,1,0:T(4,128)S(1)} copy(f32[1,1,1,3,2048]{4,2,3,1,0:T(1,128)} %param.10) | data formatting | bytes 49152 | tf_op args[1]
  1.8 0.0 copy-start.1
  1.9 0.8 %copy-done.1 = bf16[1,1,1,16,2048]{4,3,2,1,0:T(8,128)(2,1)S(1)} copy-done((bf16[1,1,1,16,2048]{4,3,2,1,0:T(8,128)(2,1)S(1)}, bf16[1,1,1,16,2048]{4,3,2,1,0:T(8,128)(2,1)}, u32[]{:S(2)}) %copy-start.1) | copy-done | bytes 65560
  2.7 0.0 copy-start.2
  2.7 0.7 %copy-done.2 = s32[1,1,1,2048]{3,2,1,0:T(1,128)S(1)} copy-done((s32[1,1,1,2048]{3,2,1,0:T(1,128)S(1)}, s32[1,1,1,2048]{3,2,1,0:T(1,128)}, u32[]{:S(2)}) %copy-start.2) | copy-done | bytes 8216
  3.4 0.0 copy-start.6
  3.4 0.0 copy-start.8
  3.4 0.0 copy-start
  3.4 3.6 %shard_map.91 = (bf16[2016,128]{1,0:T(8,128)(2,1)S(1)}, f32[64,2048]{1,0:T(8,128)S(1)}) custom-call(bf16[1,1,1,16,2048]{4,3,2,1,0:T(8,128)(2,1)S(1)} %copy-done.1, f32[1,1,1,3,2048]{4,3,2,1,0:T(4,128)S(1)} %copy.10.pos_ref, s32[1,1,1,2048]{3,2,1,0:T(1,128)S(1)} %copy-done.2, bf16[128,512]{1,0:T(8,128)(2,1)S(1)} %pad_maximum_fusion.1.up_ref), custom_call_target="tpu_custom_call" | custom-call | flops 2147483648 | bytes 2097152 | tf_op jit(solution)/shard_map/pallas_call | solution.py:476
  7.0 0.0 copy-start.4
  7.0 3.3 %collective-permute-start = (bf16[2016,128]{1,0:T(8,128)(2,1)S(1)}, bf16[2016,128]{1,0:T(8,128)(2,1)S(1)}, u32[]{:S(2)}, u32[]{:S(2)}) collective-permute-start(bf16[2016,128]{1,0:T(8,128)(2,1)S(1)} %get-tuple-element.16.own_ref), channel_id=1, source_target_pairs={{0,1},{1,0},{2,3},{3,2},{4,5},{5,4},{6,7},{7,6},{8,9},{9,8},{10,11... | collective-permute-start | bytes 1548296 | tf_op jit(solution)/shard_map/ppermute | solution.py:491
  10.3 0.0 copy-done.6
  10.3 0.2 copy.12.far_ref
  10.5 0.0 copy-done.8
  10.5 1.3 %collective-permute-done.other_ref = bf16[2016,128]{1,0:T(8,128)(2,1)S(1)} collective-permute-done((bf16[2016,128]{1,0:T(8,128)(2,1)S(1)}, bf16[2016,128]{1,0:T(8,128)(2,1)S(1)}, u32[]{:S(2)}, u32[]{:S(2)}) %collective-permute-start) | collective-permute-done | bytes 516128 | tf_op jit(solution)/shard_map/ppermute | solution.py:491
  11.8 0.0 copy-done
  11.8 1.0 %shard_map.92 = (bf16[1152,128]{1,0:T(8,128)(2,1)S(1)}, bf16[1152,128]{1,0:T(8,128)(2,1)S(1)}) custom-call(bf16[2016,128]{1,0:T(8,128)(2,1)S(1)} %get-tuple-element.16.own_ref, bf16[2016,128]{1,0:T(8,128)(2,1)S(1)} %collective-permute-done.other_ref, f32[2,104,128]{2,1,0:T(8,128)S(1)} %copy-done), custom_call_target="tpu_custom_call" | custom-call | bytes 2097152 | tf_op jit(solution)/shard_map/pallas_call | solution.py:510
  12.8 0.1 collective-permute-start.1
  12.9 3.6 %collective-permute-start.2 = (bf16[1152,128]{1,0:T(8,128)(2,1)S(1)}, bf16[1152,128]{1,0:T(8,128)(2,1)S(1)}, u32[]{:S(2)}, u32[]{:S(2)}) collective-permute-start(bf16[1152,128]{1,0:T(8,128)(2,1)S(1)} %get-tuple-element.18.sl_ref), channel_id=1, source_target_pairs={{32,0},{64,32},{96,64},{128,96},{160,128},{192,160},{224,192},{0,2... | collective-permute-start | bytes 884744 | tf_op jit(solution)/shard_map/ppermute | solution.py:515
  16.5 0.0 copy-done.4
  16.5 19.0 %shard_map.93 = (bf16[168,128,128]{2,1,0:T(8,128)(2,1)}, bf16[112,128,128]{2,1,0:T(8,128)(2,1)S(1)}) custom-call(s32[2,3,128]{2,1,0:T(4,128)S(1)} %bitcast.10, f32[160]{0:T(256)S(1)} %copy-done.4, bf16[2,49,49,128]{3,2,1,0:T(8,128)(2,1)S(1)} %copy.12.far_ref), custom_call_target="tpu_custom_call" | custom-call | flops 3596615680 | bytes 20971520 | tf_op jit(solution)/shard_map/pallas_call | solution.py:492
  35.5 0.0 copy-start.5
  35.5 1.8 %copy-done.5 = bf16[112,128,128]{2,1,0:T(8,128)(2,1)} copy-done((bf16[112,128,128]{2,1,0:T(8,128)(2,1)}, bf16[112,128,128]{2,1,0:T(8,128)(2,1)S(1)}, u32[]{:S(2)}) %copy-start.5) | copy-done | bytes 3670040
  37.4 0.0 collective-permute-done.1.a_ref
  37.4 0.0 collective-permute-done.2.b_ref
  37.4 0.0 copy-start.7
  37.4 0.0 copy-start.3
  37.4 8.1 %shard_map.94 = (bf16[1152,128]{1,0:T(8,128)(2,1)S(1)}, bf16[1152,128]{1,0:T(8,128)(2,1)S(1)}, f32[2016,128]{1,0:T(8,128)S(1)}) custom-call(bf16[1152,128]{1,0:T(8,128)(2,1)S(1)} %collective-permute-done.1.a_ref, bf16[1152,128]{1,0:T(8,128)(2,1)S(1)} %get-tuple-element.18.sl_ref, bf16[1152,128]{1,0:T(8,128)(2,1)S(1)} %get-tuple-element.17.sr_ref, ...), custom_call_target="tpu_custom_call" | custom-call | flops 5284823040 | bytes 14680064 | tf_op jit(solution)/shard_map/pallas_call | solution.py:516
  45.5 0.3 collective-permute-start.3
  45.8 6.3 %collective-permute-start.4 = (bf16[1152,128]{1,0:T(8,128)(2,1)S(1)}, bf16[1152,128]{1,0:T(8,128)(2,1)S(1)}, u32[]{:S(2)}, u32[]{:S(2)}) collective-permute-start(bf16[1152,128]{1,0:T(8,128)(2,1)S(1)} %get-tuple-element.23), channel_id=1, source_target_pairs={{2,0},{4,2},{6,4},{8,6},{10,8},{12,10},{14,12},{16,14},{18,16},{20... | collective-permute-start | bytes 884744 | tf_op jit(solution)/shard_map/ppermute | solution.py:524
  52.2 6.4 %collective-permute-done.3.from_up_ref = bf16[1152,128]{1,0:T(8,128)(2,1)S(1)} collective-permute-done((bf16[1152,128]{1,0:T(8,128)(2,1)S(1)}, bf16[1152,128]{1,0:T(8,128)(2,1)S(1)}, u32[]{:S(2)}, u32[]{:S(2)}) %collective-permute-start.3) | collective-permute-done | bytes 294944 | tf_op jit(solution)/shard_map/ppermute | solution.py:525
  58.6 0.0 collective-permute-done.4.from_dn_ref
  58.6 0.1 shard_map.95
  58.7 1.6 %collective-permute-start.5 = (bf16[2016,128]{1,0:T(8,128)(2,1)S(1)}, bf16[2016,128]{1,0:T(8,128)(2,1)S(1)}, u32[]{:S(2)}, u32[]{:S(2)}) collective-permute-start(bf16[2016,128]{1,0:T(8,128)(2,1)S(1)} %get-tuple-element.25), channel_id=1, source_target_pairs={{0,1},{1,0},{2,3},{3,2},{4,5},{5,4},{6,7},{7,6},{8,9},{9,8},{10,11... | collective-permute-start | bytes 1548296 | tf_op jit(solution)/shard_map/ppermute | solution.py:529
  60.3 0.0 copy-done.7
  60.3 0.1 pad_bitcast_fusion.1
  60.5 1.3 %collective-permute-done.5.other_ref = bf16[2016,128]{1,0:T(8,128)(2,1)S(1)} collective-permute-done((bf16[2016,128]{1,0:T(8,128)(2,1)S(1)}, bf16[2016,128]{1,0:T(8,128)(2,1)S(1)}, u32[]{:S(2)}, u32[]{:S(2)}) %collective-permute-start.5) | collective-permute-done | bytes 516128 | tf_op jit(solution)/shard_map/ppermute | solution.py:529
  61.8 0.0 copy-done.3
  61.8 4.6 %shard_map.96 = f32[1,1,1,16,2048]{4,3,2,1,0:T(8,128)} custom-call(f32[2016,128]{1,0:T(8,128)S(1)} %get-tuple-element.24.own_ref, bf16[2016,128]{1,0:T(8,128)(2,1)S(1)} %collective-permute-done.5.other_ref, f32[2,104,128]{2,1,0:T(8,128)S(1)} %copy-done, s32[1,1,1,2048]{3,2,1,0:T(1,128)S(1)} %copy-done.3, f32[64,2048]{1,0:T(8,128)S(1)} %get-tuple-element.26.h_ref, ...), custom_call_target="tpu_custom_call" | custom-call | flops 2147483648 | bytes 2097152 | tf_op jit(solution)/shard_map/pallas_call | solution.py:530
  (5 shorter events, 0.1 us)
Async XLA Ops:
  1.8 0.8 %copy-start.1 = (bf16[1,1,1,16,2048]{4,3,2,1,0:T(8,128)(2,1)S(1)}, bf16[1,1,1,16,2048]{4,3,2,1,0:T(8,128)(2,1)}, u32[]{:S(2)}) copy-start(bf16[1,1,1,16,2048]{4,3,2,1,0:T(8,128)(2,1)} %ch_ref.1) | copy-start | bytes 196612
  2.7 0.7 %copy-start.2 = (s32[1,1,1,2048]{3,2,1,0:T(1,128)S(1)}, s32[1,1,1,2048]{3,2,1,0:T(1,128)}, u32[]{:S(2)}) copy-start(s32[1,1,1,2048]{3,2,1,0:T(1,128)} %cell_ref.3) | copy-start | bytes 24580
  3.4 6.9 %copy-start.6 = (bf16[2,49,49,128]{3,0,2,1:T(2,128)(2,1)S(1)}, bf16[2,49,49,128]{3,0,2,1:T(2,128)(2,1)}, u32[]{:S(2)}) copy-start(bf16[2,49,49,128]{3,0,2,1:T(2,128)(2,1)} %param.13) | copy-start | bytes 3687940
  3.4 7.1 %copy-start.8 = (s32[2,128,3]{1,0,2:T(2,128)S(1)}, s32[2,128,3]{1,0,2:T(2,128)}, u32[]{:S(2)}) copy-start(s32[2,128,3]{1,0,2:T(2,128)} %param.12) | copy-start | bytes 9220
  3.4 8.4 %copy-start = (f32[2,104,128]{2,1,0:T(8,128)S(1)}, f32[2,104,128]{2,1,0:T(8,128)}, u32[]{:S(2)}) copy-start(f32[2,104,128]{2,1,0:T(8,128)} %constant.8.clone.coef_ref) | copy-start | bytes 319492
  7.0 9.5 %copy-start.4 = (f32[160]{0:T(256)S(1)}, f32[160]{0:T(256)}, u32[]{:S(2)}) copy-start(f32[160]{0:T(256)} %constant.9.clone.zt_ref) | copy-start | bytes 1924
  7.0 4.9 %collective-permute-start = (bf16[2016,128]{1,0:T(8,128)(2,1)S(1)}, bf16[2016,128]{1,0:T(8,128)(2,1)S(1)}, u32[]{:S(2)}, u32[]{:S(2)}) collective-permute-start(bf16[2016,128]{1,0:T(8,128)(2,1)S(1)} %get-tuple-element.16.own_ref), channel_id=1, source_target_pairs={{0,1},{1,0},{2,3},{3,2},{4,5},{5,4},{6,7},{7,6},{8,9},{9,8},{10,11... | collective-permute-start | bytes 1548296 | tf_op jit(solution)/shard_map/ppermute | solution.py:491
  12.8 24.5 %collective-permute-start.1 = (bf16[1152,128]{1,0:T(8,128)(2,1)S(1)}, bf16[1152,128]{1,0:T(8,128)(2,1)S(1)}, u32[]{:S(2)}, u32[]{:S(2)}) collective-permute-start(bf16[1152,128]{1,0:T(8,128)(2,1)S(1)} %get-tuple-element.17.sr_ref), channel_id=1, source_target_pairs={{0,32},{32,64},{64,96},{96,128},{128,160},{160,192},{192,224},{224... | collective-permute-start | bytes 884744 | tf_op jit(solution)/shard_map/ppermute | solution.py:514
  12.9 24.4 %collective-permute-start.2 = (bf16[1152,128]{1,0:T(8,128)(2,1)S(1)}, bf16[1152,128]{1,0:T(8,128)(2,1)S(1)}, u32[]{:S(2)}, u32[]{:S(2)}) collective-permute-start(bf16[1152,128]{1,0:T(8,128)(2,1)S(1)} %get-tuple-element.18.sl_ref), channel_id=1, source_target_pairs={{32,0},{64,32},{96,64},{128,96},{160,128},{192,160},{224,192},{0,2... | collective-permute-start | bytes 884744 | tf_op jit(solution)/shard_map/ppermute | solution.py:515
  35.5 1.8 %copy-start.5 = (bf16[112,128,128]{2,1,0:T(8,128)(2,1)}, bf16[112,128,128]{2,1,0:T(8,128)(2,1)S(1)}, u32[]{:S(2)}) copy-start(bf16[112,128,128]{2,1,0:T(8,128)(2,1)S(1)} %get-tuple-element.20.wp_ref) | copy-start | bytes 11010052
  37.4 22.9 %copy-start.7 = (bf16[8,49,49]{2,0,1:T(8,128)(2,1)S(1)}, bf16[8,49,49]{2,0,1:T(8,128)(2,1)}, u32[]{:S(2)}) copy-start(bf16[8,49,49]{2,0,1:T(8,128)(2,1)} %param.15) | copy-start | bytes 115252
  37.4 24.4 %copy-start.3 = (s32[1,1,1,2048]{3,2,1,0:T(1,128)S(1)}, s32[1,1,1,2048]{3,2,1,0:T(1,128)}, u32[]{:S(2)}) copy-start(s32[1,1,1,2048]{3,2,1,0:T(1,128)} %cell_ref.3) | copy-start | bytes 24580
  45.5 13.1 %collective-permute-start.3 = (bf16[1152,128]{1,0:T(8,128)(2,1)S(1)}, bf16[1152,128]{1,0:T(8,128)(2,1)S(1)}, u32[]{:S(2)}, u32[]{:S(2)}) collective-permute-start(bf16[1152,128]{1,0:T(8,128)(2,1)S(1)} %get-tuple-element.22), channel_id=1, source_target_pairs={{0,2},{2,4},{4,6},{6,8},{8,10},{10,12},{12,14},{14,16},{16,18},{18... | collective-permute-start | bytes 884744 | tf_op jit(solution)/shard_map/ppermute | solution.py:525
  45.8 12.7 %collective-permute-start.4 = (bf16[1152,128]{1,0:T(8,128)(2,1)S(1)}, bf16[1152,128]{1,0:T(8,128)(2,1)S(1)}, u32[]{:S(2)}, u32[]{:S(2)}) collective-permute-start(bf16[1152,128]{1,0:T(8,128)(2,1)S(1)} %get-tuple-element.23), channel_id=1, source_target_pairs={{2,0},{4,2},{6,4},{8,6},{10,8},{12,10},{14,12},{16,14},{18,16},{20... | collective-permute-start | bytes 884744 | tf_op jit(solution)/shard_map/ppermute | solution.py:524
  58.7 3.1 %collective-permute-start.5 = (bf16[2016,128]{1,0:T(8,128)(2,1)S(1)}, bf16[2016,128]{1,0:T(8,128)(2,1)S(1)}, u32[]{:S(2)}, u32[]{:S(2)}) collective-permute-start(bf16[2016,128]{1,0:T(8,128)(2,1)S(1)} %get-tuple-element.25), channel_id=1, source_target_pairs={{0,1},{1,0},{2,3},{3,2},{4,5},{5,4},{6,7},{7,6},{8,9},{9,8},{10,11... | collective-permute-start | bytes 1548296 | tf_op jit(solution)/shard_map/ppermute | solution.py:529

commit v2 on v1

v2 whole, which is shorter than its diff:
```python
import math

import numpy as np
import jax
import jax.numpy as jnp
from jax import lax
from jax.experimental import pallas as pl
from jax.experimental.pallas import tpu as pltpu
from jax.sharding import PartitionSpec as P

CH = 16
ORDER = 6
TERMS = 49
NOFF = 128
SLOTS = 3
PSLOTS = 2
F32 = jnp.float32
BF16 = jnp.bfloat16
NT = (((1,), (1,)), ((), ()))
TN = (((0,), (0,)), ((), ()))
radial_scale = 1.6
MIB = 1 << 20


def spectral_constants():
    leaf_freq = [[None, 2, 4], [1, 3, 5]]
    pair_freq = [[2, 0], [1, 3]]
    turn = 2 * math.pi / 12
    pturn = 2 * math.pi / 6

    def fwd(core, s, ri, z):
        f = leaf_freq[core][s]
        if f is None:
            return float(z % 2 == ri)
        return math.cos(turn * f * z) if ri == 0 else -math.sin(turn * f * z)

    def inv(core, s, ri, z):
        f = leaf_freq[core][s]
        if f is None:
            return float(z % 2 == ri) / 6
        return (math.cos(turn * f * z) if ri == 0 else -math.sin(turn * f * z)) / 6

    def pfwd(core, s, ri, z):
        f = pair_freq[core][s]
        if s == 1:
            return math.cos(pturn * f * z) if ri == 0 else 0.0
        return math.cos(pturn * f * z) if ri == 0 else -math.sin(pturn * f * z)

    def pinv(core, s, ri, z):
        return pfwd(core, s, ri, z) / (6 if s == 1 else 3)

    halves = np.zeros((2, 104, 128))
    for core in range(2):
        row = 0

        def put(a, b):
            nonlocal row
            halves[core, row, :64] = a
            halves[core, row, 64:] = b
            row += 1

        for s in range(SLOTS):
            for v in range(6):
                z = (core if v < 3 else 1 - core) * 6 + 2 * (v % 3)
                put(fwd(core, s, 0, z), fwd(core, s, 1, z + 1))
                put(fwd(core, s, 0, z + 1), fwd(core, s, 1, z))
        for p in range(3):
            z = core * 6 + 2 * p
            for u in range(6):
                own = core if u < 3 else 1 - core
                s = u % 3
                put(inv(own, s, 0, z), inv(own, s, 1, z + 1))
                put(inv(own, s, 1, z), inv(own, s, 0, z + 1))
        for s in range(PSLOTS):
            for v in range(4):
                z = (core if v < 2 else 1 - core) * 3 + 2 * (v % 2)
                on = float(v % 2 == 0)
                put(pfwd(core, s, 0, z), on * pfwd(core, s, 1, z + 1))
                put(on * pfwd(core, s, 0, z + 1), pfwd(core, s, 1, z))
        for p in range(2):
            z = core * 3 + 2 * p
            on = float(p == 0)
            for u in range(4):
                own = core if u < 2 else 1 - core
                s = u % 2
                put(pinv(own, s, 0, z), on * pinv(own, s, 1, z + 1))
                put(pinv(own, s, 1, z), on * pinv(own, s, 0, z + 1))
        assert row == 104
    table = np.zeros((2, 80))
    for core in range(2):
        for pq in range(2):
            for s in range(SLOTS):
                f = leaf_freq[core][s]
                for d in range(7):
                    dz = d - 3
                    if f is None:
                        val = float(dz % 2 == pq)
                    else:
                        val = math.sin(turn * f * dz) if pq else math.cos(turn * f * dz)
                    table[core, (pq * SLOTS + s) * 7 + d] = val
            for s in range(PSLOTS):
                f = pair_freq[core][s]
                for d in range(7):
                    dz = d - 3
                    if s == 1:
                        val = 0.0 if pq else math.cos(pturn * f * dz)
                    else:
                        val = math.sin(pturn * f * dz) if pq else math.cos(pturn * f * dz)
                    table[core, 42 + (pq * PSLOTS + s) * 7 + d] = val
        table[core, 70] = 1.0 if core == 0 else -1.0
    return halves.astype(np.float32), table.reshape(-1).astype(np.float32)


COEFS, ZTABLE = spectral_constants()


def harmonic_terms(x, y, z):
    rsq = x * x + y * y + z * z
    cosines = {(0, 0): jnp.ones_like(x)}
    sines = {}
    for deg in range(1, ORDER + 1):
        for m in range(deg):
            inv = 1.0 / float((deg + m) * (deg - m))
            for part in (cosines, sines):
                if part is sines and m == 0:
                    continue
                val = ((2 * deg - 1) * inv) * (z * part[deg - 1, m])
                if m <= deg - 2:
                    val = val - inv * (rsq * part[deg - 2, m])
                part[deg, m] = val
        scale = -1.0 / (2.0 * deg)
        pc = cosines[deg - 1, deg - 1]
        if deg == 1:
            cosines[1, 1] = scale * x
            sines[1, 1] = scale * y
        else:
            ps = sines[deg - 1, deg - 1]
            cosines[deg, deg] = scale * (x * pc - y * ps)
            sines[deg, deg] = scale * (x * ps + y * pc)
    out = []
    for deg in range(ORDER + 1):
        out.append(cosines[deg, 0] * float(math.factorial(deg)))
        for m in range(1, deg + 1):
            factor = math.sqrt(math.factorial(deg + m) * math.factorial(deg - m))
            out.append(cosines[deg, m] * factor)
            out.append(sines[deg, m] * factor)
    return out


def low_lanes(rows):
    return lax.broadcasted_iota(jnp.int32, (rows, 128), 1) < 64


def cell_number_rows():
    row = lax.broadcasted_iota(jnp.int32, (240, 128), 0)
    z = jnp.zeros_like(row)
    for i in range(1, 6):
        z = z + (row >= 40 * i).astype(jnp.int32)
    xy = row - 40 * z
    return jnp.where(xy < 36, xy * 6 + z, -1)


def start_copies(pairs, sems):
    copies = [pltpu.make_async_copy(src, dst, sems.at[i]) for i, (src, dst) in enumerate(pairs)]
    for copy in copies:
        copy.start()
    return copies


def fill_harmonics(pos_s, h3_s, h_ref):
    terms = harmonic_terms(
        radial_scale * pos_s[0:16, :], radial_scale * pos_s[16:32, :], radial_scale * pos_s[32:48, :]
    )
    for k in range(TERMS):
        h3_s[k * 16 : (k + 1) * 16, :] = terms[k]
    h3_s[TERMS * 16 : 1024, :] = jnp.zeros((1024 - TERMS * 16, 128), F32)
    for i in range(16):
        h_ref[:, i * 128 : (i + 1) * 128] = h3_s[pl.ds(i, 64, stride=16), :]


def fill_onehot(cell_s, one_ref):
    number = cell_number_rows()
    for i in range(16):
        one_ref[:, i * 128 : (i + 1) * 128] = jnp.where(number == cell_s[i : i + 1, :], 1.0, 0.0).astype(BF16)


def atom_terms_kernel(pos_ref, cell_ref, h_ref, one_ref, h3_s):
    fill_harmonics(pos_ref, h3_s, h_ref)
    fill_onehot(cell_ref, one_ref)


def poles_kernel(ch_hbm, pos_hbm, cell_hbm, zs_ref, h_s, one_s, ch_s, pos_s, cell_s, h3_s, chf_s, whi_s, wlo_s, rt_s, f_s, sems):
    copies = start_copies(((pos_hbm, pos_s), (cell_hbm, cell_s), (ch_hbm.at[0, 0, 0], ch_s)), sems)
    copies[0].wait()
    fill_harmonics(pos_s, h3_s, h_s)
    copies[1].wait()
    fill_onehot(cell_s, one_s)
    copies[2].wait()
    chf_s[...] = ch_s[...].astype(F32)
    for c in range(CH):
        for i in range(4):
            sl = slice(i * 512, (i + 1) * 512)
            w = h_s[:, sl] * chf_s[c : c + 1, sl]
            hi = w.astype(BF16)
            whi_s[c * 64 : (c + 1) * 64, sl] = hi
            wlo_s[c * 64 : (c + 1) * 64, sl] = (w - hi.astype(F32)).astype(BF16)
    low = low_lanes(40)
    rt_s[...] = lax.dot_general(whi_s[...], one_s[...], NT, preferred_element_type=F32) + lax.dot_general(
        wlo_s[...], one_s[...], NT, preferred_element_type=F32
    )
    for n in range(4):
        r = rt_s[n * 256 : (n + 1) * 256, :].T
        for half in range(2):
            c = n * 4 + half * 2
            for zp in range(3):
                a = r[zp * 80 : zp * 80 + 40, half * 128 : half * 128 + 128]
                b = r[zp * 80 + 40 : zp * 80 + 80, half * 128 : half * 128 + 128]
                f_s[zp, pl.ds(c, 40, stride=16), :] = jnp.where(low, a, pltpu.roll(b, 64, 1))
                f_s[zp, pl.ds(c + 1, 40, stride=16), :] = jnp.where(low, pltpu.roll(a, 64, 1), b)
    for zp in range(3):
        zs_ref[zp * 576 : (zp + 1) * 576, :] = f_s[zp, 0:576, :].astype(BF16)


def combine(values, coef, row):
    total = None
    for v, val in enumerate(values):
        part = val * coef(row + 2 * v) + pltpu.roll(val, 64, 1) * coef(row + 2 * v + 1)
        total = part if total is None else total + part
    return total


def lane_in_half(rows):
    return lax.broadcasted_iota(jnp.int32, (rows, 128), 1) & 63


def pack_three(firsts, seconds, thirds):
    lane = lane_in_half(16)
    outs_a, outs_b, pieces = [], [], []
    for i in range(3):
        outs_a.append(jnp.where(lane < TERMS, firsts[i], pltpu.roll(thirds[i], 49, 1)).astype(BF16))
        outs_b.append(jnp.where(lane < TERMS, seconds[i], pltpu.roll(thirds[i], 34, 1)).astype(BF16))
        pieces.append(pltpu.roll(thirds[i], (98, 117, 8)[i], 1))
    rest = jnp.where(lane < 19, pieces[0], jnp.where(lane < 38, pieces[1], pieces[2]))
    return outs_a, outs_b, rest.astype(BF16)


def unpack_third(first, second, rest, i):
    lane = lane_in_half(16)
    tail = pltpu.roll(rest, (30, 11, 120)[i], 1)
    return jnp.where(
        lane < 15, pltpu.roll(first, 79, 1), jnp.where(lane < 30, pltpu.roll(second, 94, 1), tail)
    )


def pack_pairs(ref, base, blocks):
    low = low_lanes(16)
    for i in range(5):
        other = pltpu.roll(blocks[2 * i + 1], 64, 1) if 2 * i + 1 < 9 else blocks[2 * i]
        ref[base + i * 16 : base + (i + 1) * 16, :] = jnp.where(low, blocks[2 * i], other).astype(BF16)


def unpack_pair(ref, base, b):
    val = ref[base + (b // 2) * 16 : base + (b // 2) * 16 + 16, :].astype(F32)
    return pltpu.roll(val, 64, 1) if b % 2 else val


def parents_of(ref, up_ref):
    low = low_lanes(144)
    res = []
    for zp in range(3):
        split = ref[zp * 576 : (zp + 1) * 576, :].reshape(3, 2, 3, 2, 16, 128)
        lhs = jnp.concatenate(
            [split[:, p, :, q].reshape(144, 128) for p in range(2) for q in range(2)], axis=1
        )
        res.append(lax.dot_general(lhs, up_ref[...], NT, preferred_element_type=F32))
    return jnp.where(low, res[0], res[1]).astype(BF16), jnp.where(low, res[2], 0.0).astype(BF16)


def half_kernel(own_ref, coef_ref, up_ref, part_ref, pown_ref):
    core = lax.axis_index("gz")

    def coef(row):
        return coef_ref[core, row : row + 1, :]

    for b in range(36):
        values = [own_ref[zp * 576 + b * 16 : zp * 576 + b * 16 + 16, :].astype(F32) for zp in range(3)]
        for s in range(SLOTS):
            part_ref[s, b * 16 : b * 16 + 16, :] = combine(values, coef, s * 12)
    pown_ref[0], pown_ref[1] = parents_of(own_ref, up_ref)


def forward_kernel(part_ref, pown_ref, other_ref, coef_ref, up_ref, fa_ref, fb_ref, fo_ref, po_ref, pp_s):
    core = lax.axis_index("gz")
    odd = lax.rem(lax.axis_index("gx"), 2)

    def coef(row):
        return coef_ref[core, row : row + 1, :]

    for face, base in ((fa_ref, 3 - 3 * odd), (fb_ref, 3 * odd)):
        for xx in range(3):
            for par in range(2):
                done = [[], [], []]
                for spot in range(3):
                    at = pl.multiple_of(base * 96 + (xx * 6 + 2 * spot + par) * 16, 16)
                    values = [other_ref[pl.ds(at + zp * 576, 16), :].astype(F32) for zp in range(3)]
                    for s in range(SLOTS):
                        val = part_ref[s, pl.ds(at, 16), :] + combine(values, coef, s * 12 + 6)
                        done[s].append(val)
                        fo_ref[s, base + xx, par, spot * 16 : spot * 16 + 16, :] = val.astype(BF16)
                outs_a, outs_b, rest = pack_three(*done)
                block = xx * 2 + par
                for spot in range(3):
                    at = (block * 3 + spot) * 16
                    face[at : at + 16, :] = outs_a[spot]
                    face[288 + at : 304 + at, :] = outs_b[spot]
                face[576 + block * 16 : 592 + block * 16, :] = rest
    pp_s[0:2] = pown_ref[...]
    pp_s[2], pp_s[3] = parents_of(other_ref, up_ref)
    second = []
    for x in range(3):
        for pos in range(3):
            y = (0, 2, 1)[pos]
            at = (x * 3 + y) * 16
            values = [pp_s[v, at : at + 16, :].astype(F32) for v in range(4)]
            first = combine(values, coef, 72).astype(BF16)
            row = (x * 3 + pos) * 16
            po_ref[0, x, pos * 16 : pos * 16 + 16, :] = first
            fa_ref[672 + row : 688 + row, :] = first
            fb_ref[672 + row : 688 + row, :] = first
            val = combine(values, coef, 80)
            po_ref[1, x, pos * 16 : pos * 16 + 16, :] = val.astype(BF16)
            second.append(val)
    pack_pairs(fa_ref, 816, second)
    pack_pairs(fb_ref, 816, second)


def table_kernel(off_ref, zt_ref, far_ref, wl_ref, wp_ref, t3_s, w_s, a_s):
    core = lax.axis_index("gz")
    base = core * 80

    def spread(j, carry):
        for k in range(TERMS):
            at = pl.multiple_of(j * 104, 8) + 2 * k
            t3_s[pl.ds(at, 2), :] = far_ref[j, k].astype(F32)
        return carry

    lax.fori_loop(0, TERMS, spread, 0)
    t3_s[TERMS * 104 : 64 * 104, :] = jnp.zeros((15 * 104, 128), F32)
    for level, slots, start, out_ref in ((0, SLOTS, 0, wl_ref), (1, PSLOTS, 42, wp_ref)):
        ox = off_ref[level : level + 1, :]
        oy = off_ref[2 + level : 3 + level, :]
        oz = off_ref[4 + level : 5 + level, :]
        code = (ox + 3) * 7 + (oy + 3)
        chosen = lax.broadcasted_iota(jnp.int32, (56, 128), 0) == code
        for q in range(2 * slots):
            row = jnp.zeros((1, 128), F32)
            for d in range(7):
                row = jnp.where(oz == d - 3, zt_ref[base + start + q * 7 + d], row)
            full = jnp.where(chosen, row, 0.0)
            hi = full.astype(BF16).astype(F32)
            a_s[q * 56 : (q + 1) * 56, 0:128] = hi.astype(BF16)
            a_s[q * 56 : (q + 1) * 56, 128:256] = (full - hi).astype(BF16)
        count = slots * 56
        low = low_lanes(count)
        block = lax.broadcasted_iota(jnp.int32, (count, 128), 0)
        sign = -1.0
        if level == 0:
            sign = jnp.where(block < 56, zt_ref[base + 70], -1.0)

        def two_terms(i, carry):
            k = 2 * i
            rhs = []
            for e in range(2):
                tk = t3_s[pl.ds(2 * (k + e) + level, 64, stride=104), :].astype(BF16)
                wide = jnp.concatenate([tk, tk], axis=1)
                rhs += [wide, wide]
            out = lax.dot_general(
                a_s[0 : 2 * count, :], jnp.concatenate(rhs, axis=0), NT, preferred_element_type=F32
            )
            for e in range(2):
                even = out[0:count, e * 128 : (e + 1) * 128]
                odd = out[count : 2 * count, e * 128 : (e + 1) * 128]
                w_s[pl.ds(k + e, count, stride=136), :] = jnp.where(low, even, odd)
                w_s[pl.ds(k + e + 64, count, stride=136), :] = jnp.where(low, sign * odd, even)
            return carry

        lax.fori_loop(0, 25, two_terms, 0, unroll=5)
        inner = lax.broadcasted_iota(jnp.int32, (128, 128), 0)
        filled = (inner & 63) < TERMS

        def one_block(b, carry):
            val = w_s[pl.ds(pl.multiple_of(b * 136, 8), 128), :]
            out_ref[b] = jnp.where(filled, val, 0.0).astype(BF16)
            return carry

        lax.fori_loop(0, count, one_block, 0, unroll=4)


def weight_tiles(weights, s, diff, steps):
    d = 2 * diff + 3
    zero = jnp.zeros((128, 128), BF16)

    def weight(xi, dy):
        if dy < -3 or dy > 3:
            return zero
        return weights[s * 56 + xi * 7 + dy + 3]

    return jnp.concatenate(
        [
            jnp.concatenate([weight(xi, d + p), weight(xi, d + p - 1)], axis=1)
            for xi in steps
            for p in range(2)
        ],
        axis=0,
    )


def field_rows(field, s, steps, first, xs, rows):
    return jnp.concatenate(
        [field[s, first + xi : first + xi + xs, p].reshape(rows, 128) for xi in steps for p in range(2)],
        axis=1,
    )


def share_out(accs, s, xs, pairs, ys, put):
    spots = (ys + 1) // 2
    for pair in range(pairs):
        for o in range(2):
            yo = 2 * pair - 3 + o
            if yo >= ys + 3:
                continue
            val = None
            for diff in range(-3, 1):
                spot = pair + diff
                if 0 <= spot < spots:
                    part = accs[diff + 3][:, spot, :, o * 128 : (o + 1) * 128]
                    val = part if val is None else val + part
            for x in range(xs):
                put(s, x, yo, val[x])


SENT = ((0, 0, 2), (-1, 0, 1), (-2, 2, 3), (-3, 1, 3))
KEPT = ((0, 2, 3), (-1, 1, 3), (-2, 0, 2), (-3, 0, 1))


def spot_rows(field, s, steps, xs, span):
    rows = xs * 16 * (span[1] - span[0])
    cut = slice(span[0] * 16, span[1] * 16)
    return jnp.concatenate(
        [field[s, xi : xi + xs, p, cut].reshape(rows, 128) for xi in steps for p in range(2)], axis=1
    )


def near_kernel(fo_ref, wl_ref, acc_ref, fl_s):
    zero = jnp.zeros((SLOTS, 3, 2, 48, 128), BF16)
    fl_s[:, 0:3] = zero
    fl_s[:, 9:12] = zero
    fl_s[:, 3:9] = fo_ref[...]
    at = 0
    for s in range(SLOTS):
        for diff, lo, hi in SENT:
            lhs = spot_rows(fl_s, s, range(7), 6, (lo, hi))
            size = 96 * (hi - lo)
            acc_ref[at : at + size, :] = jnp.dot(
                lhs, weight_tiles(wl_ref, s, diff, range(7)), preferred_element_type=F32
            )
            at += size


def inner_kernel(fo_ref, fh_ref, edge_ref, wl_ref, own_ref, fl_s):
    fl_s[:, 0:3] = fh_ref[:, 0:3]
    fl_s[:, 9:12] = fh_ref[:, 3:6]
    fl_s[:, 3:9] = fo_ref[...]
    for s in range(SLOTS):
        accs = {}
        for diff, lo, hi in KEPT:
            lhs = spot_rows(fl_s, s, range(7), 6, (lo, hi))
            acc = jnp.dot(lhs, weight_tiles(wl_ref, s, diff, range(7)), preferred_element_type=F32)
            acc = acc.reshape(6, hi - lo, 16, 256)
            for spot in range(lo, hi):
                accs[diff, spot] = acc[:, spot - lo]
        for pair in (2, 3):
            val = accs[-pair, 0] + accs[1 - pair, 1] + accs[2 - pair, 2]
            for x in range(6):
                for o in range(2):
                    at = ((s * 6 + x) * 6 + 2 * pair - 3 + o) * 16
                    own_ref[at : at + 16, :] = val[x, :, o * 128 : (o + 1) * 128]
        for x in range(6):
            at = (s * 6 + x) * 96
            edge = (s * 6 + x) * 32
            own_ref[at : at + 16, :] = edge_ref[edge : edge + 16, :]
            own_ref[at + 80 : at + 96, :] = edge_ref[edge + 16 : edge + 32, :]


def far_kernel(
    a_ref, b_ref, acc_ref, po_ref, wl_ref, wp_ref, sa_ref, sb_ref, fh_ref, edge_ref, pown_ref, fl_s, fp_s, ex_s, px_s
):
    xodd = lax.rem(lax.axis_index("gx"), 2)
    yodd = lax.rem(lax.axis_index("gy"), 2)
    fl_s[:, 3:6] = jnp.zeros((SLOTS, 3, 2, 48, 128), BF16)
    fp_s[:, :, 1, 16:32] = jnp.zeros((PSLOTS, 9, 16, 128), BF16)
    part = po_ref[...]
    fp_s[:, 3:6, 0] = part[:, :, 0:32]
    fp_s[:, 3:6, 1, 0:16] = part[:, :, 32:48]
    for ref, far_side in ((a_ref, 1 - xodd), (b_ref, xodd)):
        for x in range(3):
            for par in range(2):
                block = x * 2 + par
                rest = ref[576 + block * 16 : 592 + block * 16, :].astype(F32)
                for spot in range(3):
                    at = (block * 3 + spot) * 16
                    one = ref[at : at + 16, :]
                    two = ref[288 + at : 304 + at, :]
                    three = unpack_third(one.astype(F32), two.astype(F32), rest, spot)
                    for s, val in enumerate((one, two, three.astype(BF16))):
                        fl_s[s, far_side * 6 + x, par, spot * 16 : spot * 16 + 16, :] = val
                        fh_ref[s, far_side * 3 + x, par, spot * 16 : spot * 16 + 16, :] = val
            for pos in range(3):
                b = x * 3 + pos
                pieces = (
                    ref[672 + b * 16 : 688 + b * 16, :],
                    unpack_pair(ref, 816, b).astype(BF16),
                )
                at = (pos % 2) * 16
                for s in range(PSLOTS):
                    fp_s[s, far_side * 6 + x, pos // 2, at : at + 16] = pieces[s]

    def parent_put(s, x, yo, val):
        if 0 <= yo < 3:
            at = ((s * 3 + x) * 3 + yo) * 16
            pown_ref[at : at + 16, :] = val
        else:
            px_s[0 if yo < 0 else 1, s, x * 3 + (yo + 3 if yo < 0 else yo - 3)] = val

    row = 0
    for s in range(SLOTS):
        accs = {}
        for diff, lo, hi in SENT:
            half = 48 * (hi - lo)
            for i, steps in enumerate((range(3), range(4, 7))):
                lhs = spot_rows(fl_s, s, steps, 3, (lo, hi))
                acc = acc_ref[row : row + half, :] + jnp.dot(
                    lhs, weight_tiles(wl_ref, s, diff, steps), preferred_element_type=F32
                )
                row += half
                acc = acc.reshape(3, hi - lo, 16, 256)
                for spot in range(lo, hi):
                    for x in range(3):
                        accs[diff, spot, 3 * i + x] = acc[x, spot - lo]
        for x in range(6):
            low = accs[0, 0, x]
            low_next = accs[-1, 0, x] + accs[0, 1, x]
            high_next = accs[-3, 1, x] + accs[-2, 2, x]
            high = accs[-3, 2, x]
            ex_s[0, s, x, 0] = low[:, 0:128]
            ex_s[0, s, x, 1] = low[:, 128:256]
            ex_s[0, s, x, 2] = low_next[:, 0:128]
            ex_s[1, s, x, 0] = high_next[:, 128:256]
            ex_s[1, s, x, 1] = high[:, 0:128]
            ex_s[1, s, x, 2] = high[:, 128:256]
            edge = (s * 6 + x) * 32
            edge_ref[edge : edge + 16, :] = low_next[:, 128:256]
            edge_ref[edge + 16 : edge + 32, :] = high_next[:, 0:128]
    for s in range(PSLOTS):
        lhs = field_rows(fp_s, s, range(7), 0, 3, 96)
        accs = [
            jnp.dot(lhs, weight_tiles(wp_ref, s, diff, range(7)), preferred_element_type=F32).reshape(3, 2, 16, 256)
            for diff in range(-3, 1)
        ]
        share_out(accs, s, 3, 5, 3, parent_put)
    for side, ref in ((1 - yodd, sa_ref), (yodd, sb_ref)):
        for x in range(6):
            outs_a, outs_b, rest = pack_three(
                *[[ex_s[side, s, x, i] for i in range(3)] for s in range(SLOTS)]
            )
            for i in range(3):
                at = (x * 3 + i) * 16
                ref[at : at + 16, :] = outs_a[i]
                ref[288 + at : 304 + at, :] = outs_b[i]
            ref[576 + x * 16 : 592 + x * 16, :] = rest
        for b in range(9):
            ref[672 + b * 16 : 688 + b * 16, :] = px_s[side, 0, b].astype(BF16)
        pack_pairs(ref, 816, [px_s[side, 1, b] for b in range(9)])


def join_kernel(own_ref, pown_ref, a_ref, b_ref, full_ref, zs_ref):
    yodd = lax.rem(lax.axis_index("gy"), 2)
    for ref, upper in ((a_ref, 1 - yodd), (b_ref, yodd)):
        for x in range(6):
            rest = ref[576 + x * 16 : 592 + x * 16, :].astype(F32)
            for i in range(3):
                at = (x * 3 + i) * 16
                one = ref[at : at + 16, :].astype(F32)
                two = ref[288 + at : 304 + at, :].astype(F32)
                three = unpack_third(one, two, rest, i)
                for s, val in enumerate((one, two, three)):
                    row = pl.multiple_of(((s * 6 + x) * 6 + i) * 16 + upper * 48, 16)
                    total = own_ref[pl.ds(row, 16), :] + val
                    full_ref[pl.ds(row, 16), :] = total
                    zs_ref[pl.ds(row, 16), :] = total.astype(BF16)
    for b in range(9):
        for s in range(PSLOTS):
            row = 1728 + (s * 9 + b) * 16
            total = pown_ref[row - 1728 : row - 1712, :]
            for ref in (a_ref, b_ref):
                if s == 0:
                    total = total + ref[672 + b * 16 : 688 + b * 16, :].astype(F32)
                else:
                    total = total + unpack_pair(ref, 816, b)
            full_ref[row : row + 16, :] = total
            zs_ref[row : row + 16, :] = total.astype(BF16)


def back_kernel(own_ref, coef_ref, part_ref, ppart_ref):
    core = lax.axis_index("gz")

    def coef(row):
        return coef_ref[core, row : row + 1, :]

    for i in range(9):
        at = 1728 + i * 16
        values = [own_ref[at + s * 144 : at + s * 144 + 16, :] for s in range(PSLOTS)]
        for p in range(2):
            ppart_ref[p, i * 16 : (i + 1) * 16, :] = combine(values, coef, 88 + p * 8)
    for b in range(36):
        values = [own_ref[s * 576 + b * 16 : s * 576 + b * 16 + 16, :] for s in range(SLOTS)]
        for zp in range(3):
            part_ref[zp, b * 16 : b * 16 + 16, :] = combine(values, coef, 36 + zp * 12)


def atoms_kernel(part_ref, ppart_ref, other_ref, coef_ref, one_ref, h_ref, down_ref, out_ref, pf_s, lift_s, l_s, l2_s, l3_s):
    core = lax.axis_index("gz")

    def coef(row):
        return coef_ref[core, row : row + 1, :]

    for i in range(9):
        at = 1728 + i * 16
        values = [other_ref[at + s * 144 : at + s * 144 + 16, :].astype(F32) for s in range(PSLOTS)]
        for p in range(2):
            total = ppart_ref[p, i * 16 : (i + 1) * 16, :] + combine(values, coef, 92 + p * 8)
            pf_s[p, i * 16 : (i + 1) * 16, :] = total.astype(BF16)
    for k in range(3):
        lift_s[k] = lax.dot_general(pf_s[k // 2], down_ref[k % 2], NT, preferred_element_type=F32)
    for x in range(6):
        for y in range(6):
            at = (x * 6 + y) * 16
            values = [other_ref[s * 576 + at : s * 576 + at + 16, :].astype(F32) for s in range(SLOTS)]
            par = ((x // 2) * 3 + y // 2) * 16
            lane = ((x % 2) * 2 + y % 2) * 128
            for zp in range(3):
                l_s[zp, at : at + 16, :] = (
                    part_ref[zp, at : at + 16, :]
                    + combine(values, coef, 42 + zp * 12)
                    + lift_s[zp, par : par + 16, lane : lane + 128]
                )
    low = low_lanes(40)
    for zp in range(3):
        l_s[zp, 576:640, :] = jnp.zeros((64, 128), F32)
        for cp in range(8):
            a = l_s[zp, pl.ds(2 * cp, 40, stride=16), :]
            b = l_s[zp, pl.ds(2 * cp + 1, 40, stride=16), :]
            first = jnp.where(low, a, pltpu.roll(b, 64, 1))
            second = jnp.where(low, pltpu.roll(a, 64, 1), b)
            for z, val in ((2 * zp, first), (2 * zp + 1, second)):
                hi = val.astype(BF16).astype(F32)
                l2_s[z * 40 : (z + 1) * 40, cp * 128 : (cp + 1) * 128] = hi
                l3_s[z * 40 : (z + 1) * 40, cp * 128 : (cp + 1) * 128] = val - hi
    high_rows, low_rows = [
        ref[...].T.reshape(CH, 64, 240)[:, 0:56].reshape(CH * 56, 240).astype(BF16) for ref in (l2_s, l3_s)
    ]
    for i in range(8):
        one = one_ref[:, i * 256 : (i + 1) * 256]
        spread = jnp.dot(high_rows, one, preferred_element_type=F32)
        spread = spread + jnp.dot(low_rows, one, preferred_element_type=F32)
        spread = spread.reshape(CH, 56, 256) * h_ref[0:56, i * 256 : (i + 1) * 256][None]
        out_ref[0, 0, 0, :, i * 256 : (i + 1) * 256] = jnp.sum(spread, axis=1)


def call(kernel, outs, scratch, limit, flops, moved, in_specs=None):
    placed = {} if in_specs is None else {"in_specs": in_specs}
    return pl.pallas_call(
        kernel,
        out_shape=outs,
        **placed,
        scratch_shapes=scratch,
        compiler_params=pltpu.CompilerParams(vmem_limit_bytes=limit * MIB),
        cost_estimate=pl.CostEstimate(flops=flops, bytes_accessed=moved, transcendentals=0),
    )


def shape(dims, dtype):
    return jax.ShapeDtypeStruct(dims, dtype)


def swaps(axis):
    count = lax.axis_size(axis)
    inner = [(i, i ^ 1) for i in range(count)]
    outer = [(i, (i + (1 if i % 2 else -1)) % count) for i in range(count)]
    return inner, outer


def far_weights(off, table, far):
    vmem = pl.BlockSpec(memory_space=pltpu.VMEM)
    return call(
        table_kernel,
        (shape((SLOTS * 56, 128, 128), BF16), shape((PSLOTS * 56, 128, 128), BF16)),
        [
            pltpu.VMEM((64 * 104, 128), F32),
            pltpu.VMEM((SLOTS * 56 * 136, 128), F32),
            pltpu.VMEM((SLOTS * 112, 256), BF16),
        ],
        24,
        2 * 49 * 5 * 112 * 256 * 256,
        10 * MIB,
        [vmem, pl.BlockSpec(memory_space=pltpu.SMEM), vmem],
    )(off, table, far)


def per_device(charges, positions, atom_cells, offsets, far_tables, upward_tables, downward_tables):
    up = jnp.pad(upward_tables.transpose(1, 0, 2), ((0, 15), (0, 0), (0, 15))).reshape(64, 512)
    up = jnp.concatenate([up, up], axis=0)
    down = jnp.pad(downward_tables, ((0, 0), (0, 15), (0, 15))).reshape(512, 64)
    blank = jnp.zeros_like(down)
    down = jnp.stack(
        [jnp.concatenate([down, blank], axis=1), jnp.concatenate([blank, down], axis=1)], axis=0
    )
    off = offsets.transpose(2, 0, 1).reshape(6, NOFF)
    far = far_tables.transpose(1, 2, 0, 3)
    coefs = jnp.asarray(COEFS)
    ztable = jnp.asarray(ZTABLE)
    cells = atom_cells.reshape(16, 128)
    swap = [(0, 1), (1, 0)]

    positions = pltpu.with_memory_space_constraint(positions.reshape(48, 128), pltpu.HBM)
    cells = pltpu.with_memory_space_constraint(cells, pltpu.HBM)
    leaf_z = call(
        poles_kernel,
        shape((1728, 128), BF16),
        [
            pltpu.VMEM((64, 2048), F32),
            pltpu.VMEM((240, 2048), BF16),
            pltpu.VMEM((16, 2048), BF16),
            pltpu.VMEM((48, 128), F32),
            pltpu.VMEM((16, 128), jnp.int32),
            pltpu.VMEM((1024, 128), F32),
            pltpu.VMEM((16, 2048), F32),
            pltpu.VMEM((1024, 2048), BF16),
            pltpu.VMEM((1024, 2048), BF16),
            pltpu.VMEM((1024, 240), F32),
            pltpu.VMEM((3, 640, 128), F32),
            pltpu.SemaphoreType.DMA((3,)),
        ],
        20,
        2 * 2 * 256 * 2048 * 1024,
        2 * MIB,
        [pl.BlockSpec(memory_space=pltpu.HBM)] * 3,
    )(pltpu.with_memory_space_constraint(charges, pltpu.HBM), positions, cells)
    leaf_other = lax.ppermute(leaf_z, "gz", swap)
    part, pown = call(
        half_kernel,
        (shape((SLOTS, 576, 128), F32), shape((2, 144, 128), BF16)),
        [],
        8,
        1 << 27,
        2 * MIB,
    )(leaf_z, coefs, up)
    face = shape((896, 128), BF16)
    fa, fb, fo, po = call(
        forward_kernel,
        (face, face, shape((SLOTS, 6, 2, 48, 128), BF16), shape((PSLOTS, 3, 48, 128), BF16)),
        [pltpu.VMEM((4, 144, 128), BF16)],
        8,
        1 << 28,
        2 * MIB,
    )(part, pown, leaf_other, coefs, up)
    inner, outer = swaps("gx")
    fa = lax.ppermute(fa, "gx", inner)
    fb = lax.ppermute(fb, "gx", outer)
    fo, off = lax.optimization_barrier((fo, off))
    wl, wp = far_weights(off, ztable, far)
    near = call(
        near_kernel,
        shape((SLOTS * 576, 256), F32),
        [pltpu.VMEM((SLOTS, 12, 2, 48, 128), BF16)],
        16,
        2 * 144 * 1792 * 256 * 12,
        8 * MIB,
    )(fo, wl)
    sa, sb, fh, edge, pown = call(
        far_kernel,
        (
            face,
            face,
            shape((SLOTS, 6, 2, 48, 128), BF16),
            shape((SLOTS * 192, 128), F32),
            shape((288, 128), F32),
        ),
        [
            pltpu.VMEM((SLOTS, 9, 2, 48, 128), BF16),
            pltpu.VMEM((PSLOTS, 9, 2, 32, 128), BF16),
            pltpu.VMEM((2, SLOTS, 6, 3, 16, 128), F32),
            pltpu.VMEM((2, PSLOTS, 9, 16, 128), F32),
        ],
        16,
        2 * 288 * 1792 * 256 * 8,
        14 * MIB,
    )(fa, fb, near, po, wl, wp)
    inner, outer = swaps("gy")
    sa = lax.ppermute(sa, "gy", inner)
    sb = lax.ppermute(sb, "gy", outer)
    edge, positions, cells = lax.optimization_barrier((edge, positions, cells))
    own = call(
        inner_kernel,
        shape((1728, 128), F32),
        [pltpu.VMEM((SLOTS, 12, 2, 48, 128), BF16)],
        16,
        2 * 144 * 1792 * 256 * 12,
        8 * MIB,
    )(fo, fh, edge, wl)
    harm, one = call(
        atom_terms_kernel,
        (shape((64, 2048), F32), shape((240, 2048), BF16)),
        [pltpu.VMEM((1024, 128), F32)],
        8,
        1 << 24,
        2 * MIB,
    )(positions, cells)
    own, harm, one = lax.optimization_barrier((own, harm, one))
    full, zsend = call(
        join_kernel, (shape((2016, 128), F32), shape((2016, 128), BF16)), [], 8, 1 << 20, 3 * MIB
    )(own, pown, sa, sb)
    zrecv = lax.ppermute(zsend, "gz", swap)
    part, ppart = call(
        back_kernel,
        (shape((SLOTS, 576, 128), F32), shape((2, 144, 128), F32)),
        [],
        8,
        1 << 24,
        2 * MIB,
    )(full, coefs)
    potential = call(
        atoms_kernel,
        shape((1, 1, 1, CH, 2048), F32),
        [
            pltpu.VMEM((2, 144, 128), BF16),
            pltpu.VMEM((3, 144, 512), F32),
            pltpu.VMEM((3, 640, 128), F32),
            pltpu.VMEM((240, 1024), F32),
            pltpu.VMEM((240, 1024), F32),
        ],
        16,
        2 * 2 * 256 * 2048 * 1024,
        2 * MIB,
    )(part, ppart, zrecv, coefs, one, harm, down)
    return potential


def solution(mesh):
    placed = (
        P("gx", "gy", "gz", None, None),
        P("gx", "gy", "gz", None, None),
        P("gx", "gy", "gz", None),
        P(),
        P(),
        P(),
        P(),
    )
    return jax.shard_map(
        per_device,
        mesh=mesh,
        in_specs=placed,
        out_specs=P("gx", "gy", "gz", None, None),
        check_vma=False,
    )
```

time: 66.7 us -> 47.5 us (0.71)
  Pallas kernels: 36.5 us -> 27 us
  waiting for transfers between devices: 9.04 us -> 3.04 us
  local copies, waits for them, and re-layouts: 5.56 us -> 0.38 us
  starting transfers between devices: 15.2 us -> 16.8 us
    pallas_call x4 -> x9, Pallas kernels: 31.7 us -> 22.8 us  [the longest x1 7.72 us: far_weights(): call(table_kernel, (shape((SLOTS * 56, 128, 128), BF16), shape((PSLOTS *...]
    ppermute x5, waiting for transfers between devices: 7.72 us -> 2.19 us  [the longest x1 1 us: per_device(): sb = lax.ppermute(sb, 'gy', outer)]
    unnamed x22 -> x14, local copies, waits for them, and re-layouts: 4.37 us -> 0.05 us
    ppermute x5, starting transfers between devices: 13.6 us -> 14.6 us  [the longest x1 7.11 us: per_device(): sb = lax.ppermute(sb, 'gy', outer)]
    transpose x1 -> x0, local copies, waits for them, and re-layouts: 0.92 us -> none  [per_device(): jnp.pad(upward_tables, ((0, 0), (0, 15), (0, 15))).transpose(1, 0, 2)]
    pallas_call x1, Pallas kernels: 4.62 us -> 3.94 us  [per_device(): call(atoms_kernel, shape((1, 1, 1, CH, 2048), F32), [pltpu.VMEM((2, 144,...]
  transfers between devices with their start and end apart: 6 -> 6, of which waited for: 3 -> 4; matrix products, arithmetic and copies ran while one was open for 1% -> 1% of each run, Pallas kernels for 29% -> 30%
where the time goes in v2:
time: 47.5 us; the launch traced here: 47.4 us
  Pallas kernels  27 us (57%)
  starting transfers between devices  16.8 us (35%)
  waiting for transfers between devices  3.04 us (6%)
    pallas_call x1, Pallas kernels, far_weights(): call(table_kernel, (shape((SLOTS * 56, 128, 128), BF16), shape((PSLOTS *...  7.72 us
    ppermute x1, starting transfers between devices, per_device(): sb = lax.ppermute(sb, 'gy', outer)  7.11 us
    pallas_call x1, Pallas kernels, per_device(): call(poles_kernel, shape((1728, 128), BF16), [pltpu.VMEM((64, 2048), F32)...  4.46 us
    pallas_call x1, Pallas kernels, per_device(): call(atoms_kernel, shape((1, 1, 1, CH, 2048), F32), [pltpu.VMEM((2, 144,...  3.94 us
    ppermute x1, starting transfers between devices, per_device(): leaf_other = lax.ppermute(leaf_z, 'gz', swap)  3.31 us
    pallas_call x1, Pallas kernels, per_device(): call(far_kernel, (face, face, shape((SLOTS, 6, 2, 48, 128), BF16), shape(...  3.11 us
    ppermute x1, starting transfers between devices, per_device(): zrecv = lax.ppermute(zsend, 'gz', swap)  2.22 us
    ppermute x1, starting transfers between devices, per_device(): fb = lax.ppermute(fb, 'gx', outer)  2.19 us
  transfers between devices with their start and end apart: 6, of which 4 were waited for; matrix products, arithmetic and copies ran while one was open for 1% of the time, Pallas kernels for 30%

profile of v2, /device:TPU:1, one launch (start us, length us, event | category | flops | bytes accessed | tf_op | source)
XLA Modules:
  0.0 47.4 jit_solution(17731747850661075064)
XLA Ops:
  0.0 0.0 copy-start.3
  0.0 0.0 copy-start.5
  0.0 0.0 copy-start
  0.0 0.0 copy-start.1
  0.0 0.0 copy-start.2
  0.0 4.5 %shard_map.91.own_ref = bf16[1728,128]{1,0:T(8,128)(2,1)S(1)} custom-call(bf16[1,1,1,16,2048]{4,3,2,1,0:T(8,128)(2,1)} %ch_hbm.1, f32[48,128]{1,0:T(8,128)} %bitcast.14, s32[16,128]{1,0:T(8,128)} %bitcast.16), custom_call_target="tpu_custom_call" | custom-call | flops 2147483648 | bytes 2097152 | tf_op jit(solution)/shard_map/pallas_call | solution.py:737
  4.5 3.3 %collective-permute-start = (bf16[1728,128]{1,0:T(8,128)(2,1)S(1)}, bf16[1728,128]{1,0:T(8,128)(2,1)S(1)}, u32[]{:S(2)}, u32[]{:S(2)}) collective-permute-start(bf16[1728,128]{1,0:T(8,128)(2,1)S(1)} %shard_map.91.own_ref), channel_id=1, source_target_pairs={{0,1},{1,0},{2,3},{3,2},{4,5},{5,4},{6,7},{7,6},{8,9},{9,8},{10,11... | collective-permute-start | bytes 1327112 | tf_op jit(solution)/shard_map/ppermute | solution.py:759
  7.8 0.0 copy-done.3
  7.8 0.1 reshape.17
  8.0 0.0 copy-done.5
  8.0 0.0 copy-done
  8.0 0.5 %shard_map.92 = (f32[3,576,128]{2,1,0:T(8,128)S(1)}, bf16[2,144,128]{2,1,0:T(8,128)(2,1)S(1)}) custom-call(bf16[1728,128]{1,0:T(8,128)(2,1)S(1)} %shard_map.91.own_ref, f32[2,104,128]{2,1,0:T(8,128)S(1)} %copy-done, bf16[128,512]{1,0:T(8,128)(2,1)S(1)} %constant_dynamic-update-slice_fusion.up_ref), custom_call_target="tpu_custom_call" | custom-call | flops 134217728 | bytes 2097152 | tf_op jit(solution)/shard_map/pallas_call | solution.py:760
  8.6 0.7 %collective-permute-done.other_ref = bf16[1728,128]{1,0:T(8,128)(2,1)S(1)} collective-permute-done((bf16[1728,128]{1,0:T(8,128)(2,1)S(1)}, bf16[1728,128]{1,0:T(8,128)(2,1)S(1)}, u32[]{:S(2)}, u32[]{:S(2)}) %collective-permute-start) | collective-permute-done | bytes 442400 | tf_op jit(solution)/shard_map/ppermute | solution.py:759
  9.2 1.1 %shard_map.93 = (bf16[896,128]{1,0:T(8,128)(2,1)S(1)}, bf16[896,128]{1,0:T(8,128)(2,1)S(1)}, bf16[3,6,2,48,128]{4,3,2,1,0:T(8,128)(2,1)S(1)}, bf16[2,3,48,128]{3,2,1,0:T(8,128)(2,1)S(1)}) custom-call(f32[3,576,128]{2,1,0:T(8,128)S(1)} %get-tuple-element.32.part_ref, bf16[2,144,128]{2,1,0:T(8,128)(2,1)S(1)} %get-tuple-element.33.pown_ref, ...), custom_call_target="tpu_custom_call" | custom-call | flops 268435456 | bytes 2097152 | tf_op jit(solution)/shard_map/pallas_call | solution.py:769
  10.4 0.1 collective-permute-start.1
  10.4 2.2 %collective-permute-start.2 = (bf16[896,128]{1,0:T(8,128)(2,1)S(1)}, bf16[896,128]{1,0:T(8,128)(2,1)S(1)}, u32[]{:S(2)}, u32[]{:S(2)}) collective-permute-start(bf16[896,128]{1,0:T(8,128)(2,1)S(1)} %get-tuple-element.37), channel_id=1, source_target_pairs={{0,224},{32,64},{64,32},{96,128},{128,96},{160,192},{192,160},{224... | collective-permute-start | bytes 688136 | tf_op jit(solution)/shard_map/ppermute | solution.py:779
  12.6 0.0 copy-done.1
  12.6 0.0 copy-done.2
  12.6 7.7 %shard_map.94 = (bf16[168,128,128]{2,1,0:T(8,128)(2,1)S(1)}, bf16[112,128,128]{2,1,0:T(8,128)(2,1)S(1)}) custom-call(s32[6,128]{1,0:T(8,128)S(1)} %reshape.18.off_ref, f32[160]{0:T(256)S(1)} %copy-done.2, bf16[49,49,2,128]{3,2,1,0:T(2,128)(2,1)S(1)} %bitcast.10), custom_call_target="tpu_custom_call" | custom-call | flops 3596615680 | bytes 10485760 | tf_op jit(solution)/shard_map/pallas_call | solution.py:705
  20.4 2.0 %shard_map.95.acc_ref = f32[1728,256]{1,0:T(8,128)S(1)} custom-call(bf16[3,6,2,48,128]{4,3,2,1,0:T(8,128)(2,1)S(1)} %get-tuple-element.35.fo_ref, bf16[168,128,128]{2,1,0:T(8,128)(2,1)S(1)} %get-tuple-element.39.wl_ref), custom_call_target="tpu_custom_call" | custom-call | flops 1585446912 | bytes 8388608 | tf_op jit(solution)/shard_map/pallas_call | solution.py:782
  22.4 0.0 collective-permute-done.1.a_ref
  22.4 0.5 %collective-permute-done.2.b_ref = bf16[896,128]{1,0:T(8,128)(2,1)S(1)} collective-permute-done((bf16[896,128]{1,0:T(8,128)(2,1)S(1)}, bf16[896,128]{1,0:T(8,128)(2,1)S(1)}, u32[]{:S(2)}, u32[]{:S(2)}) %collective-permute-start.2) | collective-permute-done | bytes 229408 | tf_op jit(solution)/shard_map/ppermute | solution.py:779
  22.9 3.1 %shard_map.96 = (bf16[896,128]{1,0:T(8,128)(2,1)S(1)}, bf16[896,128]{1,0:T(8,128)(2,1)S(1)}, bf16[3,6,2,48,128]{4,3,2,1,0:T(8,128)(2,1)S(1)}, f32[576,128]{1,0:T(8,128)S(1)}, f32[288,128]{1,0:T(8,128)S(1)}) custom-call(bf16[896,128]{1,0:T(8,128)(2,1)S(1)} %collective-permute-done.1.a_ref, bf16[896,128]{1,0:T(8,128)(2,1)S(1)} %collective-permute-done.2.b_ref, ...), custom_call_target="tpu_custom_call" | custom-call | flops 2113929216 | bytes 14680064 | tf_op jit(solution)/shard_map/pallas_call | solution.py:790
  26.0 1.9 %collective-permute-start.3 = (bf16[896,128]{1,0:T(8,128)(2,1)S(1)}, bf16[896,128]{1,0:T(8,128)(2,1)S(1)}, u32[]{:S(2)}, u32[]{:S(2)}) collective-permute-start(bf16[896,128]{1,0:T(8,128)(2,1)S(1)} %get-tuple-element.51), channel_id=1, source_target_pairs={{0,2},{2,0},{4,6},{6,4},{8,10},{10,8},{12,14},{14,12},{16,18},{18,... | collective-permute-start | bytes 688136 | tf_op jit(solution)/shard_map/ppermute | solution.py:810
  27.9 7.1 %collective-permute-start.4 = (bf16[896,128]{1,0:T(8,128)(2,1)S(1)}, bf16[896,128]{1,0:T(8,128)(2,1)S(1)}, u32[]{:S(2)}, u32[]{:S(2)}) collective-permute-start(bf16[896,128]{1,0:T(8,128)(2,1)S(1)} %get-tuple-element.52), channel_id=1, source_target_pairs={{0,30},{2,4},{4,2},{6,8},{8,6},{10,12},{12,10},{14,16},{16,14},{18... | collective-permute-start | bytes 688136 | tf_op jit(solution)/shard_map/ppermute | solution.py:811
  35.1 1.3 %shard_map.98 = (f32[64,2048]{1,0:T(8,128)S(1)}, bf16[240,2048]{1,0:T(8,128)(2,1)S(1)}) custom-call(f32[48,128]{1,0:T(8,128)} %bitcast.15, s32[16,128]{1,0:T(8,128)} %bitcast.17), custom_call_target="tpu_custom_call" | custom-call | flops 16777216 | bytes 2097152 | tf_op jit(solution)/shard_map/pallas_call | solution.py:821
  36.3 0.0 copy-start.4
  36.4 2.1 %shard_map.97.own_ref = f32[1728,128]{1,0:T(8,128)S(1)} custom-call(bf16[3,6,2,48,128]{4,3,2,1,0:T(8,128)(2,1)S(1)} %get-tuple-element.35.fo_ref, bf16[3,6,2,48,128]{4,3,2,1,0:T(8,128)(2,1)S(1)} %get-tuple-element.42.fh_ref, f32[576,128]{1,0:T(8,128)S(1)} %get-tuple-element.44.edge_ref, bf16[168,128,128]{2,1,0:T(8,128)(2,1)S(1)} %get-tuple-element.39.wl_ref), custom_call_target="tpu_custom_call" | custom-call | flops 1585446912 | bytes 8388608 | tf_op jit(solution)/shard_map/pallas_call | solution.py:813
  38.5 0.0 collective-permute-done.3.a_ref
  38.5 1.0 %collective-permute-done.4.b_ref = bf16[896,128]{1,0:T(8,128)(2,1)S(1)} collective-permute-done((bf16[896,128]{1,0:T(8,128)(2,1)S(1)}, bf16[896,128]{1,0:T(8,128)(2,1)S(1)}, u32[]{:S(2)}, u32[]{:S(2)}) %collective-permute-start.4) | collective-permute-done | bytes 229408 | tf_op jit(solution)/shard_map/ppermute | solution.py:811
  39.5 0.2 shard_map.99
  39.7 2.2 %collective-permute-start.5 = (bf16[2016,128]{1,0:T(8,128)(2,1)S(1)}, bf16[2016,128]{1,0:T(8,128)(2,1)S(1)}, u32[]{:S(2)}, u32[]{:S(2)}) collective-permute-start(bf16[2016,128]{1,0:T(8,128)(2,1)S(1)} %get-tuple-element.56), channel_id=1, source_target_pairs={{0,1},{1,0},{2,3},{3,2},{4,5},{5,4},{6,7},{7,6},{8,9},{9,8},{10,11... | collective-permute-start | bytes 1548296 | tf_op jit(solution)/shard_map/ppermute | solution.py:833
  41.9 0.0 copy-done.4
  42.0 0.1 pad_bitcast_fusion.1
  42.1 0.5 shard_map.100
  42.6 0.8 %collective-permute-done.5.other_ref = bf16[2016,128]{1,0:T(8,128)(2,1)S(1)} collective-permute-done((bf16[2016,128]{1,0:T(8,128)(2,1)S(1)}, bf16[2016,128]{1,0:T(8,128)(2,1)S(1)}, u32[]{:S(2)}, u32[]{:S(2)}) %collective-permute-start.5) | collective-permute-done | bytes 516128 | tf_op jit(solution)/shard_map/ppermute | solution.py:833
  43.5 3.9 %shard_map.101 = f32[1,1,1,16,2048]{4,3,2,1,0:T(8,128)} custom-call(f32[3,576,128]{2,1,0:T(8,128)S(1)} %get-tuple-element.54.part_ref, f32[2,144,128]{2,1,0:T(8,128)S(1)} %get-tuple-element.55.ppart_ref, bf16[2016,128]{1,0:T(8,128)(2,1)S(1)} %collective-permute-done.5.other_ref, f32[2,104,128]{2,1,0:T(8,128)S(1)} %copy-done, ...), custom_call_target="tpu_custom_call" | custom-call | flops 2147483648 | bytes 2097152 | tf_op jit(solution)/shard_map/pallas_call | solution.py:842
  (7 shorter events, 0.1 us)
Async XLA Ops:
  0.0 7.8 %copy-start.3 = (bf16[8,49,49]{2,0,1:T(8,128)(2,1)S(1)}, bf16[8,49,49]{2,0,1:T(8,128)(2,1)}, u32[]{:S(2)}) copy-start(bf16[8,49,49]{2,0,1:T(8,128)(2,1)} %param.14) | copy-start | bytes 115252
  0.0 8.0 %copy-start.5 = (s32[2,128,3]{1,0,2:T(2,128)S(1)}, s32[2,128,3]{1,0,2:T(2,128)}, u32[]{:S(2)}) copy-start(s32[2,128,3]{1,0,2:T(2,128)} %param.12) | copy-start | bytes 9220
  0.0 8.0 %copy-start = (f32[2,104,128]{2,1,0:T(8,128)S(1)}, f32[2,104,128]{2,1,0:T(8,128)}, u32[]{:S(2)}) copy-start(f32[2,104,128]{2,1,0:T(8,128)} %constant.8.clone.coef_ref) | copy-start | bytes 319492
  0.0 12.6 %copy-start.1 = (bf16[2,49,49,128]{3,0,2,1:T(2,128)(2,1)S(1)}, bf16[2,49,49,128]{3,0,2,1:T(2,128)(2,1)}, u32[]{:S(2)}) copy-start(bf16[2,49,49,128]{3,0,2,1:T(2,128)(2,1)} %param.13) | copy-start | bytes 3687940
  0.0 12.6 %copy-start.2 = (f32[160]{0:T(256)S(1)}, f32[160]{0:T(256)}, u32[]{:S(2)}) copy-start(f32[160]{0:T(256)} %constant.9.clone.zt_ref) | copy-start | bytes 1924
  4.5 4.7 %collective-permute-start = (bf16[1728,128]{1,0:T(8,128)(2,1)S(1)}, bf16[1728,128]{1,0:T(8,128)(2,1)S(1)}, u32[]{:S(2)}, u32[]{:S(2)}) collective-permute-start(bf16[1728,128]{1,0:T(8,128)(2,1)S(1)} %shard_map.91.own_ref), channel_id=1, source_target_pairs={{0,1},{1,0},{2,3},{3,2},{4,5},{5,4},{6,7},{7,6},{8,9},{9,8},{10,11... | collective-permute-start | bytes 1327112 | tf_op jit(solution)/shard_map/ppermute | solution.py:759
  10.4 12.0 %collective-permute-start.1 = (bf16[896,128]{1,0:T(8,128)(2,1)S(1)}, bf16[896,128]{1,0:T(8,128)(2,1)S(1)}, u32[]{:S(2)}, u32[]{:S(2)}) collective-permute-start(bf16[896,128]{1,0:T(8,128)(2,1)S(1)} %get-tuple-element.36), channel_id=1, source_target_pairs={{0,32},{32,0},{64,96},{96,64},{128,160},{160,128},{192,224},{224,1... | collective-permute-start | bytes 688136 | tf_op jit(solution)/shard_map/ppermute | solution.py:778
  10.4 12.5 %collective-permute-start.2 = (bf16[896,128]{1,0:T(8,128)(2,1)S(1)}, bf16[896,128]{1,0:T(8,128)(2,1)S(1)}, u32[]{:S(2)}, u32[]{:S(2)}) collective-permute-start(bf16[896,128]{1,0:T(8,128)(2,1)S(1)} %get-tuple-element.37), channel_id=1, source_target_pairs={{0,224},{32,64},{64,32},{96,128},{128,96},{160,192},{192,160},{224... | collective-permute-start | bytes 688136 | tf_op jit(solution)/shard_map/ppermute | solution.py:779
  26.0 12.4 %collective-permute-start.3 = (bf16[896,128]{1,0:T(8,128)(2,1)S(1)}, bf16[896,128]{1,0:T(8,128)(2,1)S(1)}, u32[]{:S(2)}, u32[]{:S(2)}) collective-permute-start(bf16[896,128]{1,0:T(8,128)(2,1)S(1)} %get-tuple-element.51), channel_id=1, source_target_pairs={{0,2},{2,0},{4,6},{6,4},{8,10},{10,8},{12,14},{14,12},{16,18},{18,... | collective-permute-start | bytes 688136 | tf_op jit(solution)/shard_map/ppermute | solution.py:810
  27.9 11.5 %collective-permute-start.4 = (bf16[896,128]{1,0:T(8,128)(2,1)S(1)}, bf16[896,128]{1,0:T(8,128)(2,1)S(1)}, u32[]{:S(2)}, u32[]{:S(2)}) collective-permute-start(bf16[896,128]{1,0:T(8,128)(2,1)S(1)} %get-tuple-element.52), channel_id=1, source_target_pairs={{0,30},{2,4},{4,2},{6,8},{8,6},{10,12},{12,10},{14,16},{16,14},{18... | collective-permute-start | bytes 688136 | tf_op jit(solution)/shard_map/ppermute | solution.py:811
  36.3 5.6 %copy-start.4 = (bf16[8,49,49]{2,0,1:T(8,128)(2,1)S(1)}, bf16[8,49,49]{2,0,1:T(8,128)(2,1)}, u32[]{:S(2)}) copy-start(bf16[8,49,49]{2,0,1:T(8,128)(2,1)} %param.15) | copy-start | bytes 115252
  39.7 3.7 %collective-permute-start.5 = (bf16[2016,128]{1,0:T(8,128)(2,1)S(1)}, bf16[2016,128]{1,0:T(8,128)(2,1)S(1)}, u32[]{:S(2)}, u32[]{:S(2)}) collective-permute-start(bf16[2016,128]{1,0:T(8,128)(2,1)S(1)} %get-tuple-element.56), channel_id=1, source_target_pairs={{0,1},{1,0},{2,3},{3,2},{4,5},{5,4},{6,7},{7,6},{8,9},{9,8},{10,11... | collective-permute-start | bytes 1548296 | tf_op jit(solution)/shard_map/ppermute | solution.py:833

commit v3 on v2

--- a/solution.py
+++ b/solution.py
@@ -189,7 +189,7 @@
     fill_onehot(cell_ref, one_ref)
 
 
-def poles_kernel(ch_hbm, pos_hbm, cell_hbm, zs_ref, h_s, one_s, ch_s, pos_s, cell_s, h3_s, chf_s, whi_s, wlo_s, rt_s, f_s, sems):
+def poles_kernel(ch_hbm, pos_hbm, cell_hbm, zs_ref, h_s, one_s, ch_s, pos_s, cell_s, h3_s, chf_s, whi_s, wlo_s, f_s, sems):
     copies = start_copies(((pos_hbm, pos_s), (cell_hbm, cell_s), (ch_hbm.at[0, 0, 0], ch_s)), sems)
     copies[0].wait()
     fill_harmonics(pos_s, h3_s, h_s)
@@ -197,19 +197,18 @@
     fill_onehot(cell_s, one_s)
     copies[2].wait()
     chf_s[...] = ch_s[...].astype(F32)
-    for c in range(CH):
-        for i in range(4):
-            sl = slice(i * 512, (i + 1) * 512)
-            w = h_s[:, sl] * chf_s[c : c + 1, sl]
-            hi = w.astype(BF16)
-            whi_s[c * 64 : (c + 1) * 64, sl] = hi
-            wlo_s[c * 64 : (c + 1) * 64, sl] = (w - hi.astype(F32)).astype(BF16)
     low = low_lanes(40)
-    rt_s[...] = lax.dot_general(whi_s[...], one_s[...], NT, preferred_element_type=F32) + lax.dot_general(
-        wlo_s[...], one_s[...], NT, preferred_element_type=F32
-    )
     for n in range(4):
-        r = rt_s[n * 256 : (n + 1) * 256, :].T
+        for c in range(4 * n, 4 * n + 4):
+            for i in range(4):
+                sl = slice(i * 512, (i + 1) * 512)
+                w = h_s[:, sl] * chf_s[c : c + 1, sl]
+                hi = w.astype(BF16)
+                whi_s[c * 64 : (c + 1) * 64, sl] = hi
+                wlo_s[c * 64 : (c + 1) * 64, sl] = (w - hi.astype(F32)).astype(BF16)
+        rows = slice(n * 256, (n + 1) * 256)
+        r = lax.dot_general(one_s[...], whi_s[rows, :], NT, preferred_element_type=F32)
+        r = r + lax.dot_general(one_s[...], wlo_s[rows, :], NT, preferred_element_type=F32)
         for half in range(2):
             c = n * 4 + half * 2
             for zp in range(3):
@@ -252,16 +251,42 @@
     )
 
 
-def pack_pairs(ref, base, blocks):
+def rest_shift(b):
+    piece = b % 6
+    return (64 * (piece // 3) + 19 * (piece % 3) - 30) % 128
+
+
+def pack_parents(refs, firsts, seconds):
+    lane = lax.broadcasted_iota(jnp.int32, (16, 128), 1)
+    inner = lane & 63
+    for b in range(9):
+        spare = jnp.where(lane < 64, pltpu.roll(seconds[b], 49, 1), pltpu.roll(seconds[b], 98, 1))
+        val = jnp.where(inner < TERMS, firsts[b], spare).astype(BF16)
+        for ref in refs:
+            ref[672 + b * 16 : 688 + b * 16, :] = val
+    for i in range(2):
+        pieces = [pltpu.roll(seconds[b], rest_shift(b), 1) for b in range(6 * i, min(6 * i + 6, 9))]
+        halves = [
+            jnp.where(inner < 19, part[0], jnp.where(inner < 38, part[1], part[2]))
+            for part in (pieces[0:3], pieces[-3:])
+        ]
+        val = jnp.where(lane < 64, halves[0], halves[1]).astype(BF16)
+        for ref in refs:
+            ref[816 + i * 16 : 832 + i * 16, :] = val
+
+
+def side_by_side(vals):
     low = low_lanes(16)
-    for i in range(5):
-        other = pltpu.roll(blocks[2 * i + 1], 64, 1) if 2 * i + 1 < 9 else blocks[2 * i]
-        ref[base + i * 16 : base + (i + 1) * 16, :] = jnp.where(low, blocks[2 * i], other).astype(BF16)
-
-
-def unpack_pair(ref, base, b):
-    val = ref[base + (b // 2) * 16 : base + (b // 2) * 16 + 16, :].astype(F32)
-    return pltpu.roll(val, 64, 1) if b % 2 else val
+    first = jnp.where(low, vals[0], pltpu.roll(vals[2], 64, 1))
+    return jnp.concatenate([first, jnp.where(low, vals[1], 0.0)], axis=0).astype(BF16)
+
+
+def unpack_second(ref, b):
+    lane = lax.broadcasted_iota(jnp.int32, (16, 128), 1)
+    first = ref[672 + b * 16 : 688 + b * 16, :].astype(F32)
+    rest = ref[816 + b // 6 * 16 : 832 + b // 6 * 16, :].astype(F32)
+    tail = pltpu.roll(rest, (128 - rest_shift(b)) % 128, 1)
+    return jnp.where(lane < 15, pltpu.roll(first, 79, 1), jnp.where(lane < 30, pltpu.roll(first, 30, 1), tail))
 
 
 def parents_of(ref, up_ref):
@@ -289,7 +314,7 @@
     pown_ref[0], pown_ref[1] = parents_of(own_ref, up_ref)
 
 
-def forward_kernel(part_ref, pown_ref, other_ref, coef_ref, up_ref, fa_ref, fb_ref, fo_ref, po_ref, pp_s):
+def forward_kernel(part_ref, pown_ref, other_ref, coef_ref, up_ref, fb_ref, fa_ref, fo_ref, po_ref, pq_ref, pp_s):
     core = lax.axis_index("gz")
     odd = lax.rem(lax.axis_index("gx"), 2)
 
@@ -316,25 +341,19 @@
                 face[576 + block * 16 : 592 + block * 16, :] = rest
     pp_s[0:2] = pown_ref[...]
     pp_s[2], pp_s[3] = parents_of(other_ref, up_ref)
-    second = []
+    firsts, seconds = [], []
     for x in range(3):
         for pos in range(3):
-            y = (0, 2, 1)[pos]
-            at = (x * 3 + y) * 16
+            at = (x * 3 + (0, 2, 1)[pos]) * 16
             values = [pp_s[v, at : at + 16, :].astype(F32) for v in range(4)]
-            first = combine(values, coef, 72).astype(BF16)
-            row = (x * 3 + pos) * 16
-            po_ref[0, x, pos * 16 : pos * 16 + 16, :] = first
-            fa_ref[672 + row : 688 + row, :] = first
-            fb_ref[672 + row : 688 + row, :] = first
-            val = combine(values, coef, 80)
-            po_ref[1, x, pos * 16 : pos * 16 + 16, :] = val.astype(BF16)
-            second.append(val)
-    pack_pairs(fa_ref, 816, second)
-    pack_pairs(fb_ref, 816, second)
-
-
-def table_kernel(off_ref, zt_ref, far_ref, wl_ref, wp_ref, t3_s, w_s, a_s):
+            firsts.append(combine(values, coef, 72))
+            seconds.append(combine(values, coef, 80))
+            po_ref[x, pos * 16 : pos * 16 + 16, :] = firsts[-1].astype(BF16)
+        pq_ref[x] = side_by_side(seconds[3 * x : 3 * x + 3])
+    pack_parents((fa_ref, fb_ref), firsts, seconds)
+
+
+def table_kernel(off_ref, zt_ref, far_ref, wl_ref, wp_ref, wq_ref, t3_s, w_s, a_s):
     core = lax.axis_index("gz")
     base = core * 80
 
@@ -364,8 +383,12 @@
         low = low_lanes(count)
         block = lax.broadcasted_iota(jnp.int32, (count, 128), 0)
         sign = -1.0
+        both = low
         if level == 0:
             sign = jnp.where(block < 56, zt_ref[base + 70], -1.0)
+        else:
+            both = low | (block >= 56)
+        turned = 168 if level == 0 else 56
 
         def two_terms(i, carry):
             k = 2 * i
@@ -380,8 +403,8 @@
             for e in range(2):
                 even = out[0:count, e * 128 : (e + 1) * 128]
                 odd = out[count : 2 * count, e * 128 : (e + 1) * 128]
-                w_s[pl.ds(k + e, count, stride=136), :] = jnp.where(low, even, odd)
-                w_s[pl.ds(k + e + 64, count, stride=136), :] = jnp.where(low, sign * odd, even)
+                w_s[pl.ds(k + e, count, stride=136), :] = jnp.where(both, even, odd)
+                w_s[pl.ds(k + e + 64, turned, stride=136), :] = jnp.where(low, sign * odd, even)[0:turned]
             return carry
 
         lax.fori_loop(0, 25, two_terms, 0, unroll=5)
@@ -393,7 +416,24 @@
             out_ref[b] = jnp.where(filled, val, 0.0).astype(BF16)
             return carry
 
-        lax.fori_loop(0, count, one_block, 0, unroll=4)
+        lax.fori_loop(0, turned, one_block, 0, unroll=4)
+    half = low_lanes(64)
+    kept = lax.broadcasted_iota(jnp.int32, (64, 128), 0) < TERMS
+
+    def one_step(xi, carry):
+        def block_of(dy):
+            if dy < -3 or dy > 3:
+                return jnp.zeros((64, 128), F32)
+            return w_s[pl.ds(pl.multiple_of((56 + xi * 7 + dy + 3) * 136, 8), 64), :]
+
+        for i in range(4):
+            d = 2 * i - 3
+            for p in range(2):
+                val = jnp.where(half, block_of(d + p), block_of(d + p - 1))
+                wq_ref[xi, p * 64 : p * 64 + 64, i * 128 : (i + 1) * 128] = jnp.where(kept, val, 0.0).astype(BF16)
+        return carry
+
+    lax.fori_loop(0, 7, one_step, 0)
 
 
 def weight_tiles(weights, s, diff, steps):
@@ -493,15 +533,17 @@
 
 
 def far_kernel(
-    a_ref, b_ref, acc_ref, po_ref, wl_ref, wp_ref, sa_ref, sb_ref, fh_ref, edge_ref, pown_ref, fl_s, fp_s, ex_s, px_s
+    b_ref, a_ref, acc_ref, po_ref, pq_ref, wl_ref, wp_ref, wq_ref,
+    sb_ref, sa_ref, fh_ref, edge_ref, pown_ref, fl_s, fp_s, fq_s, ex_s, px_s
 ):
     xodd = lax.rem(lax.axis_index("gx"), 2)
     yodd = lax.rem(lax.axis_index("gy"), 2)
     fl_s[:, 3:6] = jnp.zeros((SLOTS, 3, 2, 48, 128), BF16)
-    fp_s[:, :, 1, 16:32] = jnp.zeros((PSLOTS, 9, 16, 128), BF16)
+    fp_s[0, :, 1, 16:32] = jnp.zeros((9, 16, 128), BF16)
     part = po_ref[...]
-    fp_s[:, 3:6, 0] = part[:, :, 0:32]
-    fp_s[:, 3:6, 1, 0:16] = part[:, :, 32:48]
+    fp_s[0, 3:6, 0] = part[:, 0:32]
+    fp_s[0, 3:6, 1, 0:16] = part[:, 32:48]
+    fq_s[3:6] = pq_ref[...]
     for ref, far_side in ((a_ref, 1 - xodd), (b_ref, xodd)):
         for x in range(3):
             for par in range(2):
@@ -517,13 +559,9 @@
                         fh_ref[s, far_side * 3 + x, par, spot * 16 : spot * 16 + 16, :] = val
             for pos in range(3):
                 b = x * 3 + pos
-                pieces = (
-                    ref[672 + b * 16 : 688 + b * 16, :],
-                    unpack_pair(ref, 816, b).astype(BF16),
-                )
                 at = (pos % 2) * 16
-                for s in range(PSLOTS):
-                    fp_s[s, far_side * 6 + x, pos // 2, at : at + 16] = pieces[s]
+                fp_s[0, far_side * 6 + x, pos // 2, at : at + 16] = ref[672 + b * 16 : 688 + b * 16, :]
+            fq_s[far_side * 6 + x] = side_by_side([unpack_second(ref, x * 3 + pos) for pos in range(3)])
 
     def parent_put(s, x, yo, val):
         if 0 <= yo < 3:
@@ -561,13 +599,25 @@
             edge = (s * 6 + x) * 32
             edge_ref[edge : edge + 16, :] = low_next[:, 128:256]
             edge_ref[edge + 16 : edge + 32, :] = high_next[:, 0:128]
-    for s in range(PSLOTS):
-        lhs = field_rows(fp_s, s, range(7), 0, 3, 96)
-        accs = [
-            jnp.dot(lhs, weight_tiles(wp_ref, s, diff, range(7)), preferred_element_type=F32).reshape(3, 2, 16, 256)
-            for diff in range(-3, 1)
-        ]
-        share_out(accs, s, 3, 5, 3, parent_put)
+    lhs = field_rows(fp_s, 0, range(7), 0, 3, 96)
+    accs = [
+        jnp.dot(lhs, weight_tiles(wp_ref, 0, diff, range(7)), preferred_element_type=F32).reshape(3, 2, 16, 256)
+        for diff in range(-3, 1)
+    ]
+    share_out(accs, 0, 3, 5, 3, parent_put)
+    lhs = jnp.concatenate([fq_s[xi : xi + 3].reshape(96, 128) for xi in range(7)], axis=1)
+    acc = jnp.dot(lhs, wq_ref[...].reshape(896, 512), preferred_element_type=F32).reshape(3, 2, 16, 512)
+    for pair in range(5):
+        val = None
+        for diff in range(-3, 1):
+            spot = pair + diff
+            if 0 <= spot < 2:
+                piece = acc[:, spot, :, (diff + 3) * 128 : (diff + 4) * 128]
+                val = piece if val is None else val + piece
+        for x in range(3):
+            parent_put(1, x, 2 * pair - 3, val[x])
+            if pair < 4:
+                parent_put(1, x, 2 * pair - 2, pltpu.roll(val[x], 64, 1))
     for side, ref in ((1 - yodd, sa_ref), (yodd, sb_ref)):
         for x in range(6):
             outs_a, outs_b, rest = pack_three(
@@ -578,12 +628,10 @@
                 ref[at : at + 16, :] = outs_a[i]
                 ref[288 + at : 304 + at, :] = outs_b[i]
             ref[576 + x * 16 : 592 + x * 16, :] = rest
-        for b in range(9):
-            ref[672 + b * 16 : 688 + b * 16, :] = px_s[side, 0, b].astype(BF16)
-        pack_pairs(ref, 816, [px_s[side, 1, b] for b in range(9)])
-
-
-def join_kernel(own_ref, pown_ref, a_ref, b_ref, full_ref, zs_ref):
+        pack_parents((ref,), *[[px_s[side, s, b] for b in range(9)] for s in range(PSLOTS)])
+
+
+def join_kernel(own_ref, pown_ref, b_ref, a_ref, full_ref, zs_ref):
     yodd = lax.rem(lax.axis_index("gy"), 2)
     for ref, upper in ((a_ref, 1 - yodd), (b_ref, yodd)):
         for x in range(6):
@@ -606,7 +654,7 @@
                 if s == 0:
                     total = total + ref[672 + b * 16 : 688 + b * 16, :].astype(F32)
                 else:
-                    total = total + unpack_pair(ref, 816, b)
+                    total = total + unpack_second(ref, b)
             full_ref[row : row + 16, :] = total
             zs_ref[row : row + 16, :] = total.astype(BF16)
 
@@ -704,7 +752,7 @@
     vmem = pl.BlockSpec(memory_space=pltpu.VMEM)
     return call(
         table_kernel,
-        (shape((SLOTS * 56, 128, 128), BF16), shape((PSLOTS * 56, 128, 128), BF16)),
+        (shape((SLOTS * 56, 128, 128), BF16), shape((56, 128, 128), BF16), shape((7, 128, 512), BF16)),
         [
             pltpu.VMEM((64 * 104, 128), F32),
             pltpu.VMEM((SLOTS * 56 * 136, 128), F32),
@@ -747,7 +795,6 @@
             pltpu.VMEM((16, 2048), F32),
             pltpu.VMEM((1024, 2048), BF16),
             pltpu.VMEM((1024, 2048), BF16),
-            pltpu.VMEM((1024, 240), F32),
             pltpu.VMEM((3, 640, 128), F32),
             pltpu.SemaphoreType.DMA((3,)),
         ],
@@ -765,10 +812,10 @@
         1 << 27,
         2 * MIB,
     )(leaf_z, coefs, up)
-    face = shape((896, 128), BF16)
-    fa, fb, fo, po = call(
+    face = shape((848, 128), BF16)
+    fb, fa, fo, po, pq = call(
         forward_kernel,
-        (face, face, shape((SLOTS, 6, 2, 48, 128), BF16), shape((PSLOTS, 3, 48, 128), BF16)),
+        (face, face, shape((SLOTS, 6, 2, 48, 128), BF16), shape((3, 48, 128), BF16), shape((3, 32, 128), BF16)),
         [pltpu.VMEM((4, 144, 128), BF16)],
         8,
         1 << 28,
@@ -778,7 +825,7 @@
     fa = lax.ppermute(fa, "gx", inner)
     fb = lax.ppermute(fb, "gx", outer)
     fo, off = lax.optimization_barrier((fo, off))
-    wl, wp = far_weights(off, ztable, far)
+    wl, wp, wq = far_weights(off, ztable, far)
     near = call(
         near_kernel,
         shape((SLOTS * 576, 256), F32),
@@ -787,7 +834,7 @@
         2 * 144 * 1792 * 256 * 12,
         8 * MIB,
     )(fo, wl)
-    sa, sb, fh, edge, pown = call(
+    sb, sa, fh, edge, pown = call(
         far_kernel,
         (
             face,
@@ -798,14 +845,15 @@
         ),
         [
             pltpu.VMEM((SLOTS, 9, 2, 48, 128), BF16),
-            pltpu.VMEM((PSLOTS, 9, 2, 32, 128), BF16),
+            pltpu.VMEM((1, 9, 2, 32, 128), BF16),
+            pltpu.VMEM((9, 32, 128), BF16),
             pltpu.VMEM((2, SLOTS, 6, 3, 16, 128), F32),
             pltpu.VMEM((2, PSLOTS, 9, 16, 128), F32),
         ],
         16,
         2 * 288 * 1792 * 256 * 8,
         14 * MIB,
-    )(fa, fb, near, po, wl, wp)
+    )(fb, fa, near, po, pq, wl, wp, wq)
     inner, outer = swaps("gy")
     sa = lax.ppermute(sa, "gy", inner)
     sb = lax.ppermute(sb, "gy", outer)
@@ -829,7 +877,7 @@
     own, harm, one = lax.optimization_barrier((own, harm, one))
     full, zsend = call(
         join_kernel, (shape((2016, 128), F32), shape((2016, 128), BF16)), [], 8, 1 << 20, 3 * MIB
-    )(own, pown, sa, sb)
+    )(own, pown, sb, sa)
     zrecv = lax.ppermute(zsend, "gz", swap)
     part, ppart = call(
         back_kernel,

time: 47.5 us -> 46 us (0.968)
  starting transfers between devices: 16.8 us -> 15.1 us
  waiting for transfers between devices: 3.04 us -> 4.03 us
  Pallas kernels: 27 us -> 26.2 us
    ppermute x1, starting transfers between devices: 1.91 us -> 0.01 us  [per_device(): sa = lax.ppermute(sa, 'gy', inner)]
    ppermute x1, waiting for transfers between devices: 0.01 us -> 0.82 us  [per_device(): sa = lax.ppermute(sa, 'gy', inner)]
    ppermute x1, starting transfers between devices: 7.11 us -> 7.81 us  [per_device(): sb = lax.ppermute(sb, 'gy', outer)]
    ppermute x1, waiting for transfers between devices: 1 us -> 1.68 us  [per_device(): sb = lax.ppermute(sb, 'gy', outer)]
    ppermute x1, waiting for transfers between devices: 0.53 us -> 0.01 us  [per_device(): fb = lax.ppermute(fb, 'gx', outer)]
where the time goes in v3:
time: 46 us; the launch traced here: 45.9 us
  Pallas kernels  26.2 us (57%)
  starting transfers between devices  15.1 us (33%)
  waiting for transfers between devices  4.03 us (9%)
    ppermute x1, starting transfers between devices, per_device(): sb = lax.ppermute(sb, 'gy', outer)  7.81 us
    pallas_call x1, Pallas kernels, far_weights(): call(table_kernel, (shape((SLOTS * 56, 128, 128), BF16), shape((56, 128,...  7.51 us
    pallas_call x1, Pallas kernels, per_device(): call(poles_kernel, shape((1728, 128), BF16), [pltpu.VMEM((64, 2048), F32)...  4.28 us
    pallas_call x1, Pallas kernels, per_device(): call(atoms_kernel, shape((1, 1, 1, CH, 2048), F32), [pltpu.VMEM((2, 144,...  3.93 us
    ppermute x1, starting transfers between devices, per_device(): leaf_other = lax.ppermute(leaf_z, 'gz', swap)  3.32 us
    pallas_call x1, Pallas kernels, per_device(): call(far_kernel, (face, face, shape((SLOTS, 6, 2, 48, 128), BF16), shape(...  2.69 us
    pallas_call x1, Pallas kernels, per_device(): call(inner_kernel, shape((1728, 128), F32), [pltpu.VMEM((SLOTS, 12, 2, 48...  2.09 us
    ppermute x1, starting transfers between devices, per_device(): fb = lax.ppermute(fb, 'gx', outer)  2.02 us
  transfers between devices with their start and end apart: 6, of which 4 were waited for; matrix products, arithmetic and copies ran while one was open for 1% of the time, Pallas kernels for 30%

profile of v3, /device:TPU:1, one launch (start us, length us, event | category | flops | bytes accessed | tf_op | source)
XLA Modules:
  0.0 45.9 jit_solution(8514323905374586651)
XLA Ops:
  0.0 0.0 copy-start.3
  0.0 0.0 copy-start.5
  0.0 0.0 copy-start
  0.0 4.3 %shard_map.91.own_ref = bf16[1728,128]{1,0:T(8,128)(2,1)S(1)} custom-call(bf16[1,1,1,16,2048]{4,3,2,1,0:T(8,128)(2,1)} %ch_hbm.1, f32[48,128]{1,0:T(8,128)} %bitcast.14, s32[16,128]{1,0:T(8,128)} %bitcast.16), custom_call_target="tpu_custom_call" | custom-call | flops 2147483648 | bytes 2097152 | tf_op jit(solution)/shard_map/pallas_call | solution.py:785
  4.3 0.0 copy-start.1
  4.3 0.0 copy-start.2
  4.3 3.3 %collective-permute-start = (bf16[1728,128]{1,0:T(8,128)(2,1)S(1)}, bf16[1728,128]{1,0:T(8,128)(2,1)S(1)}, u32[]{:S(2)}, u32[]{:S(2)}) collective-permute-start(bf16[1728,128]{1,0:T(8,128)(2,1)S(1)} %shard_map.91.own_ref), channel_id=1, source_target_pairs={{0,1},{1,0},{2,3},{3,2},{4,5},{5,4},{6,7},{7,6},{8,9},{9,8},{10,11... | collective-permute-start | bytes 1327112 | tf_op jit(solution)/shard_map/ppermute | solution.py:806
  7.6 0.0 copy-done.3
  7.7 0.1 reshape.17
  7.8 0.0 copy-done.5
  7.9 0.0 copy-done
  7.9 0.5 %shard_map.92 = (f32[3,576,128]{2,1,0:T(8,128)S(1)}, bf16[2,144,128]{2,1,0:T(8,128)(2,1)S(1)}) custom-call(bf16[1728,128]{1,0:T(8,128)(2,1)S(1)} %shard_map.91.own_ref, f32[2,104,128]{2,1,0:T(8,128)S(1)} %copy-done, bf16[128,512]{1,0:T(8,128)(2,1)S(1)} %constant_dynamic-update-slice_fusion.up_ref), custom_call_target="tpu_custom_call" | custom-call | flops 134217728 | bytes 2097152 | tf_op jit(solution)/shard_map/pallas_call | solution.py:807
  8.4 0.7 %collective-permute-done.other_ref = bf16[1728,128]{1,0:T(8,128)(2,1)S(1)} collective-permute-done((bf16[1728,128]{1,0:T(8,128)(2,1)S(1)}, bf16[1728,128]{1,0:T(8,128)(2,1)S(1)}, u32[]{:S(2)}, u32[]{:S(2)}) %collective-permute-start) | collective-permute-done | bytes 442400 | tf_op jit(solution)/shard_map/ppermute | solution.py:806
  9.1 1.2 %shard_map.93 = (bf16[848,128]{1,0:T(8,128)(2,1)S(1)}, bf16[848,128]{1,0:T(8,128)(2,1)S(1)}, bf16[3,6,2,48,128]{4,3,2,1,0:T(8,128)(2,1)S(1)}, bf16[3,48,128]{2,1,0:T(8,128)(2,1)S(1)}, bf16[3,32,128]{2,1,0:T(8,128)(2,1)S(1)}) custom-call(f32[3,576,128]{2,1,0:T(8,128)S(1)} %get-tuple-element.34.part_ref, bf16[2,144,128]{2,1,0:T(8,128)(2,1)S(1)} %get-tuple-element.35.pown_ref, ...), custom_call_target="tpu_custom_call" | custom-call | flops 268435456 | bytes 2097152 | tf_op jit(solution)/shard_map/pallas_call | solution.py:816
  10.2 2.0 %collective-permute-start.1 = (bf16[848,128]{1,0:T(8,128)(2,1)S(1)}, bf16[848,128]{1,0:T(8,128)(2,1)S(1)}, u32[]{:S(2)}, u32[]{:S(2)}) collective-permute-start(bf16[848,128]{1,0:T(8,128)(2,1)S(1)} %get-tuple-element.38), channel_id=1, source_target_pairs={{0,224},{32,64},{64,32},{96,128},{128,96},{160,192},{192,160},{224... | collective-permute-start | bytes 651272 | tf_op jit(solution)/shard_map/ppermute | solution.py:826
  12.3 0.0 collective-permute-start.2
  12.3 0.0 copy-done.1
  12.3 0.0 copy-done.2
  12.3 7.5 %shard_map.94 = (bf16[168,128,128]{2,1,0:T(8,128)(2,1)S(1)}, bf16[56,128,128]{2,1,0:T(8,128)(2,1)S(1)}, bf16[7,128,512]{2,1,0:T(8,128)(2,1)S(1)}) custom-call(s32[6,128]{1,0:T(8,128)S(1)} %reshape.18.off_ref, f32[160]{0:T(256)S(1)} %copy-done.2, bf16[49,49,2,128]{3,2,1,0:T(2,128)(2,1)S(1)} %bitcast.10), custom_call_target="tpu_custom_call" | custom-call | flops 3596615680 | bytes 10485760 | tf_op jit(solution)/shard_map/pallas_call | solution.py:753
  19.8 2.0 %shard_map.95.acc_ref = f32[1728,256]{1,0:T(8,128)S(1)} custom-call(bf16[3,6,2,48,128]{4,3,2,1,0:T(8,128)(2,1)S(1)} %get-tuple-element.37.fo_ref, bf16[168,128,128]{2,1,0:T(8,128)(2,1)S(1)} %get-tuple-element.41.wl_ref), custom_call_target="tpu_custom_call" | custom-call | flops 1585446912 | bytes 8388608 | tf_op jit(solution)/shard_map/pallas_call | solution.py:829
  21.8 0.0 collective-permute-done.1.b_ref
  21.8 0.0 collective-permute-done.2.a_ref
  21.8 2.7 %shard_map.96 = (bf16[848,128]{1,0:T(8,128)(2,1)S(1)}, bf16[848,128]{1,0:T(8,128)(2,1)S(1)}, bf16[3,6,2,48,128]{4,3,2,1,0:T(8,128)(2,1)S(1)}, f32[576,128]{1,0:T(8,128)S(1)}, f32[288,128]{1,0:T(8,128)S(1)}) custom-call(bf16[848,128]{1,0:T(8,128)(2,1)S(1)} %collective-permute-done.1.b_ref, bf16[848,128]{1,0:T(8,128)(2,1)S(1)} %collective-permute-done.2.a_ref, ...), custom_call_target="tpu_custom_call" | custom-call | flops 2113929216 | bytes 14680064 | tf_op jit(solution)/shard_map/pallas_call | solution.py:837
  24.5 7.8 %collective-permute-start.3 = (bf16[848,128]{1,0:T(8,128)(2,1)S(1)}, bf16[848,128]{1,0:T(8,128)(2,1)S(1)}, u32[]{:S(2)}, u32[]{:S(2)}) collective-permute-start(bf16[848,128]{1,0:T(8,128)(2,1)S(1)} %get-tuple-element.55), channel_id=1, source_target_pairs={{0,30},{2,4},{4,2},{6,8},{8,6},{10,12},{12,10},{14,16},{16,14},{18... | collective-permute-start | bytes 651272 | tf_op jit(solution)/shard_map/ppermute | solution.py:859
  32.3 0.0 collective-permute-start.4
  32.3 1.3 %shard_map.98 = (f32[64,2048]{1,0:T(8,128)S(1)}, bf16[240,2048]{1,0:T(8,128)(2,1)S(1)}) custom-call(f32[48,128]{1,0:T(8,128)} %bitcast.15, s32[16,128]{1,0:T(8,128)} %bitcast.17), custom_call_target="tpu_custom_call" | custom-call | flops 16777216 | bytes 2097152 | tf_op jit(solution)/shard_map/pallas_call | solution.py:869
  33.6 0.0 copy-start.4
  33.6 2.1 %shard_map.97.own_ref = f32[1728,128]{1,0:T(8,128)S(1)} custom-call(bf16[3,6,2,48,128]{4,3,2,1,0:T(8,128)(2,1)S(1)} %get-tuple-element.37.fo_ref, bf16[3,6,2,48,128]{4,3,2,1,0:T(8,128)(2,1)S(1)} %get-tuple-element.46.fh_ref, f32[576,128]{1,0:T(8,128)S(1)} %get-tuple-element.48.edge_ref, bf16[168,128,128]{2,1,0:T(8,128)(2,1)S(1)} %get-tuple-element.41.wl_ref), custom_call_target="tpu_custom_call" | custom-call | flops 1585446912 | bytes 8388608 | tf_op jit(solution)/shard_map/pallas_call | solution.py:861
  35.7 1.7 %collective-permute-done.3.b_ref = bf16[848,128]{1,0:T(8,128)(2,1)S(1)} collective-permute-done((bf16[848,128]{1,0:T(8,128)(2,1)S(1)}, bf16[848,128]{1,0:T(8,128)(2,1)S(1)}, u32[]{:S(2)}, u32[]{:S(2)}) %collective-permute-start.3) | collective-permute-done | bytes 217120 | tf_op jit(solution)/shard_map/ppermute | solution.py:859
  37.4 0.8 %collective-permute-done.4.a_ref = bf16[848,128]{1,0:T(8,128)(2,1)S(1)} collective-permute-done((bf16[848,128]{1,0:T(8,128)(2,1)S(1)}, bf16[848,128]{1,0:T(8,128)(2,1)S(1)}, u32[]{:S(2)}, u32[]{:S(2)}) %collective-permute-start.4) | collective-permute-done | bytes 217120 | tf_op jit(solution)/shard_map/ppermute | solution.py:858
  38.2 0.3 shard_map.99
  38.5 1.9 %collective-permute-start.5 = (bf16[2016,128]{1,0:T(8,128)(2,1)S(1)}, bf16[2016,128]{1,0:T(8,128)(2,1)S(1)}, u32[]{:S(2)}, u32[]{:S(2)}) collective-permute-start(bf16[2016,128]{1,0:T(8,128)(2,1)S(1)} %get-tuple-element.60), channel_id=1, source_target_pairs={{0,1},{1,0},{2,3},{3,2},{4,5},{5,4},{6,7},{7,6},{8,9},{9,8},{10,11... | collective-permute-start | bytes 1548296 | tf_op jit(solution)/shard_map/ppermute | solution.py:881
  40.4 0.0 copy-done.4
  40.5 0.1 pad_bitcast_fusion.1
  40.6 0.4 shard_map.100
  41.1 0.9 %collective-permute-done.5.other_ref = bf16[2016,128]{1,0:T(8,128)(2,1)S(1)} collective-permute-done((bf16[2016,128]{1,0:T(8,128)(2,1)S(1)}, bf16[2016,128]{1,0:T(8,128)(2,1)S(1)}, u32[]{:S(2)}, u32[]{:S(2)}) %collective-permute-start.5) | collective-permute-done | bytes 516128 | tf_op jit(solution)/shard_map/ppermute | solution.py:881
  42.0 3.9 %shard_map.101 = f32[1,1,1,16,2048]{4,3,2,1,0:T(8,128)} custom-call(f32[3,576,128]{2,1,0:T(8,128)S(1)} %get-tuple-element.58.part_ref, f32[2,144,128]{2,1,0:T(8,128)S(1)} %get-tuple-element.59.ppart_ref, bf16[2016,128]{1,0:T(8,128)(2,1)S(1)} %collective-permute-done.5.other_ref, f32[2,104,128]{2,1,0:T(8,128)S(1)} %copy-done, ...), custom_call_target="tpu_custom_call" | custom-call | flops 2147483648 | bytes 2097152 | tf_op jit(solution)/shard_map/pallas_call | solution.py:890
  (7 shorter events, 0.1 us)
Async XLA Ops:
  0.0 7.6 %copy-start.3 = (bf16[8,49,49]{2,0,1:T(8,128)(2,1)S(1)}, bf16[8,49,49]{2,0,1:T(8,128)(2,1)}, u32[]{:S(2)}) copy-start(bf16[8,49,49]{2,0,1:T(8,128)(2,1)} %param.14) | copy-start | bytes 115252
  0.0 7.8 %copy-start.5 = (s32[2,128,3]{1,0,2:T(2,128)S(1)}, s32[2,128,3]{1,0,2:T(2,128)}, u32[]{:S(2)}) copy-start(s32[2,128,3]{1,0,2:T(2,128)} %param.12) | copy-start | bytes 9220
  0.0 7.9 %copy-start = (f32[2,104,128]{2,1,0:T(8,128)S(1)}, f32[2,104,128]{2,1,0:T(8,128)}, u32[]{:S(2)}) copy-start(f32[2,104,128]{2,1,0:T(8,128)} %constant.8.clone.coef_ref) | copy-start | bytes 319492
  4.3 8.0 %copy-start.1 = (bf16[2,49,49,128]{3,0,2,1:T(2,128)(2,1)S(1)}, bf16[2,49,49,128]{3,0,2,1:T(2,128)(2,1)}, u32[]{:S(2)}) copy-start(bf16[2,49,49,128]{3,0,2,1:T(2,128)(2,1)} %param.13) | copy-start | bytes 3687940
  4.3 8.0 %copy-start.2 = (f32[160]{0:T(256)S(1)}, f32[160]{0:T(256)}, u32[]{:S(2)}) copy-start(f32[160]{0:T(256)} %constant.9.clone.zt_ref) | copy-start | bytes 1924
  4.3 4.7 %collective-permute-start = (bf16[1728,128]{1,0:T(8,128)(2,1)S(1)}, bf16[1728,128]{1,0:T(8,128)(2,1)S(1)}, u32[]{:S(2)}, u32[]{:S(2)}) collective-permute-start(bf16[1728,128]{1,0:T(8,128)(2,1)S(1)} %shard_map.91.own_ref), channel_id=1, source_target_pairs={{0,1},{1,0},{2,3},{3,2},{4,5},{5,4},{6,7},{7,6},{8,9},{9,8},{10,11... | collective-permute-start | bytes 1327112 | tf_op jit(solution)/shard_map/ppermute | solution.py:806
  10.2 11.6 %collective-permute-start.1 = (bf16[848,128]{1,0:T(8,128)(2,1)S(1)}, bf16[848,128]{1,0:T(8,128)(2,1)S(1)}, u32[]{:S(2)}, u32[]{:S(2)}) collective-permute-start(bf16[848,128]{1,0:T(8,128)(2,1)S(1)} %get-tuple-element.38), channel_id=1, source_target_pairs={{0,224},{32,64},{64,32},{96,128},{128,96},{160,192},{192,160},{224... | collective-permute-start | bytes 651272 | tf_op jit(solution)/shard_map/ppermute | solution.py:826
  12.3 9.5 %collective-permute-start.2 = (bf16[848,128]{1,0:T(8,128)(2,1)S(1)}, bf16[848,128]{1,0:T(8,128)(2,1)S(1)}, u32[]{:S(2)}, u32[]{:S(2)}) collective-permute-start(bf16[848,128]{1,0:T(8,128)(2,1)S(1)} %get-tuple-element.39), channel_id=1, source_target_pairs={{0,32},{32,0},{64,96},{96,64},{128,160},{160,128},{192,224},{224,1... | collective-permute-start | bytes 651272 | tf_op jit(solution)/shard_map/ppermute | solution.py:825
  24.5 12.9 %collective-permute-start.3 = (bf16[848,128]{1,0:T(8,128)(2,1)S(1)}, bf16[848,128]{1,0:T(8,128)(2,1)S(1)}, u32[]{:S(2)}, u32[]{:S(2)}) collective-permute-start(bf16[848,128]{1,0:T(8,128)(2,1)S(1)} %get-tuple-element.55), channel_id=1, source_target_pairs={{0,30},{2,4},{4,2},{6,8},{8,6},{10,12},{12,10},{14,16},{16,14},{18... | collective-permute-start | bytes 651272 | tf_op jit(solution)/shard_map/ppermute | solution.py:859
  32.3 5.9 %collective-permute-start.4 = (bf16[848,128]{1,0:T(8,128)(2,1)S(1)}, bf16[848,128]{1,0:T(8,128)(2,1)S(1)}, u32[]{:S(2)}, u32[]{:S(2)}) collective-permute-start(bf16[848,128]{1,0:T(8,128)(2,1)S(1)} %get-tuple-element.56), channel_id=1, source_target_pairs={{0,2},{2,0},{4,6},{6,4},{8,10},{10,8},{12,14},{14,12},{16,18},{18,... | collective-permute-start | bytes 651272 | tf_op jit(solution)/shard_map/ppermute | solution.py:858
  33.6 6.8 %copy-start.4 = (bf16[8,49,49]{2,0,1:T(8,128)(2,1)S(1)}, bf16[8,49,49]{2,0,1:T(8,128)(2,1)}, u32[]{:S(2)}) copy-start(bf16[8,49,49]{2,0,1:T(8,128)(2,1)} %param.15) | copy-start | bytes 115252
  38.5 3.5 %collective-permute-start.5 = (bf16[2016,128]{1,0:T(8,128)(2,1)S(1)}, bf16[2016,128]{1,0:T(8,128)(2,1)S(1)}, u32[]{:S(2)}, u32[]{:S(2)}) collective-permute-start(bf16[2016,128]{1,0:T(8,128)(2,1)S(1)} %get-tuple-element.60), channel_id=1, source_target_pairs={{0,1},{1,0},{2,3},{3,2},{4,5},{5,4},{6,7},{7,6},{8,9},{9,8},{10,11... | collective-permute-start | bytes 1548296 | tf_op jit(solution)/shard_map/ppermute | solution.py:881

commit v4 on v3

--- a/solution.py
+++ b/solution.py
@@ -152,7 +152,7 @@
 
 
 def cell_number_rows():
-    row = lax.broadcasted_iota(jnp.int32, (240, 128), 0)
+    row = lax.broadcasted_iota(jnp.int32, (256, 128), 0)
     z = jnp.zeros_like(row)
     for i in range(1, 6):
         z = z + (row >= 40 * i).astype(jnp.int32)
@@ -189,7 +189,7 @@
     fill_onehot(cell_ref, one_ref)
 
 
-def poles_kernel(ch_hbm, pos_hbm, cell_hbm, zs_ref, h_s, one_s, ch_s, pos_s, cell_s, h3_s, chf_s, whi_s, wlo_s, f_s, sems):
+def poles_kernel(ch_hbm, pos_hbm, cell_hbm, zs_ref, h_s, one_s, ch_s, pos_s, cell_s, h3_s, chf_s, w_s, f_s, sems):
     copies = start_copies(((pos_hbm, pos_s), (cell_hbm, cell_s), (ch_hbm.at[0, 0, 0], ch_s)), sems)
     copies[0].wait()
     fill_harmonics(pos_s, h3_s, h_s)
@@ -204,11 +204,11 @@
                 sl = slice(i * 512, (i + 1) * 512)
                 w = h_s[:, sl] * chf_s[c : c + 1, sl]
                 hi = w.astype(BF16)
-                whi_s[c * 64 : (c + 1) * 64, sl] = hi
-                wlo_s[c * 64 : (c + 1) * 64, sl] = (w - hi.astype(F32)).astype(BF16)
+                w_s[c * 64 : (c + 1) * 64, sl] = hi
+                w_s[c * 64 : (c + 1) * 64, 2048 + i * 512 : 2560 + i * 512] = (w - hi.astype(F32)).astype(BF16)
         rows = slice(n * 256, (n + 1) * 256)
-        r = lax.dot_general(one_s[...], whi_s[rows, :], NT, preferred_element_type=F32)
-        r = r + lax.dot_general(one_s[...], wlo_s[rows, :], NT, preferred_element_type=F32)
+        twice = jnp.concatenate([one_s[...], one_s[...]], axis=1)
+        r = lax.dot_general(twice, w_s[rows, :], NT, preferred_element_type=F32)
         for half in range(2):
             c = n * 4 + half * 2
             for zp in range(3):
@@ -687,9 +687,12 @@
         values = [other_ref[at + s * 144 : at + s * 144 + 16, :].astype(F32) for s in range(PSLOTS)]
         for p in range(2):
             total = ppart_ref[p, i * 16 : (i + 1) * 16, :] + combine(values, coef, 92 + p * 8)
-            pf_s[p, i * 16 : (i + 1) * 16, :] = total.astype(BF16)
+            hi = total.astype(BF16)
+            pf_s[p, i * 16 : (i + 1) * 16, 0:128] = hi
+            pf_s[p, i * 16 : (i + 1) * 16, 128:256] = (total - hi.astype(F32)).astype(BF16)
     for k in range(3):
-        lift_s[k] = lax.dot_general(pf_s[k // 2], down_ref[k % 2], NT, preferred_element_type=F32)
+        table = jnp.concatenate([down_ref[k % 2], down_ref[k % 2]], axis=1)
+        lift_s[k] = lax.dot_general(pf_s[k // 2], table, NT, preferred_element_type=F32)
     for x in range(6):
         for y in range(6):
             at = (x * 6 + y) * 16
@@ -714,13 +717,18 @@
                 hi = val.astype(BF16).astype(F32)
                 l2_s[z * 40 : (z + 1) * 40, cp * 128 : (cp + 1) * 128] = hi
                 l3_s[z * 40 : (z + 1) * 40, cp * 128 : (cp + 1) * 128] = val - hi
-    high_rows, low_rows = [
-        ref[...].T.reshape(CH, 64, 240)[:, 0:56].reshape(CH * 56, 240).astype(BF16) for ref in (l2_s, l3_s)
-    ]
+    for ref in (l2_s, l3_s):
+        ref[240:256, :] = jnp.zeros((16, 1024), F32)
+    rows = jnp.concatenate(
+        [
+            ref[...].T.reshape(CH, 64, 256)[:, 0:56].reshape(CH * 56, 256).astype(BF16)
+            for ref in (l2_s, l3_s)
+        ],
+        axis=1,
+    )
     for i in range(8):
         one = one_ref[:, i * 256 : (i + 1) * 256]
-        spread = jnp.dot(high_rows, one, preferred_element_type=F32)
-        spread = spread + jnp.dot(low_rows, one, preferred_element_type=F32)
+        spread = jnp.dot(rows, jnp.concatenate([one, one], axis=0), preferred_element_type=F32)
         spread = spread.reshape(CH, 56, 256) * h_ref[0:56, i * 256 : (i + 1) * 256][None]
         out_ref[0, 0, 0, :, i * 256 : (i + 1) * 256] = jnp.sum(spread, axis=1)
 
@@ -787,14 +795,13 @@
         shape((1728, 128), BF16),
         [
             pltpu.VMEM((64, 2048), F32),
-            pltpu.VMEM((240, 2048), BF16),
+            pltpu.VMEM((256, 2048), BF16),
             pltpu.VMEM((16, 2048), BF16),
             pltpu.VMEM((48, 128), F32),
             pltpu.VMEM((16, 128), jnp.int32),
             pltpu.VMEM((1024, 128), F32),
             pltpu.VMEM((16, 2048), F32),
-            pltpu.VMEM((1024, 2048), BF16),
-            pltpu.VMEM((1024, 2048), BF16),
+            pltpu.VMEM((1024, 4096), BF16),
             pltpu.VMEM((3, 640, 128), F32),
             pltpu.SemaphoreType.DMA((3,)),
         ],
@@ -868,7 +875,7 @@
     )(fo, fh, edge, wl)
     harm, one = call(
         atom_terms_kernel,
-        (shape((64, 2048), F32), shape((240, 2048), BF16)),
+        (shape((64, 2048), F32), shape((256, 2048), BF16)),
         [pltpu.VMEM((1024, 128), F32)],
         8,
         1 << 24,
@@ -891,11 +898,11 @@
         atoms_kernel,
         shape((1, 1, 1, CH, 2048), F32),
         [
-            pltpu.VMEM((2, 144, 128), BF16),
+            pltpu.VMEM((2, 144, 256), BF16),
             pltpu.VMEM((3, 144, 512), F32),
             pltpu.VMEM((3, 640, 128), F32),
-            pltpu.VMEM((240, 1024), F32),
-            pltpu.VMEM((240, 1024), F32),
+            pltpu.VMEM((256, 1024), F32),
+            pltpu.VMEM((256, 1024), F32),
         ],
         16,
         2 * 2 * 256 * 2048 * 1024,

time: 46 us -> 45.9 us (level)
  no operation moved by 1% of the time
where the time goes in v4:
time: 45.9 us; the launch traced here: 45.8 us
  Pallas kernels  26.1 us (57%)
  starting transfers between devices  15.1 us (33%)
  waiting for transfers between devices  4.01 us (9%)
    ppermute x1, starting transfers between devices, per_device(): sb = lax.ppermute(sb, 'gy', outer)  7.82 us
    pallas_call x1, Pallas kernels, far_weights(): call(table_kernel, (shape((SLOTS * 56, 128, 128), BF16), shape((56, 128,...  7.5 us
    pallas_call x1, Pallas kernels, per_device(): call(poles_kernel, shape((1728, 128), BF16), [pltpu.VMEM((64, 2048), F32)...  4.11 us
    pallas_call x1, Pallas kernels, per_device(): call(atoms_kernel, shape((1, 1, 1, CH, 2048), F32), [pltpu.VMEM((2, 144,...  4.01 us
    ppermute x1, starting transfers between devices, per_device(): leaf_other = lax.ppermute(leaf_z, 'gz', swap)  3.31 us
    pallas_call x1, Pallas kernels, per_device(): call(far_kernel, (face, face, shape((SLOTS, 6, 2, 48, 128), BF16), shape(...  2.69 us
    pallas_call x1, Pallas kernels, per_device(): call(inner_kernel, shape((1728, 128), F32), [pltpu.VMEM((SLOTS, 12, 2, 48...  2.09 us
    ppermute x1, starting transfers between devices, per_device(): fb = lax.ppermute(fb, 'gx', outer)  2.01 us
  transfers between devices with their start and end apart: 6, of which 4 were waited for; matrix products, arithmetic and copies ran while one was open for 1% of the time, Pallas kernels for 30%

profile of v4, /device:TPU:1, one launch (start us, length us, event | category | flops | bytes accessed | tf_op | source)
XLA Modules:
  0.0 45.8 jit_solution(2423395247780891235)
XLA Ops:
  0.0 0.0 copy-start.3
  0.0 0.0 copy-start.5
  0.0 0.0 copy-start
  0.0 4.1 %shard_map.91.own_ref = bf16[1728,128]{1,0:T(8,128)(2,1)S(1)} custom-call(bf16[1,1,1,16,2048]{4,3,2,1,0:T(8,128)(2,1)} %ch_hbm.1, f32[48,128]{1,0:T(8,128)} %bitcast.14, s32[16,128]{1,0:T(8,128)} %bitcast.16), custom_call_target="tpu_custom_call" | custom-call | flops 2147483648 | bytes 2097152 | tf_op jit(solution)/shard_map/pallas_call | solution.py:793
  4.1 0.0 copy-start.1
  4.1 0.0 copy-start.2
  4.2 3.3 %collective-permute-start = (bf16[1728,128]{1,0:T(8,128)(2,1)S(1)}, bf16[1728,128]{1,0:T(8,128)(2,1)S(1)}, u32[]{:S(2)}, u32[]{:S(2)}) collective-permute-start(bf16[1728,128]{1,0:T(8,128)(2,1)S(1)} %shard_map.91.own_ref), channel_id=1, source_target_pairs={{0,1},{1,0},{2,3},{3,2},{4,5},{5,4},{6,7},{7,6},{8,9},{9,8},{10,11... | collective-permute-start | bytes 1327112 | tf_op jit(solution)/shard_map/ppermute | solution.py:813
  7.5 0.0 copy-done.3
  7.5 0.1 reshape.17
  7.6 0.0 copy-done.5
  7.7 0.0 copy-done
  7.7 0.5 %shard_map.92 = (f32[3,576,128]{2,1,0:T(8,128)S(1)}, bf16[2,144,128]{2,1,0:T(8,128)(2,1)S(1)}) custom-call(bf16[1728,128]{1,0:T(8,128)(2,1)S(1)} %shard_map.91.own_ref, f32[2,104,128]{2,1,0:T(8,128)S(1)} %copy-done, bf16[128,512]{1,0:T(8,128)(2,1)S(1)} %constant_dynamic-update-slice_fusion.up_ref), custom_call_target="tpu_custom_call" | custom-call | flops 134217728 | bytes 2097152 | tf_op jit(solution)/shard_map/pallas_call | solution.py:814
  8.2 0.7 %collective-permute-done.other_ref = bf16[1728,128]{1,0:T(8,128)(2,1)S(1)} collective-permute-done((bf16[1728,128]{1,0:T(8,128)(2,1)S(1)}, bf16[1728,128]{1,0:T(8,128)(2,1)S(1)}, u32[]{:S(2)}, u32[]{:S(2)}) %collective-permute-start) | collective-permute-done | bytes 442400 | tf_op jit(solution)/shard_map/ppermute | solution.py:813
  8.9 1.2 %shard_map.93 = (bf16[848,128]{1,0:T(8,128)(2,1)S(1)}, bf16[848,128]{1,0:T(8,128)(2,1)S(1)}, bf16[3,6,2,48,128]{4,3,2,1,0:T(8,128)(2,1)S(1)}, bf16[3,48,128]{2,1,0:T(8,128)(2,1)S(1)}, bf16[3,32,128]{2,1,0:T(8,128)(2,1)S(1)}) custom-call(f32[3,576,128]{2,1,0:T(8,128)S(1)} %get-tuple-element.34.part_ref, bf16[2,144,128]{2,1,0:T(8,128)(2,1)S(1)} %get-tuple-element.35.pown_ref, ...), custom_call_target="tpu_custom_call" | custom-call | flops 268435456 | bytes 2097152 | tf_op jit(solution)/shard_map/pallas_call | solution.py:823
  10.1 2.0 %collective-permute-start.1 = (bf16[848,128]{1,0:T(8,128)(2,1)S(1)}, bf16[848,128]{1,0:T(8,128)(2,1)S(1)}, u32[]{:S(2)}, u32[]{:S(2)}) collective-permute-start(bf16[848,128]{1,0:T(8,128)(2,1)S(1)} %get-tuple-element.38), channel_id=1, source_target_pairs={{0,224},{32,64},{64,32},{96,128},{128,96},{160,192},{192,160},{224... | collective-permute-start | bytes 651272 | tf_op jit(solution)/shard_map/ppermute | solution.py:833
  12.1 0.0 collective-permute-start.2
  12.1 0.0 copy-done.1
  12.1 0.0 copy-done.2
  12.1 7.5 %shard_map.94 = (bf16[168,128,128]{2,1,0:T(8,128)(2,1)S(1)}, bf16[56,128,128]{2,1,0:T(8,128)(2,1)S(1)}, bf16[7,128,512]{2,1,0:T(8,128)(2,1)S(1)}) custom-call(s32[6,128]{1,0:T(8,128)S(1)} %reshape.18.off_ref, f32[160]{0:T(256)S(1)} %copy-done.2, bf16[49,49,2,128]{3,2,1,0:T(2,128)(2,1)S(1)} %bitcast.10), custom_call_target="tpu_custom_call" | custom-call | flops 3596615680 | bytes 10485760 | tf_op jit(solution)/shard_map/pallas_call | solution.py:761
  19.6 2.0 %shard_map.95.acc_ref = f32[1728,256]{1,0:T(8,128)S(1)} custom-call(bf16[3,6,2,48,128]{4,3,2,1,0:T(8,128)(2,1)S(1)} %get-tuple-element.37.fo_ref, bf16[168,128,128]{2,1,0:T(8,128)(2,1)S(1)} %get-tuple-element.41.wl_ref), custom_call_target="tpu_custom_call" | custom-call | flops 1585446912 | bytes 8388608 | tf_op jit(solution)/shard_map/pallas_call | solution.py:836
  21.6 0.0 collective-permute-done.1.b_ref
  21.6 0.0 collective-permute-done.2.a_ref
  21.6 2.7 %shard_map.96 = (bf16[848,128]{1,0:T(8,128)(2,1)S(1)}, bf16[848,128]{1,0:T(8,128)(2,1)S(1)}, bf16[3,6,2,48,128]{4,3,2,1,0:T(8,128)(2,1)S(1)}, f32[576,128]{1,0:T(8,128)S(1)}, f32[288,128]{1,0:T(8,128)S(1)}) custom-call(bf16[848,128]{1,0:T(8,128)(2,1)S(1)} %collective-permute-done.1.b_ref, bf16[848,128]{1,0:T(8,128)(2,1)S(1)} %collective-permute-done.2.a_ref, ...), custom_call_target="tpu_custom_call" | custom-call | flops 2113929216 | bytes 14680064 | tf_op jit(solution)/shard_map/pallas_call | solution.py:844
  24.3 7.8 %collective-permute-start.3 = (bf16[848,128]{1,0:T(8,128)(2,1)S(1)}, bf16[848,128]{1,0:T(8,128)(2,1)S(1)}, u32[]{:S(2)}, u32[]{:S(2)}) collective-permute-start(bf16[848,128]{1,0:T(8,128)(2,1)S(1)} %get-tuple-element.55), channel_id=1, source_target_pairs={{0,30},{2,4},{4,2},{6,8},{8,6},{10,12},{12,10},{14,16},{16,14},{18... | collective-permute-start | bytes 651272 | tf_op jit(solution)/shard_map/ppermute | solution.py:866
  32.1 0.0 collective-permute-start.4
  32.1 1.3 %shard_map.98 = (f32[64,2048]{1,0:T(8,128)S(1)}, bf16[256,2048]{1,0:T(8,128)(2,1)S(1)}) custom-call(f32[48,128]{1,0:T(8,128)} %bitcast.15, s32[16,128]{1,0:T(8,128)} %bitcast.17), custom_call_target="tpu_custom_call" | custom-call | flops 16777216 | bytes 2097152 | tf_op jit(solution)/shard_map/pallas_call | solution.py:876
  33.5 0.0 copy-start.4
  33.5 2.1 %shard_map.97.own_ref = f32[1728,128]{1,0:T(8,128)S(1)} custom-call(bf16[3,6,2,48,128]{4,3,2,1,0:T(8,128)(2,1)S(1)} %get-tuple-element.37.fo_ref, bf16[3,6,2,48,128]{4,3,2,1,0:T(8,128)(2,1)S(1)} %get-tuple-element.46.fh_ref, f32[576,128]{1,0:T(8,128)S(1)} %get-tuple-element.48.edge_ref, bf16[168,128,128]{2,1,0:T(8,128)(2,1)S(1)} %get-tuple-element.41.wl_ref), custom_call_target="tpu_custom_call" | custom-call | flops 1585446912 | bytes 8388608 | tf_op jit(solution)/shard_map/pallas_call | solution.py:868
  35.6 1.7 %collective-permute-done.3.b_ref = bf16[848,128]{1,0:T(8,128)(2,1)S(1)} collective-permute-done((bf16[848,128]{1,0:T(8,128)(2,1)S(1)}, bf16[848,128]{1,0:T(8,128)(2,1)S(1)}, u32[]{:S(2)}, u32[]{:S(2)}) %collective-permute-start.3) | collective-permute-done | bytes 217120 | tf_op jit(solution)/shard_map/ppermute | solution.py:866
  37.2 0.8 %collective-permute-done.4.a_ref = bf16[848,128]{1,0:T(8,128)(2,1)S(1)} collective-permute-done((bf16[848,128]{1,0:T(8,128)(2,1)S(1)}, bf16[848,128]{1,0:T(8,128)(2,1)S(1)}, u32[]{:S(2)}, u32[]{:S(2)}) %collective-permute-start.4) | collective-permute-done | bytes 217120 | tf_op jit(solution)/shard_map/ppermute | solution.py:865
  38.0 0.3 shard_map.99
  38.3 1.9 %collective-permute-start.5 = (bf16[2016,128]{1,0:T(8,128)(2,1)S(1)}, bf16[2016,128]{1,0:T(8,128)(2,1)S(1)}, u32[]{:S(2)}, u32[]{:S(2)}) collective-permute-start(bf16[2016,128]{1,0:T(8,128)(2,1)S(1)} %get-tuple-element.60), channel_id=1, source_target_pairs={{0,1},{1,0},{2,3},{3,2},{4,5},{5,4},{6,7},{7,6},{8,9},{9,8},{10,11... | collective-permute-start | bytes 1548296 | tf_op jit(solution)/shard_map/ppermute | solution.py:888
  40.2 0.0 copy-done.4
  40.3 0.1 pad_bitcast_fusion.1
  40.4 0.4 shard_map.100
  40.9 0.9 %collective-permute-done.5.other_ref = bf16[2016,128]{1,0:T(8,128)(2,1)S(1)} collective-permute-done((bf16[2016,128]{1,0:T(8,128)(2,1)S(1)}, bf16[2016,128]{1,0:T(8,128)(2,1)S(1)}, u32[]{:S(2)}, u32[]{:S(2)}) %collective-permute-start.5) | collective-permute-done | bytes 516128 | tf_op jit(solution)/shard_map/ppermute | solution.py:888
  41.8 4.0 %shard_map.101 = f32[1,1,1,16,2048]{4,3,2,1,0:T(8,128)} custom-call(f32[3,576,128]{2,1,0:T(8,128)S(1)} %get-tuple-element.58.part_ref, f32[2,144,128]{2,1,0:T(8,128)S(1)} %get-tuple-element.59.ppart_ref, bf16[2016,128]{1,0:T(8,128)(2,1)S(1)} %collective-permute-done.5.other_ref, f32[2,104,128]{2,1,0:T(8,128)S(1)} %copy-done, ...), custom_call_target="tpu_custom_call" | custom-call | flops 2147483648 | bytes 2097152 | tf_op jit(solution)/shard_map/pallas_call | solution.py:897
  (7 shorter events, 0.1 us)
Async XLA Ops:
  0.0 7.5 %copy-start.3 = (bf16[8,49,49]{2,0,1:T(8,128)(2,1)S(1)}, bf16[8,49,49]{2,0,1:T(8,128)(2,1)}, u32[]{:S(2)}) copy-start(bf16[8,49,49]{2,0,1:T(8,128)(2,1)} %param.14) | copy-start | bytes 115252
  0.0 7.6 %copy-start.5 = (s32[2,128,3]{1,0,2:T(2,128)S(1)}, s32[2,128,3]{1,0,2:T(2,128)}, u32[]{:S(2)}) copy-start(s32[2,128,3]{1,0,2:T(2,128)} %param.12) | copy-start | bytes 9220
  0.0 7.7 %copy-start = (f32[2,104,128]{2,1,0:T(8,128)S(1)}, f32[2,104,128]{2,1,0:T(8,128)}, u32[]{:S(2)}) copy-start(f32[2,104,128]{2,1,0:T(8,128)} %constant.8.clone.coef_ref) | copy-start | bytes 319492
  4.1 7.9 %copy-start.1 = (bf16[2,49,49,128]{3,0,2,1:T(2,128)(2,1)S(1)}, bf16[2,49,49,128]{3,0,2,1:T(2,128)(2,1)}, u32[]{:S(2)}) copy-start(bf16[2,49,49,128]{3,0,2,1:T(2,128)(2,1)} %param.13) | copy-start | bytes 3687940
  4.1 7.9 %copy-start.2 = (f32[160]{0:T(256)S(1)}, f32[160]{0:T(256)}, u32[]{:S(2)}) copy-start(f32[160]{0:T(256)} %constant.9.clone.zt_ref) | copy-start | bytes 1924
  4.2 4.7 %collective-permute-start = (bf16[1728,128]{1,0:T(8,128)(2,1)S(1)}, bf16[1728,128]{1,0:T(8,128)(2,1)S(1)}, u32[]{:S(2)}, u32[]{:S(2)}) collective-permute-start(bf16[1728,128]{1,0:T(8,128)(2,1)S(1)} %shard_map.91.own_ref), channel_id=1, source_target_pairs={{0,1},{1,0},{2,3},{3,2},{4,5},{5,4},{6,7},{7,6},{8,9},{9,8},{10,11... | collective-permute-start | bytes 1327112 | tf_op jit(solution)/shard_map/ppermute | solution.py:813
  10.1 11.5 %collective-permute-start.1 = (bf16[848,128]{1,0:T(8,128)(2,1)S(1)}, bf16[848,128]{1,0:T(8,128)(2,1)S(1)}, u32[]{:S(2)}, u32[]{:S(2)}) collective-permute-start(bf16[848,128]{1,0:T(8,128)(2,1)S(1)} %get-tuple-element.38), channel_id=1, source_target_pairs={{0,224},{32,64},{64,32},{96,128},{128,96},{160,192},{192,160},{224... | collective-permute-start | bytes 651272 | tf_op jit(solution)/shard_map/ppermute | solution.py:833
  12.1 9.5 %collective-permute-start.2 = (bf16[848,128]{1,0:T(8,128)(2,1)S(1)}, bf16[848,128]{1,0:T(8,128)(2,1)S(1)}, u32[]{:S(2)}, u32[]{:S(2)}) collective-permute-start(bf16[848,128]{1,0:T(8,128)(2,1)S(1)} %get-tuple-element.39), channel_id=1, source_target_pairs={{0,32},{32,0},{64,96},{96,64},{128,160},{160,128},{192,224},{224,1... | collective-permute-start | bytes 651272 | tf_op jit(solution)/shard_map/ppermute | solution.py:832
  24.3 12.9 %collective-permute-start.3 = (bf16[848,128]{1,0:T(8,128)(2,1)S(1)}, bf16[848,128]{1,0:T(8,128)(2,1)S(1)}, u32[]{:S(2)}, u32[]{:S(2)}) collective-permute-start(bf16[848,128]{1,0:T(8,128)(2,1)S(1)} %get-tuple-element.55), channel_id=1, source_target_pairs={{0,30},{2,4},{4,2},{6,8},{8,6},{10,12},{12,10},{14,16},{16,14},{18... | collective-permute-start | bytes 651272 | tf_op jit(solution)/shard_map/ppermute | solution.py:866
  32.1 5.9 %collective-permute-start.4 = (bf16[848,128]{1,0:T(8,128)(2,1)S(1)}, bf16[848,128]{1,0:T(8,128)(2,1)S(1)}, u32[]{:S(2)}, u32[]{:S(2)}) collective-permute-start(bf16[848,128]{1,0:T(8,128)(2,1)S(1)} %get-tuple-element.56), channel_id=1, source_target_pairs={{0,2},{2,0},{4,6},{6,4},{8,10},{10,8},{12,14},{14,12},{16,18},{18,... | collective-permute-start | bytes 651272 | tf_op jit(solution)/shard_map/ppermute | solution.py:865
  33.5 6.8 %copy-start.4 = (bf16[8,49,49]{2,0,1:T(8,128)(2,1)S(1)}, bf16[8,49,49]{2,0,1:T(8,128)(2,1)}, u32[]{:S(2)}) copy-start(bf16[8,49,49]{2,0,1:T(8,128)(2,1)} %param.15) | copy-start | bytes 115252
  38.3 3.5 %collective-permute-start.5 = (bf16[2016,128]{1,0:T(8,128)(2,1)S(1)}, bf16[2016,128]{1,0:T(8,128)(2,1)S(1)}, u32[]{:S(2)}, u32[]{:S(2)}) collective-permute-start(bf16[2016,128]{1,0:T(8,128)(2,1)S(1)} %get-tuple-element.60), channel_id=1, source_target_pairs={{0,1},{1,0},{2,3},{3,2},{4,5},{5,4},{6,7},{7,6},{8,9},{9,8},{10,11... | collective-permute-start | bytes 1548296 | tf_op jit(solution)/shard_map/ppermute | solution.py:888

commit v5 on v4

--- a/solution.py
+++ b/solution.py
@@ -676,7 +676,7 @@
             part_ref[zp, b * 16 : b * 16 + 16, :] = combine(values, coef, 36 + zp * 12)
 
 
-def atoms_kernel(part_ref, ppart_ref, other_ref, coef_ref, one_ref, h_ref, down_ref, out_ref, pf_s, lift_s, l_s, l2_s, l3_s):
+def atoms_kernel(part_ref, ppart_ref, other_ref, coef_ref, one_ref, h_ref, down_ref, out_ref, pf_s, lift_s, l_s, l2_s):
     core = lax.axis_index("gz")
 
     def coef(row):
@@ -714,21 +714,11 @@
             first = jnp.where(low, a, pltpu.roll(b, 64, 1))
             second = jnp.where(low, pltpu.roll(a, 64, 1), b)
             for z, val in ((2 * zp, first), (2 * zp + 1, second)):
-                hi = val.astype(BF16).astype(F32)
-                l2_s[z * 40 : (z + 1) * 40, cp * 128 : (cp + 1) * 128] = hi
-                l3_s[z * 40 : (z + 1) * 40, cp * 128 : (cp + 1) * 128] = val - hi
-    for ref in (l2_s, l3_s):
-        ref[240:256, :] = jnp.zeros((16, 1024), F32)
-    rows = jnp.concatenate(
-        [
-            ref[...].T.reshape(CH, 64, 256)[:, 0:56].reshape(CH * 56, 256).astype(BF16)
-            for ref in (l2_s, l3_s)
-        ],
-        axis=1,
-    )
+                l2_s[z * 40 : (z + 1) * 40, cp * 128 : (cp + 1) * 128] = val
+    l2_s[240:256, :] = jnp.zeros((16, 1024), F32)
+    rows = l2_s[...].T.reshape(CH, 64, 256)[:, 0:56].reshape(CH * 56, 256).astype(BF16)
     for i in range(8):
-        one = one_ref[:, i * 256 : (i + 1) * 256]
-        spread = jnp.dot(rows, jnp.concatenate([one, one], axis=0), preferred_element_type=F32)
+        spread = jnp.dot(rows, one_ref[:, i * 256 : (i + 1) * 256], preferred_element_type=F32)
         spread = spread.reshape(CH, 56, 256) * h_ref[0:56, i * 256 : (i + 1) * 256][None]
         out_ref[0, 0, 0, :, i * 256 : (i + 1) * 256] = jnp.sum(spread, axis=1)
 
@@ -902,7 +892,6 @@
             pltpu.VMEM((3, 144, 512), F32),
             pltpu.VMEM((3, 640, 128), F32),
             pltpu.VMEM((256, 1024), F32),
-            pltpu.VMEM((256, 1024), F32),
         ],
         16,
         2 * 2 * 256 * 2048 * 1024,

time: 45.9 us -> 44.9 us (0.978)
  Pallas kernels: 26.1 us -> 25 us
    pallas_call x1, Pallas kernels: 4.01 us -> 2.93 us  [per_device(): call(atoms_kernel, shape((1, 1, 1, CH, 2048), F32), [pltpu.VMEM((2, 144,...]
  transfers between devices with their start and end apart: 6 -> 6, of which waited for: 4 -> 4; matrix products, arithmetic and copies ran while one was open for 1% -> 1% of each run, Pallas kernels for 30% -> 31%
where the time goes in v5:
time: 44.9 us; the launch traced here: 44.7 us
  Pallas kernels  25 us (56%)
  starting transfers between devices  15.1 us (34%)
  waiting for transfers between devices  4.01 us (9%)
    ppermute x1, starting transfers between devices, per_device(): sb = lax.ppermute(sb, 'gy', outer)  7.82 us
    pallas_call x1, Pallas kernels, far_weights(): call(table_kernel, (shape((SLOTS * 56, 128, 128), BF16), shape((56, 128,...  7.5 us
    pallas_call x1, Pallas kernels, per_device(): call(poles_kernel, shape((1728, 128), BF16), [pltpu.VMEM((64, 2048), F32)...  4.11 us
    ppermute x1, starting transfers between devices, per_device(): leaf_other = lax.ppermute(leaf_z, 'gz', swap)  3.31 us
    pallas_call x1, Pallas kernels, per_device(): call(atoms_kernel, shape((1, 1, 1, CH, 2048), F32), [pltpu.VMEM((2, 144,...  2.93 us
    pallas_call x1, Pallas kernels, per_device(): call(far_kernel, (face, face, shape((SLOTS, 6, 2, 48, 128), BF16), shape(...  2.69 us
    pallas_call x1, Pallas kernels, per_device(): call(inner_kernel, shape((1728, 128), F32), [pltpu.VMEM((SLOTS, 12, 2, 48...  2.09 us
    ppermute x1, starting transfers between devices, per_device(): fb = lax.ppermute(fb, 'gx', outer)  2.01 us
  transfers between devices with their start and end apart: 6, of which 4 were waited for; matrix products, arithmetic and copies ran while one was open for 1% of the time, Pallas kernels for 31%

profile of v5, /device:TPU:1, one launch (start us, length us, event | category | flops | bytes accessed | tf_op | source)
XLA Modules:
  0.0 44.7 jit_solution(15480744624930293708)
XLA Ops:
  0.0 0.0 copy-start.3
  0.0 0.0 copy-start.5
  0.0 0.0 copy-start
  0.0 4.1 %shard_map.91.own_ref = bf16[1728,128]{1,0:T(8,128)(2,1)S(1)} custom-call(bf16[1,1,1,16,2048]{4,3,2,1,0:T(8,128)(2,1)} %ch_hbm.1, f32[48,128]{1,0:T(8,128)} %bitcast.14, s32[16,128]{1,0:T(8,128)} %bitcast.16), custom_call_target="tpu_custom_call" | custom-call | flops 2147483648 | bytes 2097152 | tf_op jit(solution)/shard_map/pallas_call | solution.py:783
  4.1 0.0 copy-start.1
  4.1 0.0 copy-start.2
  4.2 3.3 %collective-permute-start = (bf16[1728,128]{1,0:T(8,128)(2,1)S(1)}, bf16[1728,128]{1,0:T(8,128)(2,1)S(1)}, u32[]{:S(2)}, u32[]{:S(2)}) collective-permute-start(bf16[1728,128]{1,0:T(8,128)(2,1)S(1)} %shard_map.91.own_ref), channel_id=1, source_target_pairs={{0,1},{1,0},{2,3},{3,2},{4,5},{5,4},{6,7},{7,6},{8,9},{9,8},{10,11... | collective-permute-start | bytes 1327112 | tf_op jit(solution)/shard_map/ppermute | solution.py:803
  7.5 0.0 copy-done.3
  7.5 0.1 reshape.17
  7.6 0.0 copy-done.5
  7.7 0.0 copy-done
  7.7 0.5 %shard_map.92 = (f32[3,576,128]{2,1,0:T(8,128)S(1)}, bf16[2,144,128]{2,1,0:T(8,128)(2,1)S(1)}) custom-call(bf16[1728,128]{1,0:T(8,128)(2,1)S(1)} %shard_map.91.own_ref, f32[2,104,128]{2,1,0:T(8,128)S(1)} %copy-done, bf16[128,512]{1,0:T(8,128)(2,1)S(1)} %constant_dynamic-update-slice_fusion.up_ref), custom_call_target="tpu_custom_call" | custom-call | flops 134217728 | bytes 2097152 | tf_op jit(solution)/shard_map/pallas_call | solution.py:804
  8.2 0.7 %collective-permute-done.other_ref = bf16[1728,128]{1,0:T(8,128)(2,1)S(1)} collective-permute-done((bf16[1728,128]{1,0:T(8,128)(2,1)S(1)}, bf16[1728,128]{1,0:T(8,128)(2,1)S(1)}, u32[]{:S(2)}, u32[]{:S(2)}) %collective-permute-start) | collective-permute-done | bytes 442400 | tf_op jit(solution)/shard_map/ppermute | solution.py:803
  8.9 1.2 %shard_map.93 = (bf16[848,128]{1,0:T(8,128)(2,1)S(1)}, bf16[848,128]{1,0:T(8,128)(2,1)S(1)}, bf16[3,6,2,48,128]{4,3,2,1,0:T(8,128)(2,1)S(1)}, bf16[3,48,128]{2,1,0:T(8,128)(2,1)S(1)}, bf16[3,32,128]{2,1,0:T(8,128)(2,1)S(1)}) custom-call(f32[3,576,128]{2,1,0:T(8,128)S(1)} %get-tuple-element.34.part_ref, bf16[2,144,128]{2,1,0:T(8,128)(2,1)S(1)} %get-tuple-element.35.pown_ref, ...), custom_call_target="tpu_custom_call" | custom-call | flops 268435456 | bytes 2097152 | tf_op jit(solution)/shard_map/pallas_call | solution.py:813
  10.1 2.0 %collective-permute-start.1 = (bf16[848,128]{1,0:T(8,128)(2,1)S(1)}, bf16[848,128]{1,0:T(8,128)(2,1)S(1)}, u32[]{:S(2)}, u32[]{:S(2)}) collective-permute-start(bf16[848,128]{1,0:T(8,128)(2,1)S(1)} %get-tuple-element.38), channel_id=1, source_target_pairs={{0,224},{32,64},{64,32},{96,128},{128,96},{160,192},{192,160},{224... | collective-permute-start | bytes 651272 | tf_op jit(solution)/shard_map/ppermute | solution.py:823
  12.1 0.0 collective-permute-start.2
  12.1 0.0 copy-done.1
  12.1 0.0 copy-done.2
  12.1 7.5 %shard_map.94 = (bf16[168,128,128]{2,1,0:T(8,128)(2,1)S(1)}, bf16[56,128,128]{2,1,0:T(8,128)(2,1)S(1)}, bf16[7,128,512]{2,1,0:T(8,128)(2,1)S(1)}) custom-call(s32[6,128]{1,0:T(8,128)S(1)} %reshape.18.off_ref, f32[160]{0:T(256)S(1)} %copy-done.2, bf16[49,49,2,128]{3,2,1,0:T(2,128)(2,1)S(1)} %bitcast.10), custom_call_target="tpu_custom_call" | custom-call | flops 3596615680 | bytes 10485760 | tf_op jit(solution)/shard_map/pallas_call | solution.py:751
  19.6 2.0 %shard_map.95.acc_ref = f32[1728,256]{1,0:T(8,128)S(1)} custom-call(bf16[3,6,2,48,128]{4,3,2,1,0:T(8,128)(2,1)S(1)} %get-tuple-element.37.fo_ref, bf16[168,128,128]{2,1,0:T(8,128)(2,1)S(1)} %get-tuple-element.41.wl_ref), custom_call_target="tpu_custom_call" | custom-call | flops 1585446912 | bytes 8388608 | tf_op jit(solution)/shard_map/pallas_call | solution.py:826
  21.6 0.0 collective-permute-done.1.b_ref
  21.6 0.0 collective-permute-done.2.a_ref
  21.6 2.7 %shard_map.96 = (bf16[848,128]{1,0:T(8,128)(2,1)S(1)}, bf16[848,128]{1,0:T(8,128)(2,1)S(1)}, bf16[3,6,2,48,128]{4,3,2,1,0:T(8,128)(2,1)S(1)}, f32[576,128]{1,0:T(8,128)S(1)}, f32[288,128]{1,0:T(8,128)S(1)}) custom-call(bf16[848,128]{1,0:T(8,128)(2,1)S(1)} %collective-permute-done.1.b_ref, bf16[848,128]{1,0:T(8,128)(2,1)S(1)} %collective-permute-done.2.a_ref, ...), custom_call_target="tpu_custom_call" | custom-call | flops 2113929216 | bytes 14680064 | tf_op jit(solution)/shard_map/pallas_call | solution.py:834
  24.3 7.8 %collective-permute-start.3 = (bf16[848,128]{1,0:T(8,128)(2,1)S(1)}, bf16[848,128]{1,0:T(8,128)(2,1)S(1)}, u32[]{:S(2)}, u32[]{:S(2)}) collective-permute-start(bf16[848,128]{1,0:T(8,128)(2,1)S(1)} %get-tuple-element.55), channel_id=1, source_target_pairs={{0,30},{2,4},{4,2},{6,8},{8,6},{10,12},{12,10},{14,16},{16,14},{18... | collective-permute-start | bytes 651272 | tf_op jit(solution)/shard_map/ppermute | solution.py:856
  32.1 0.0 collective-permute-start.4
  32.1 1.3 %shard_map.98 = (f32[64,2048]{1,0:T(8,128)S(1)}, bf16[256,2048]{1,0:T(8,128)(2,1)S(1)}) custom-call(f32[48,128]{1,0:T(8,128)} %bitcast.15, s32[16,128]{1,0:T(8,128)} %bitcast.17), custom_call_target="tpu_custom_call" | custom-call | flops 16777216 | bytes 2097152 | tf_op jit(solution)/shard_map/pallas_call | solution.py:866
  33.5 0.0 copy-start.4
  33.5 2.1 %shard_map.97.own_ref = f32[1728,128]{1,0:T(8,128)S(1)} custom-call(bf16[3,6,2,48,128]{4,3,2,1,0:T(8,128)(2,1)S(1)} %get-tuple-element.37.fo_ref, bf16[3,6,2,48,128]{4,3,2,1,0:T(8,128)(2,1)S(1)} %get-tuple-element.46.fh_ref, f32[576,128]{1,0:T(8,128)S(1)} %get-tuple-element.48.edge_ref, bf16[168,128,128]{2,1,0:T(8,128)(2,1)S(1)} %get-tuple-element.41.wl_ref), custom_call_target="tpu_custom_call" | custom-call | flops 1585446912 | bytes 8388608 | tf_op jit(solution)/shard_map/pallas_call | solution.py:858
  35.6 1.7 %collective-permute-done.3.b_ref = bf16[848,128]{1,0:T(8,128)(2,1)S(1)} collective-permute-done((bf16[848,128]{1,0:T(8,128)(2,1)S(1)}, bf16[848,128]{1,0:T(8,128)(2,1)S(1)}, u32[]{:S(2)}, u32[]{:S(2)}) %collective-permute-start.3) | collective-permute-done | bytes 217120 | tf_op jit(solution)/shard_map/ppermute | solution.py:856
  37.2 0.8 %collective-permute-done.4.a_ref = bf16[848,128]{1,0:T(8,128)(2,1)S(1)} collective-permute-done((bf16[848,128]{1,0:T(8,128)(2,1)S(1)}, bf16[848,128]{1,0:T(8,128)(2,1)S(1)}, u32[]{:S(2)}, u32[]{:S(2)}) %collective-permute-start.4) | collective-permute-done | bytes 217120 | tf_op jit(solution)/shard_map/ppermute | solution.py:855
  38.0 0.3 shard_map.99
  38.3 1.9 %collective-permute-start.5 = (bf16[2016,128]{1,0:T(8,128)(2,1)S(1)}, bf16[2016,128]{1,0:T(8,128)(2,1)S(1)}, u32[]{:S(2)}, u32[]{:S(2)}) collective-permute-start(bf16[2016,128]{1,0:T(8,128)(2,1)S(1)} %get-tuple-element.60), channel_id=1, source_target_pairs={{0,1},{1,0},{2,3},{3,2},{4,5},{5,4},{6,7},{7,6},{8,9},{9,8},{10,11... | collective-permute-start | bytes 1548296 | tf_op jit(solution)/shard_map/ppermute | solution.py:878
  40.2 0.0 copy-done.4
  40.3 0.1 pad_bitcast_fusion.1
  40.4 0.4 shard_map.100
  40.9 0.9 %collective-permute-done.5.other_ref = bf16[2016,128]{1,0:T(8,128)(2,1)S(1)} collective-permute-done((bf16[2016,128]{1,0:T(8,128)(2,1)S(1)}, bf16[2016,128]{1,0:T(8,128)(2,1)S(1)}, u32[]{:S(2)}, u32[]{:S(2)}) %collective-permute-start.5) | collective-permute-done | bytes 516128 | tf_op jit(solution)/shard_map/ppermute | solution.py:878
  41.8 2.9 %shard_map.101 = f32[1,1,1,16,2048]{4,3,2,1,0:T(8,128)} custom-call(f32[3,576,128]{2,1,0:T(8,128)S(1)} %get-tuple-element.58.part_ref, f32[2,144,128]{2,1,0:T(8,128)S(1)} %get-tuple-element.59.ppart_ref, bf16[2016,128]{1,0:T(8,128)(2,1)S(1)} %collective-permute-done.5.other_ref, f32[2,104,128]{2,1,0:T(8,128)S(1)} %copy-done, ...), custom_call_target="tpu_custom_call" | custom-call | flops 2147483648 | bytes 2097152 | tf_op jit(solution)/shard_map/pallas_call | solution.py:887
  (7 shorter events, 0.1 us)
Async XLA Ops:
  0.0 7.5 %copy-start.3 = (bf16[8,49,49]{2,0,1:T(8,128)(2,1)S(1)}, bf16[8,49,49]{2,0,1:T(8,128)(2,1)}, u32[]{:S(2)}) copy-start(bf16[8,49,49]{2,0,1:T(8,128)(2,1)} %param.14) | copy-start | bytes 115252
  0.0 7.6 %copy-start.5 = (s32[2,128,3]{1,0,2:T(2,128)S(1)}, s32[2,128,3]{1,0,2:T(2,128)}, u32[]{:S(2)}) copy-start(s32[2,128,3]{1,0,2:T(2,128)} %param.12) | copy-start | bytes 9220
  0.0 7.7 %copy-start = (f32[2,104,128]{2,1,0:T(8,128)S(1)}, f32[2,104,128]{2,1,0:T(8,128)}, u32[]{:S(2)}) copy-start(f32[2,104,128]{2,1,0:T(8,128)} %constant.8.clone.coef_ref) | copy-start | bytes 319492
  4.1 7.9 %copy-start.1 = (bf16[2,49,49,128]{3,0,2,1:T(2,128)(2,1)S(1)}, bf16[2,49,49,128]{3,0,2,1:T(2,128)(2,1)}, u32[]{:S(2)}) copy-start(bf16[2,49,49,128]{3,0,2,1:T(2,128)(2,1)} %param.13) | copy-start | bytes 3687940
  4.1 7.9 %copy-start.2 = (f32[160]{0:T(256)S(1)}, f32[160]{0:T(256)}, u32[]{:S(2)}) copy-start(f32[160]{0:T(256)} %constant.9.clone.zt_ref) | copy-start | bytes 1924
  4.2 4.7 %collective-permute-start = (bf16[1728,128]{1,0:T(8,128)(2,1)S(1)}, bf16[1728,128]{1,0:T(8,128)(2,1)S(1)}, u32[]{:S(2)}, u32[]{:S(2)}) collective-permute-start(bf16[1728,128]{1,0:T(8,128)(2,1)S(1)} %shard_map.91.own_ref), channel_id=1, source_target_pairs={{0,1},{1,0},{2,3},{3,2},{4,5},{5,4},{6,7},{7,6},{8,9},{9,8},{10,11... | collective-permute-start | bytes 1327112 | tf_op jit(solution)/shard_map/ppermute | solution.py:803
  10.1 11.5 %collective-permute-start.1 = (bf16[848,128]{1,0:T(8,128)(2,1)S(1)}, bf16[848,128]{1,0:T(8,128)(2,1)S(1)}, u32[]{:S(2)}, u32[]{:S(2)}) collective-permute-start(bf16[848,128]{1,0:T(8,128)(2,1)S(1)} %get-tuple-element.38), channel_id=1, source_target_pairs={{0,224},{32,64},{64,32},{96,128},{128,96},{160,192},{192,160},{224... | collective-permute-start | bytes 651272 | tf_op jit(solution)/shard_map/ppermute | solution.py:823
  12.1 9.5 %collective-permute-start.2 = (bf16[848,128]{1,0:T(8,128)(2,1)S(1)}, bf16[848,128]{1,0:T(8,128)(2,1)S(1)}, u32[]{:S(2)}, u32[]{:S(2)}) collective-permute-start(bf16[848,128]{1,0:T(8,128)(2,1)S(1)} %get-tuple-element.39), channel_id=1, source_target_pairs={{0,32},{32,0},{64,96},{96,64},{128,160},{160,128},{192,224},{224,1... | collective-permute-start | bytes 651272 | tf_op jit(solution)/shard_map/ppermute | solution.py:822
  24.3 12.9 %collective-permute-start.3 = (bf16[848,128]{1,0:T(8,128)(2,1)S(1)}, bf16[848,128]{1,0:T(8,128)(2,1)S(1)}, u32[]{:S(2)}, u32[]{:S(2)}) collective-permute-start(bf16[848,128]{1,0:T(8,128)(2,1)S(1)} %get-tuple-element.55), channel_id=1, source_target_pairs={{0,30},{2,4},{4,2},{6,8},{8,6},{10,12},{12,10},{14,16},{16,14},{18... | collective-permute-start | bytes 651272 | tf_op jit(solution)/shard_map/ppermute | solution.py:856
  32.1 5.9 %collective-permute-start.4 = (bf16[848,128]{1,0:T(8,128)(2,1)S(1)}, bf16[848,128]{1,0:T(8,128)(2,1)S(1)}, u32[]{:S(2)}, u32[]{:S(2)}) collective-permute-start(bf16[848,128]{1,0:T(8,128)(2,1)S(1)} %get-tuple-element.56), channel_id=1, source_target_pairs={{0,2},{2,0},{4,6},{6,4},{8,10},{10,8},{12,14},{14,12},{16,18},{18,... | collective-permute-start | bytes 651272 | tf_op jit(solution)/shard_map/ppermute | solution.py:855
  33.5 6.8 %copy-start.4 = (bf16[8,49,49]{2,0,1:T(8,128)(2,1)S(1)}, bf16[8,49,49]{2,0,1:T(8,128)(2,1)}, u32[]{:S(2)}) copy-start(bf16[8,49,49]{2,0,1:T(8,128)(2,1)} %param.15) | copy-start | bytes 115252
  38.3 3.5 %collective-permute-start.5 = (bf16[2016,128]{1,0:T(8,128)(2,1)S(1)}, bf16[2016,128]{1,0:T(8,128)(2,1)S(1)}, u32[]{:S(2)}, u32[]{:S(2)}) collective-permute-start(bf16[2016,128]{1,0:T(8,128)(2,1)S(1)} %get-tuple-element.60), channel_id=1, source_target_pairs={{0,1},{1,0},{2,3},{3,2},{4,5},{5,4},{6,7},{7,6},{8,9},{9,8},{10,11... | collective-permute-start | bytes 1548296 | tf_op jit(solution)/shard_map/ppermute | solution.py:878
